TPU v7x, 256 devices: a whole 4x4x8 slice. The times are simulated.
256 devices in a mesh: pipe: 16 (over y, z_hi), tensor: 16 (over x, z_lo, core).
Axes of the slice: x: 4, y: 4, z: 8 (z_hi: 4, z_lo: 2; z = z_hi * 2 + z_lo), core: 2. Of those that a mesh axis runs over, the one named last changes fastest.
Arguments:
- hidden: bfloat16 [256, 12288], P('pipe', 'tensor'), may hold values from -9 to 9
- targets: int32 [256], P('pipe'), may hold values from 0 to 65535
- weight: bfloat16 [65536, 12288], P('pipe', 'tensor'), may hold values from -1 to 1
Outputs:
- losses: float32 [256], P('pipe')
- hidden_grad: bfloat16 [256, 12288], P('pipe', 'tensor')
- weight_grad: bfloat16 [65536, 12288], P('pipe', 'tensor')
All inputs are finite; a program needn't handle non-finite values.
Results may differ from a plain program's by a relative error of at most 0.0039.
Values may be sent and summed in bfloat16 or wider, within the bound.
No kernel may reach another device: no remote copies, remote signals or barrier semaphores. Data moves between devices by JAX's collectives and lax.ppermute only.
A program may use at most 64 MiB of HBM per device.

v0:
```python
import jax
import jax.numpy as jnp
from jax import lax
from jax.sharding import PartitionSpec as P


def local_terms(logits, offset, all_targets):
    columns = jnp.arange(logits.shape[1], dtype=jnp.int32) + offset
    onehot = (columns[None, :] == all_targets[:, None]).astype(jnp.float32)
    local_top = jnp.max(logits, axis=1)
    local_pick = jnp.sum(logits * onehot, axis=1)
    return (onehot, local_top, local_pick)


def section_stats(logits, local_top, local_pick):
    upper = lax.pmax(local_top, "pipe")
    shifted = jnp.exp(logits - upper[:, None])
    total, picked = lax.psum((jnp.sum(shifted, axis=1), local_pick), "pipe")
    return (upper, total, picked, shifted)


def shards(hidden, targets, weight):
    rows_here = hidden.shape[0]
    section_vocab = weight.shape[0]
    section_index = lax.axis_index("pipe")
    gathered, all_targets = (
        lax.all_gather(hidden, "pipe", axis=0, tiled=True),
        lax.all_gather(targets, "pipe", axis=0, tiled=True),
    )
    partial_value = lax.dot_general(
        gathered, weight, (((1,), (1,)), ((), ())), preferred_element_type=jnp.float32
    )
    logits = lax.psum(partial_value, "tensor")
    offset = section_index * section_vocab
    onehot, local_top, local_pick = local_terms(logits, offset, all_targets)
    upper, total, picked, shifted = section_stats(logits, local_top, local_pick)
    full_grad = (4.0 * (shifted / total[:, None] - onehot)).astype(jnp.bfloat16)
    weight_grad = lax.dot_general(
        full_grad, gathered, (((0,), (0,)), ((), ())), preferred_element_type=jnp.float32
    ).astype(jnp.bfloat16)
    hidden_grad = lax.psum_scatter(
        jnp.dot(full_grad, weight, preferred_element_type=jnp.float32),
        "pipe",
        scatter_dimension=0,
        tiled=True,
    ).astype(jnp.bfloat16)
    every_loss = upper + jnp.log(total) - picked
    losses = lax.dynamic_slice_in_dim(every_loss, section_index * rows_here, rows_here, 0)
    return (losses, hidden_grad, weight_grad)


def solution(mesh):
    return jax.shard_map(
        shards,
        mesh=mesh,
        in_specs=(P("pipe", "tensor"), P("pipe"), P("pipe", "tensor")),
        out_specs=(P("pipe"), P("pipe", "tensor"), P("pipe", "tensor")),
        check_vma=False,
    )
```

profile of v0, /device:TPU:1, one launch (start us, length us, event | category | flops | bytes accessed | tf_op | source)
XLA Modules:
  0.0 384.3 jit_solution(8877293040976038882)
XLA Ops:
  7.2 0.0 all-reduce.4.cloned.1.call-start
  7.2 43.6 %all_gather.6 = bf16[256,768]{1,0:T(8,128)(2,1)S(1)} all-gather(bf16[16,768]{1,0:T(8,128)(2,1)} %param.3), channel_id=1, replica_groups=mesh['pipe'=16,'tensor'=16] {'pipe'}, dimensions={0}, use_global_device_ids=true | all-gather | bytes 417792 | tf_op jit(solution)/shard_map/all_gather | solution.py:27
  50.8 6.6 %fusion.5 = f32[256,4096]{1,0:T(8,128)} fusion(bf16[256,768]{1,0:T(8,128)(2,1)S(1)} %all_gather.6, bf16[4096,768]{1,0:T(8,128)(2,1)} %param.5), kind=kOutput, calls=%fused_computation.11 | convolution fusion | flops 1610612736 | bytes 10878976 | tf_op jit(solution)/shard_map/dot_general | solution.py:30
  57.4 0.0 copy-start.1
  57.4 0.0 copy-start
  57.4 0.0 all-reduce.4.cloned.1.call-update
  57.4 0.0 reduce-scatter.2.cloned.1.call-start
  57.5 0.6 copy-done.1
  58.1 0.6 dynamic-slice
  59.3 0.0 copy-done
  59.3 0.2 dynamic-update-slice
  59.6 8.5 %all-reduce = s32[256]{0:T(256)S(1)} all-reduce(s32[256]{0:T(256)S(1)} %dynamic-update-slice), channel_id=1, replica_groups=mesh['pipe'=16,'tensor'=16] {'pipe'}, use_global_device_ids=true, to_apply=%add | all-reduce | flops 256 | bytes 2048
  68.1 129.8 %all-reduce.4.cloned.1.call-done = f32[256,4096]{1,0:T(8,128)} async-done(((f32[256,4096]{1,0:T(8,128)}), f32[256,4096]{1,0:T(8,128)}) %all-reduce.4.cloned.1.call-update) | async-done | bytes 4194320 | tf_op jit(solution)/shard_map/psum | solution.py:33
  197.9 2.5 reduce_max.9
  200.3 37.4 %pmax.7 = f32[256]{0:T(256)S(1)} all-reduce(f32[256]{0:T(256)S(1)} %reduce_max.9), channel_id=1, replica_groups=mesh['pipe'=16,'tensor'=16] {'pipe'}, use_global_device_ids=true, to_apply=%region_2.0 | all-reduce | flops 256 | bytes 2048 | tf_op jit(solution)/shard_map/pmax | solution.py:16
  237.7 3.3 fusion.4
  241.0 32.1 %all-reduce.1 = (f32[256]{0:T(256)S(1)}, f32[256]{0:T(256)S(1)}) all-reduce(f32[256]{0:T(256)S(1)} %get-tuple-element.4, f32[256]{0:T(256)S(1)} %get-tuple-element.3), channel_id=1, replica_groups=mesh['pipe'=16,'tensor'=16] {'pipe'}, use_global_device_ids=true, to_apply=%region_6.0 | all-reduce | flops 512 | bytes 4096 | tf_op jit(solution)/shard_map/psum | solution.py:18
  273.1 3.6 fusion.3
  276.7 5.5 %fusion.6 = f32[256,768]{1,0:T(8,128)} fusion(bf16[256,4096]{1,0:T(8,128)(2,1)S(1)} %fusion.3, bf16[4096,768]{1,0:T(8,128)(2,1)} %param.5), kind=kOutput, calls=%fused_computation.12 | convolution fusion | flops 1610612736 | bytes 9175040 | tf_op jit(solution)/shard_map/dot_general | solution.py:42
  282.2 0.0 reduce-scatter.2.cloned.1.call-update
  282.2 0.6 dynamic_slice.3
  282.8 4.6 %convolution_convert_fusion = bf16[4096,768]{1,0:T(8,128)(2,1)} fusion(bf16[256,4096]{1,0:T(8,128)(2,1)S(1)} %fusion.3, bf16[256,768]{1,0:T(8,128)(2,1)S(1)} %all_gather.6), kind=kOutput, calls=%fused_computation | convolution fusion | flops 1613758464 | bytes 8781824 | tf_op jit(solution)/shard_map/dot_general | solution.py:38
  287.4 88.7 %reduce-scatter.2.cloned.1.call-done = f32[16,768]{1,0:T(8,128)} async-done(((f32[256,768]{1,0:T(8,128)}), f32[16,768]{1,0:T(8,128)}) %reduce-scatter.2.cloned.1.call-update) | async-done | bytes 49168 | tf_op jit(solution)/shard_map/reduce_scatter | solution.py:41
  376.1 1.4 convert_element_type.14
  (3 shorter events, 0.0 us)
Async XLA Ops:
  7.2 190.7 %all-reduce.4.cloned.1.call-start = ((), (), s32[]{:S(2)}) async-start(), calls=%async_computation.1 | async-start | bytes 8388608 | tf_op jit(solution)/shard_map/psum | solution.py:33
  57.4 0.7 copy-start.1
  57.4 1.9 copy-start
  57.4 318.7 %reduce-scatter.2.cloned.1.call-start = ((), (), s32[]{:S(2)}) async-start(), calls=%async_computation.2 | async-start | bytes 835584 | tf_op jit(solution)/shard_map/reduce_scatter | solution.py:41
Sparse Core Ops, SparseCore 0:
  57.5 140.2 all-reduce.3
  282.3 93.7 reduce-scatter.1
where the time goes:
time: 386 us; the launch traced here: 384 us
  waiting for transfers between devices  219 us (57%)
  blocking collectives  122 us (32%)
  matrix products  16.7 us (4%)
  between operations  14.7 us (4%)
  other arithmetic  10.7 us (3%)
    psum x1, waiting for transfers between devices, shards(): logits = lax.psum(partial_value, 'tensor')  130 us
    reduce_scatter x1, waiting for transfers between devices, shards(): lax.psum_scatter(jnp.dot(full_grad, weight, preferred_element_type=jnp.fl...  88.7 us
    all_gather x1, blocking collectives, shards(): lax.all_gather(hidden, 'pipe', axis=0, tiled=True)  43.6 us
    pmax x1, blocking collectives, section_stats(): upper = lax.pmax(local_top, 'pipe')  37.4 us
    psum x1, blocking collectives, section_stats(): total, picked = lax.psum((jnp.sum(shifted, axis=1), local_pick), 'pipe')  32.1 us
    unnamed x1, blocking collectives  8.51 us
  transfers between devices with their start and end apart: 2, of which 2 were waited for; matrix products, arithmetic and copies ran while one was open for 2% of the time, Pallas kernels for 0%

commit v1 on v0

v1 whole, which is shorter than its diff:
```python
import jax
import jax.numpy as jnp
from jax import lax
from jax.sharding import Mesh, PartitionSpec as P

PIPE = ("y", "zh")
CHIPS = ("x", "zl")
TENSOR = ("x", "zl", "core")
SWAP = [(0, 1), (1, 0)]


def split3(v):
    a = v.astype(jnp.bfloat16)
    r = v - lax.reduce_precision(v, 8, 7)
    b = r.astype(jnp.bfloat16)
    r = r - lax.reduce_precision(r, 8, 7)
    return jnp.stack([a, b, r.astype(jnp.bfloat16)], axis=-1)


def join3(v):
    v = v.astype(jnp.float32)
    return v[..., 0] + v[..., 1] + v[..., 2]


def spread(v, axes, n):
    return lax.all_to_all(jnp.broadcast_to(v[None], (n,) + v.shape), axes, 0, 0)


def shards(hidden, targets, weight):
    rows, width = hidden.shape
    vocab = weight.shape[0]
    half = vocab // 2
    section = lax.axis_index(PIPE)
    core = lax.axis_index("core")
    chip = lax.axis_index(CHIPS)

    ids = jnp.stack([targets // 256, targets % 256], axis=1).astype(jnp.bfloat16)
    packed = jnp.concatenate([hidden, jnp.pad(ids, ((0, 0), (0, 126)))], axis=1)
    gathered = spread(packed, PIPE, 16).reshape(16 * rows, width + 128)
    tokens = gathered.shape[0]
    per_chip = tokens // 8
    full = gathered[:, :width]
    ids = gathered[:, width : width + 2].astype(jnp.int32)
    all_targets = ids[:, 0] * 256 + ids[:, 1]

    w_own = lax.dynamic_slice_in_dim(weight, core * half, half, 0)
    w_oth = lax.dynamic_slice_in_dim(weight, (1 - core) * half, half, 0)
    dims = (((1,), (1,)), ((), ()))
    send = lax.dot_general(full, w_oth, dims, preferred_element_type=jnp.float32)
    got = lax.ppermute(send.astype(jnp.float16), "core", SWAP)
    keep = lax.dot_general(full, w_own, dims, preferred_element_type=jnp.float32)
    keep = (keep + got.astype(jnp.float32)).astype(jnp.float16)
    parts = lax.all_to_all(keep.reshape(8, per_chip, half), CHIPS, 0, 0)
    logits = jnp.sum(parts.astype(jnp.float32), axis=0)

    mine = lax.dynamic_slice_in_dim(all_targets, chip * per_chip, per_chip, 0)
    columns = section * vocab + core * half + jnp.arange(half, dtype=jnp.int32)
    top = jnp.max(logits, axis=1)
    e = jnp.exp(logits - top[:, None])
    s = jnp.sum(e, axis=1)
    pick = jnp.sum(jnp.where(columns[None, :] == mine[:, None], logits, 0.0), axis=1)
    stats = jnp.concatenate([split3(top), split3(s), split3(pick)], axis=1)
    block = jnp.concatenate([e.astype(jnp.bfloat16), jnp.pad(stats, ((0, 0), (0, 119)))], axis=1)
    own = spread(block, CHIPS, 8).reshape(tokens, half + 128)
    oth = lax.ppermute(own, "core", SWAP)

    def unpack(b):
        st = b[:, half : half + 9].reshape(tokens, 3, 3)
        return join3(st)

    st_own, st_oth = unpack(own), unpack(oth)
    all_stats = jnp.concatenate([st_own.T, st_oth.T, jnp.zeros((2, tokens), jnp.float32)], axis=0)
    everyone = spread(all_stats, PIPE, 16)
    upper = jnp.maximum(jnp.max(everyone[:, 0], axis=0), jnp.max(everyone[:, 3], axis=0))
    total = jnp.sum(
        everyone[:, 1] * jnp.exp(everyone[:, 0] - upper) + everyone[:, 4] * jnp.exp(everyone[:, 3] - upper), axis=0
    )
    picked = jnp.sum(everyone[:, 2] + everyone[:, 5], axis=0)
    every_loss = upper + jnp.log(total) - picked
    losses = lax.dynamic_slice_in_dim(every_loss, section * rows, rows, 0)

    def grad(b, st, which):
        scale = jnp.exp(st[:, 0] - upper) / total
        columns = section * vocab + which * half + jnp.arange(half, dtype=jnp.int32)
        onehot = (columns[None, :] == all_targets[:, None]).astype(jnp.float32)
        return (4.0 * (b[:, :half].astype(jnp.float32) * scale[:, None] - onehot)).astype(jnp.bfloat16)

    g_own, g_oth = grad(own, st_own, core), grad(oth, st_oth, 1 - core)
    hg = jnp.dot(g_own, w_own, preferred_element_type=jnp.float32)
    hg = hg + jnp.dot(g_oth, w_oth, preferred_element_type=jnp.float32)
    sent = (hg * 4096.0).astype(jnp.float16).reshape(16, rows, width)
    parts = lax.all_to_all(sent, PIPE, 0, 0)
    hidden_grad = (jnp.sum(parts.astype(jnp.float32), axis=0) * (1.0 / 4096.0)).astype(jnp.bfloat16)

    g_full = jnp.where(
        core == 0, jnp.concatenate([g_own, g_oth], axis=1), jnp.concatenate([g_oth, g_own], axis=1)
    )
    weight_grad = lax.dot_general(
        g_full, full, (((0,), (0,)), ((), ())), preferred_element_type=jnp.float32
    ).astype(jnp.bfloat16)
    return (losses, hidden_grad, weight_grad)


def solution(mesh):
    fine = Mesh(mesh.devices.reshape(4, 4, 4, 2, 2), PIPE + TENSOR)
    return jax.shard_map(
        shards,
        mesh=fine,
        in_specs=(P(PIPE, TENSOR), P(PIPE), P(PIPE, TENSOR)),
        out_specs=(P(PIPE), P(PIPE, TENSOR), P(PIPE, TENSOR)),
        check_vma=False,
    )
```

time: 386 us -> 130 us (0.34)
  waiting for transfers between devices: 219 us -> 52.8 us
  blocking collectives: 122 us -> 19.1 us
  starting transfers between devices: 0.08 us -> 27.8 us
  between operations: 14.7 us -> 0.83 us
  other arithmetic: 10.7 us -> 4.56 us
  matrix products: 16.7 us -> 20.8 us
    psum x1 -> x0, waiting for transfers between devices: 130 us -> none  [shards(): logits = lax.psum(partial_value, 'tensor')]
    reduce_scatter x1 -> x0, waiting for transfers between devices: 88.7 us -> none  [shards(): lax.psum_scatter(jnp.dot(full_grad, weight, preferred_element_type=jnp.fl...]
    all_to_all x0 -> x4, waiting for transfers between devices: none -> 48.2 us  [the longest x2 25.7 us: spread(): return lax.all_to_all(jnp.broadcast_to(v[None], (n,) + v.shape), axes, 0, 0)]
    all_gather x1 -> x0, blocking collectives: 43.6 us -> none  [shards(): lax.all_gather(hidden, 'pipe', axis=0, tiled=True)]
    pmax x1 -> x0, blocking collectives: 37.4 us -> none  [section_stats(): upper = lax.pmax(local_top, 'pipe')]
    psum x1 -> x0, blocking collectives: 32.1 us -> none  [section_stats(): total, picked = lax.psum((jnp.sum(shifted, axis=1), local_pick), 'pipe')]
    all_to_all x0 -> x4, starting transfers between devices: none -> 23.1 us  [the longest x2 15.3 us: spread(): return lax.all_to_all(jnp.broadcast_to(v[None], (n,) + v.shape), axes, 0, 0)]
    all_to_all x0 -> x1, blocking collectives: none -> 19.1 us  [spread(): return lax.all_to_all(jnp.broadcast_to(v[None], (n,) + v.shape), axes, 0, 0)]
  transfers between devices with their start and end apart: 2 -> 6, of which waited for: 2 -> 6; matrix products, arithmetic and copies ran while one was open for 2% -> 6% of each run, Pallas kernels for 0% -> 0%
where the time goes in v1:
time: 130 us; the launch traced here: 129 us
  waiting for transfers between devices  52.8 us (41%)
  starting transfers between devices  27.8 us (21%)
  matrix products  20.8 us (16%)
  blocking collectives  19.1 us (15%)
  other arithmetic  4.56 us (4%)
  local copies, waits for them, and re-layouts  3.33 us (3%)
    all_to_all x2, waiting for transfers between devices, spread(): return lax.all_to_all(jnp.broadcast_to(v[None], (n,) + v.shape), axes, 0, 0)  25.7 us
    all_to_all x1, blocking collectives, spread(): return lax.all_to_all(jnp.broadcast_to(v[None], (n,) + v.shape), axes, 0, 0)  19.1 us
    all_to_all x2, starting transfers between devices, spread(): return lax.all_to_all(jnp.broadcast_to(v[None], (n,) + v.shape), axes, 0, 0)  15.3 us
    all_to_all x1, waiting for transfers between devices, shards(): parts = lax.all_to_all(keep.reshape(8, per_chip, half), CHIPS, 0, 0)  14.8 us
    all_to_all x1, waiting for transfers between devices, shards(): parts = lax.all_to_all(sent, PIPE, 0, 0)  7.68 us
    dot_general x1, matrix products, shards(): lax.dot_general(g_full, full, (((0,), (0,)), ((), ())), preferred_element...  6.71 us
    all_to_all x1, starting transfers between devices, shards(): parts = lax.all_to_all(keep.reshape(8, per_chip, half), CHIPS, 0, 0)  4.31 us
    dot_general x1, matrix products, shards(): lax.dot_general(full, w_own, dims, preferred_element_type=jnp.float32)  3.94 us
  transfers between devices with their start and end apart: 6, of which 6 were waited for; matrix products, arithmetic and copies ran while one was open for 6% of the time, Pallas kernels for 0%

profile of v1, /device:TPU:1, one launch (start us, length us, event | category | flops | bytes accessed | tf_op | source)
XLA Modules:
  0.0 129.2 jit_solution(2943366889072791749)
XLA Ops:
  0.6 0.7 convert_bitcast_fusion
  1.3 0.1 copy.55
  1.4 0.7 fusion.38
  2.2 0.8 broadcast_in_dim.12
  3.0 11.7 %all-to-all-start = ((bf16[16,16,896]{2,1,0:T(8,128)(2,1)}), bf16[16,16,896]{2,1,0:T(8,128)(2,1)S(1)}, u32[]{:S(2)}, u32[]{:S(2)}) async-start(bf16[16,16,896]{2,1,0:T(8,128)(2,1)} %broadcast_in_dim.12), calls=%async_computation | async-start | bytes 917504 | tf_op jit(solution)/shard_map/all_to_all | solution.py:26
  14.7 15.4 %all-to-all-done = bf16[16,16,896]{2,1,0:T(8,128)(2,1)S(1)} async-done(((bf16[16,16,896]{2,1,0:T(8,128)(2,1)}), bf16[16,16,896]{2,1,0:T(8,128)(2,1)S(1)}, u32[]{:S(2)}, u32[]{:S(2)}) %all-to-all-start) | async-done | bytes 458784 | tf_op jit(solution)/shard_map/all_to_all | solution.py:26
  30.1 0.0 copy-start.2
  30.1 3.1 %fusion.8 = f16[256,2048]{1,0:T(8,128)(2,1)S(1)} fusion(bf16[4096,768]{1,0:T(8,128)(2,1)} %param.5, s32[]{:T(128)S(6)} %select_n.39, bf16[256,896]{1,0:T(8,128)(2,1)S(1)} %bitcast.80), kind=kOutput, calls=%fused_computation.9 | convolution fusion | flops 805830656 | bytes 4587524 | tf_op jit(solution)/shard_map/dot_general | solution.py:49
  33.2 2.9 %collective-permute-start = (f16[256,2048]{1,0:T(8,128)(2,1)S(1)}, f16[256,2048]{1,0:T(8,128)(2,1)S(1)}, u32[]{:S(2)}, u32[]{:S(2)}) collective-permute-start(f16[256,2048]{1,0:T(8,128)(2,1)S(1)} %fusion.8), channel_id=1, source_target_pairs={{0,1},{1,0},{2,3},{3,2},{4,5},{5,4},{6,7},{7,6},{8,9},{9,8},{10,11... | collective-permute-start | bytes 3145736 | tf_op jit(solution)/shard_map/ppermute | solution.py:50
  36.1 2.3 %collective-permute-done = f16[256,2048]{1,0:T(8,128)(2,1)S(1)} collective-permute-done((f16[256,2048]{1,0:T(8,128)(2,1)S(1)}, f16[256,2048]{1,0:T(8,128)(2,1)S(1)}, u32[]{:S(2)}, u32[]{:S(2)}) %collective-permute-start) | collective-permute-done | bytes 1048608 | tf_op jit(solution)/shard_map/ppermute | solution.py:50
  38.4 3.9 %add_convert_fusion = f16[256,2048]{1,0:T(8,128)(2,1)} fusion(f16[256,2048]{1,0:T(8,128)(2,1)S(1)} %collective-permute-done, bf16[4096,768]{1,0:T(8,128)(2,1)} %param.5, s32[]{:T(128)S(6)} %select_n.38, bf16[256,896]{1,0:T(8,128)(2,1)S(1)} %bitcast.81), kind=kOutput, calls=%fused_computation.19 | convolution fusion | flops 806879232 | bytes 5636100 | tf_op jit(solution)/shard_map/dot_general | solution.py:51
  42.3 4.3 %all-to-all-start.1 = ((f16[8,32,2048]{2,1,0:T(8,128)(2,1)}), f16[8,32,2048]{2,1,0:T(8,128)(2,1)S(1)}, u32[]{:S(2)}, u32[]{:S(2)}) async-start(f16[8,32,2048]{2,1,0:T(8,128)(2,1)} %bitcast.3), calls=%async_computation.1 | async-start | bytes 2097152 | tf_op jit(solution)/shard_map/all_to_all | solution.py:53
  46.6 0.0 copy-done.2
  46.7 0.2 fusion.65
  46.8 0.1 dynamic-slice_reduce_fusion
  47.0 14.8 %all-to-all-done.1 = f16[8,32,2048]{2,1,0:T(8,128)(2,1)S(1)} async-done(((f16[8,32,2048]{2,1,0:T(8,128)(2,1)}), f16[8,32,2048]{2,1,0:T(8,128)(2,1)S(1)}, u32[]{:S(2)}, u32[]{:S(2)}) %all-to-all-start.1) | async-done | bytes 1048608 | tf_op jit(solution)/shard_map/all_to_all | solution.py:53
  61.8 0.2 convert_reduce_fusion
  62.0 0.1 reduce_max.29
  62.1 0.2 select_reduce_fusion
  62.4 0.1 concatenate.19
  62.5 0.1 copy.56
  62.6 0.1 broadcast_in_dim.14
  62.7 19.1 %all_to_all.25 = bf16[8,32,2176]{2,1,0:T(8,128)(2,1)S(1)} all-to-all(bf16[8,32,2176]{2,1,0:T(8,128)(2,1)S(1)} %broadcast_in_dim.14), channel_id=1, replica_groups=mesh['y'=4,'zh'=4,'x'=4,'zl'=2,'core'=2] {'x','zl'}, dimensions={0} | all-to-all | bytes 2228224 | tf_op jit(solution)/shard_map/all_to_all | solution.py:26
  81.7 0.7 copy.41
  82.4 1.8 %collective-permute-start.1 = (bf16[256,2176]{0,1:T(8,128)(2,1)S(1)}, bf16[256,2176]{0,1:T(8,128)(2,1)S(1)}, u32[]{:S(2)}, u32[]{:S(2)}) collective-permute-start(bf16[256,2176]{0,1:T(8,128)(2,1)S(1)} %copy.41), channel_id=1, source_target_pairs={{0,1},{1,0},{2,3},{3,2},{4,5},{5,4},{6,7},{7,6},{8,9},{9,8},{10,11... | collective-permute-start | bytes 3342344 | tf_op jit(solution)/shard_map/ppermute | solution.py:65
  84.2 0.1 pad.16.clone
  84.4 2.3 %collective-permute-done.1 = bf16[256,2176]{0,1:T(8,128)(2,1)S(1)} collective-permute-done((bf16[256,2176]{0,1:T(8,128)(2,1)S(1)}, bf16[256,2176]{0,1:T(8,128)(2,1)S(1)}, u32[]{:S(2)}, u32[]{:S(2)}) %collective-permute-start.1) | collective-permute-done | bytes 1114144 | tf_op jit(solution)/shard_map/ppermute | solution.py:65
  86.7 0.1 maximum_maximum_fusion
  86.7 0.7 broadcast_in_dim.16
  87.4 3.5 %all-to-all-start.3 = ((f32[16,8,256]{2,1,0:T(8,128)}), f32[16,8,256]{2,1,0:T(8,128)S(1)}, u32[]{:S(2)}, u32[]{:S(2)}) async-start(f32[16,8,256]{2,1,0:T(8,128)} %broadcast_in_dim.16), calls=%async_computation.3 | async-start | bytes 262144 | tf_op jit(solution)/shard_map/all_to_all | solution.py:26
  90.9 10.3 %all-to-all-done.3 = f32[16,8,256]{2,1,0:T(8,128)S(1)} async-done(((f32[16,8,256]{2,1,0:T(8,128)}), f32[16,8,256]{2,1,0:T(8,128)S(1)}, u32[]{:S(2)}, u32[]{:S(2)}) %all-to-all-start.3) | async-done | bytes 131104 | tf_op jit(solution)/shard_map/all_to_all | solution.py:26
  101.3 0.1 fusion.66
  101.4 1.4 %multiply_convert_fusion = (bf16[256,2048]{0,1:T(8,128)(2,1)S(1)}, bf16[256,2048]{0,1:T(8,128)(2,1)S(1)}) fusion(bf16[256,2176]{0,1:T(8,128)(2,1)S(1)} %collective-permute-done.1, f32[256]{0:T(256)S(1)} %bitcast.91, s32[256]{0:T(256)S(1)} %get-tuple-element.8, s32[2048]{0:T(1024)S(1)} %iota_add_fusion, s32[2048]{0:T(1024)S(1)} %iota_add_fusion.1, ...), kind=kLoop, calls=%fused_computation.16 | loop fusion | flops 7340032 | bytes 4213760 | tf_op jit(solution)/shard_map/convert_element_type | solution.py:86
  102.8 0.0 copy-start
  102.8 3.3 %fusion.4 = f32[256,768]{1,0:T(8,128)S(1)} fusion(bf16[256,2048]{0,1:T(8,128)(2,1)S(1)} %get-tuple-element.25, bf16[4096,768]{1,0:T(8,128)(2,1)} %param.5, s32[]{:T(128)S(6)} %select_n.38), kind=kOutput, calls=%fused_computation.5 | convolution fusion | flops 805306368 | bytes 4980740 | tf_op jit(solution)/shard_map/dot_general | solution.py:89
  106.1 0.0 copy-done
  106.1 0.0 copy-start.1
  106.1 0.0 copy-start.3
  106.1 3.8 %fusion.23 = f16[256,768]{1,0:T(8,128)(2,1)} fusion(f32[256,768]{1,0:T(8,128)S(1)} %fusion.4, bf16[256,2048]{0,1:T(8,128)(2,1)S(1)} %get-tuple-element.24, bf16[4096,768]{1,0:T(8,128)(2,1)} %param.5, s32[]{:T(128)S(6)} %select_n.39), kind=kOutput, calls=%fused_computation.23 | convolution fusion | flops 805896192 | bytes 5373956 | tf_op jit(solution)/shard_map/dot_general | solution.py:90
  109.9 3.6 %all-to-all-start.4 = ((f16[16,16,768]{2,1,0:T(8,128)(2,1)}), f16[16,16,768]{2,1,0:T(8,128)(2,1)S(1)}, u32[]{:S(2)}, u32[]{:S(2)}) async-start(f16[16,16,768]{2,1,0:T(8,128)(2,1)} %bitcast.84), calls=%async_computation.4 | async-start | bytes 786432 | tf_op jit(solution)/shard_map/all_to_all | solution.py:92
  113.5 0.6 dynamic_slice.18
  114.1 0.0 copy-done.1
  114.1 0.0 copy-done.3
  114.1 6.7 %convolution_convert_fusion = bf16[4096,768]{1,0:T(8,128)(2,1)} fusion(bf16[256,2048]{0,1:T(8,128)(2,1)S(1)} %get-tuple-element.24, bf16[256,2048]{0,1:T(8,128)(2,1)S(1)} %copy-done.1, pred[]{:T(512)S(6)} %eq.53, bf16[256,896]{1,0:T(8,128)(2,1)S(1)} %bitcast.83), kind=kOutput, calls=%fused_computation | convolution fusion | flops 1623195648 | bytes 8781825 | tf_op jit(solution)/shard_map/dot_general | solution.py:98
  120.8 7.7 %all-to-all-done.4 = f16[16,16,768]{2,1,0:T(8,128)(2,1)S(1)} async-done(((f16[16,16,768]{2,1,0:T(8,128)(2,1)}), f16[16,16,768]{2,1,0:T(8,128)(2,1)S(1)}, u32[]{:S(2)}, u32[]{:S(2)}) %all-to-all-start.4) | async-done | bytes 393248 | tf_op jit(solution)/shard_map/all_to_all | solution.py:92
  128.5 0.1 convert_reduce_fusion.1
  128.6 0.6 multiply_convert_fusion.2
  (22 shorter events, 0.2 us)
Async XLA Ops:
  3.0 27.2 %all-to-all-start = ((bf16[16,16,896]{2,1,0:T(8,128)(2,1)}), bf16[16,16,896]{2,1,0:T(8,128)(2,1)S(1)}, u32[]{:S(2)}, u32[]{:S(2)}) async-start(bf16[16,16,896]{2,1,0:T(8,128)(2,1)} %broadcast_in_dim.12), calls=%async_computation | async-start | bytes 917504 | tf_op jit(solution)/shard_map/all_to_all | solution.py:26
  30.1 16.5 %copy-start.2 = (bf16[16,16,896]{2,1,0:T(8,128)(2,1)}, bf16[16,16,896]{2,1,0:T(8,128)(2,1)S(1)}, u32[]{:S(2)}) copy-start(bf16[16,16,896]{2,1,0:T(8,128)(2,1)S(1)} %all-to-all-done) | copy-start | bytes 1376260
  33.2 5.1 %collective-permute-start = (f16[256,2048]{1,0:T(8,128)(2,1)S(1)}, f16[256,2048]{1,0:T(8,128)(2,1)S(1)}, u32[]{:S(2)}, u32[]{:S(2)}) collective-permute-start(f16[256,2048]{1,0:T(8,128)(2,1)S(1)} %fusion.8), channel_id=1, source_target_pairs={{0,1},{1,0},{2,3},{3,2},{4,5},{5,4},{6,7},{7,6},{8,9},{9,8},{10,11... | collective-permute-start | bytes 3145736 | tf_op jit(solution)/shard_map/ppermute | solution.py:50
  42.3 19.5 %all-to-all-start.1 = ((f16[8,32,2048]{2,1,0:T(8,128)(2,1)}), f16[8,32,2048]{2,1,0:T(8,128)(2,1)S(1)}, u32[]{:S(2)}, u32[]{:S(2)}) async-start(f16[8,32,2048]{2,1,0:T(8,128)(2,1)} %bitcast.3), calls=%async_computation.1 | async-start | bytes 2097152 | tf_op jit(solution)/shard_map/all_to_all | solution.py:53
  82.4 4.2 %collective-permute-start.1 = (bf16[256,2176]{0,1:T(8,128)(2,1)S(1)}, bf16[256,2176]{0,1:T(8,128)(2,1)S(1)}, u32[]{:S(2)}, u32[]{:S(2)}) collective-permute-start(bf16[256,2176]{0,1:T(8,128)(2,1)S(1)} %copy.41), channel_id=1, source_target_pairs={{0,1},{1,0},{2,3},{3,2},{4,5},{5,4},{6,7},{7,6},{8,9},{9,8},{10,11... | collective-permute-start | bytes 3342344 | tf_op jit(solution)/shard_map/ppermute | solution.py:65
  87.4 13.8 %all-to-all-start.3 = ((f32[16,8,256]{2,1,0:T(8,128)}), f32[16,8,256]{2,1,0:T(8,128)S(1)}, u32[]{:S(2)}, u32[]{:S(2)}) async-start(f32[16,8,256]{2,1,0:T(8,128)} %broadcast_in_dim.16), calls=%async_computation.3 | async-start | bytes 262144 | tf_op jit(solution)/shard_map/all_to_all | solution.py:26
  102.8 3.3 %copy-start = (bf16[256,2048]{0,1:T(8,128)(2,1)}, bf16[256,2048]{0,1:T(8,128)(2,1)S(1)}, u32[]{:S(2)}) copy-start(bf16[256,2048]{0,1:T(8,128)(2,1)S(1)} %get-tuple-element.25) | copy-start | bytes 3145732
  106.1 8.0 %copy-start.1 = (bf16[256,2048]{0,1:T(8,128)(2,1)S(1)}, bf16[256,2048]{0,1:T(8,128)(2,1)}, u32[]{:S(2)}) copy-start(bf16[256,2048]{0,1:T(8,128)(2,1)} %copy-done) | copy-start | bytes 3145732
  106.1 8.0 %copy-start.3 = (bf16[16,16,896]{2,1,0:T(8,128)(2,1)S(1)}, bf16[16,16,896]{2,1,0:T(8,128)(2,1)}, u32[]{:S(2)}) copy-start(bf16[16,16,896]{2,1,0:T(8,128)(2,1)} %copy-done.2) | copy-start | bytes 1376260
  109.9 18.6 %all-to-all-start.4 = ((f16[16,16,768]{2,1,0:T(8,128)(2,1)}), f16[16,16,768]{2,1,0:T(8,128)(2,1)S(1)}, u32[]{:S(2)}, u32[]{:S(2)}) async-start(f16[16,16,768]{2,1,0:T(8,128)(2,1)} %bitcast.84), calls=%async_computation.4 | async-start | bytes 786432 | tf_op jit(solution)/shard_map/all_to_all | solution.py:92

commit v2 on v1

v2 whole, which is shorter than its diff:
```python
import functools

import jax
import jax.numpy as jnp
from jax import lax
from jax.experimental import pallas as pl
from jax.experimental.pallas import tpu as pltpu
from jax.sharding import Mesh, PartitionSpec as P

PIPE = ("y", "zh")
CHIPS = ("x", "zl")
TENSOR = ("x", "zl", "core")
SWAP = [(0, 1), (1, 0)]
TILE = 512


def join3(v, k):
    return v[3 * k : 3 * k + 1] + v[3 * k + 1 : 3 * k + 2] + v[3 * k + 2 : 3 * k + 3]


def decode(ids):
    ids = ids.astype(jnp.float32).astype(jnp.int32)
    return ids[:, 0:1] * 256 + ids[:, 1:2]


def spread(v, axes, n):
    return lax.all_to_all(jnp.broadcast_to(v[None], (n,) + v.shape), axes, 0, 0)


def far(v):
    return pltpu.with_memory_space_constraint(v, pltpu.HBM)


def params(mib):
    return pltpu.CompilerParams(vmem_limit_bytes=mib << 20)


def pack_kernel(targets, hidden_ref, out_ref):
    rows, width = hidden_ref.shape
    row = lax.broadcasted_iota(jnp.int32, (rows, 128), 0)
    lane = lax.broadcasted_iota(jnp.int32, (rows, 128), 1)
    ids = jnp.zeros((rows, 128), jnp.int32)
    for r in range(rows):
        t = targets[r]
        high = lax.shift_right_logical(t, 8)
        low = t - high * 256
        ids = jnp.where((row == r) & (lane == 0), high, ids)
        ids = jnp.where((row == r) & (lane == 1), low, ids)
    ids = ids.astype(jnp.float32).astype(jnp.bfloat16)
    for d in range(out_ref.shape[0]):
        out_ref[d, :, :width] = hidden_ref[...]
        out_ref[d, :, width:] = ids


def pack(hidden, targets, copies):
    rows, width = hidden.shape
    return pl.pallas_call(
        pack_kernel,
        in_specs=[pl.BlockSpec(memory_space=pltpu.SMEM), pl.BlockSpec(memory_space=pltpu.VMEM)],
        out_specs=pl.BlockSpec(memory_space=pltpu.VMEM),
        out_shape=jax.ShapeDtypeStruct((copies, rows, width + 128), jnp.bfloat16),
        compiler_params=params(60),
    )(targets, hidden)


def softmax_kernel(place, logits_ref, ids_ref, picks_ref, out_ref):
    rows, half = logits_ref.shape
    logits = logits_ref[...]
    top = jnp.max(logits, axis=1, keepdims=True)
    e = jnp.exp(logits - top)
    s = jnp.sum(e, axis=1, keepdims=True)
    columns = lax.broadcasted_iota(jnp.int32, logits.shape, 1) + place[1]
    pick = jnp.sum(jnp.where(columns == decode(ids_ref[...]), logits, 0.0), axis=1, keepdims=True)
    lane = lax.broadcasted_iota(jnp.int32, (rows, 128), 1)
    stats = jnp.zeros((rows, 128), jnp.float32)
    for k, v in enumerate((top, s, pick)):
        for part in range(3):
            rounded = v.astype(jnp.bfloat16).astype(jnp.float32)
            stats = jnp.where(lane == 3 * k + part, rounded, stats)
            v = v - rounded
    e, stats = e.astype(jnp.bfloat16), stats.astype(jnp.bfloat16)
    for d in range(out_ref.shape[0]):
        out_ref[d, :, :half] = e
        out_ref[d, :, half:] = stats


def softmax(place, logits, gathered, picks, copies):
    rows, half = logits.shape
    last = gathered.shape[1] // 128 - 1
    return pl.pallas_call(
        softmax_kernel,
        grid_spec=pltpu.PrefetchScalarGridSpec(
            num_scalar_prefetch=1,
            grid=(1,),
            in_specs=[
                pl.BlockSpec((rows, half), lambda i, s: (0, 0)),
                pl.BlockSpec((rows, 128), lambda i, s: (s[0], last)),
                pl.BlockSpec(memory_space=pltpu.HBM),
            ],
            out_specs=pl.BlockSpec((copies, rows, half + 128), lambda i, s: (0, 0, 0)),
        ),
        out_shape=jax.ShapeDtypeStruct((copies, rows, half + 128), jnp.bfloat16),
        compiler_params=params(8),
    )(place, logits, gathered, far(picks))


def rows_kernel(block_ref, out_ref):
    v = block_ref[...].astype(jnp.float32).T
    out_ref[...] = jnp.concatenate([join3(v, 0), join3(v, 1), join3(v, 2), v[16:21]], axis=0)


def stat_rows(own):
    tokens, width = own.shape
    return pl.pallas_call(
        rows_kernel,
        grid=(1,),
        in_specs=[pl.BlockSpec((tokens, 128), lambda i: (0, width // 128 - 1))],
        out_specs=pl.BlockSpec((8, tokens), lambda i: (0, 0)),
        out_shape=jax.ShapeDtypeStruct((8, tokens), jnp.float32),
        compiler_params=params(4),
    )(own)


def join_kernel(own_ref, oth_ref, out_ref):
    both = jnp.concatenate([own_ref[0:3], oth_ref[0:3], own_ref[6:8]], axis=0)
    for d in range(out_ref.shape[0]):
        out_ref[d] = both


def join_stats(own, oth, copies):
    return pl.pallas_call(
        join_kernel,
        out_shape=jax.ShapeDtypeStruct((copies,) + own.shape, jnp.float32),
        compiler_params=params(4),
    )(own, oth)


def scale_kernel(every_ref, own_ref, oth_ref, u_ref, scale_ref, loss_ref):
    every = every_ref[...]
    upper = jnp.max(jnp.maximum(every[:, 0], every[:, 3]), axis=0, keepdims=True)
    total = jnp.sum(
        every[:, 1] * jnp.exp(every[:, 0] - upper) + every[:, 4] * jnp.exp(every[:, 3] - upper), axis=0, keepdims=True
    )
    picked = jnp.sum(every[:, 2] + every[:, 5], axis=0, keepdims=True)
    loss_ref[...] = upper + jnp.log(total) - picked
    a = jnp.exp(own_ref[0:1] - upper) / total
    b = jnp.exp(oth_ref[0:1] - upper) / total
    scale_ref[...] = jnp.concatenate([a, b, jnp.zeros((126, a.shape[1]), jnp.float32)], axis=0).T


def scale_columns(everyone, own, oth, u):
    tokens = own.shape[1]
    return pl.pallas_call(
        scale_kernel,
        in_specs=[pl.BlockSpec(memory_space=pltpu.VMEM)] * 3 + [pl.BlockSpec(memory_space=pl.ANY)],
        out_shape=[
            jax.ShapeDtypeStruct((tokens, 128), jnp.float32),
            jax.ShapeDtypeStruct((1, tokens), jnp.float32),
        ],
        compiler_params=params(4),
    )(everyone, own, oth, u)


def row_blocks(place, w_ref, held, sems):
    step = held.shape[0] // sems.shape[0]
    copies = []
    for slot in range(sems.shape[0]):
        which, k = divmod(slot, sems.shape[0] // 2)
        source = pl.ds(pl.multiple_of(place[which], step) + k * step, step)
        copies.append(
            pltpu.make_async_copy(w_ref.at[source], held.at[pl.ds(slot * step, step)], sems.at[slot])
        )
    return step, copies


def picks_kernel(place, ids_ref, w_ref, t_ref, held, sems):
    step, copies = row_blocks(place, w_ref, held, sems)
    for copy in copies:
        copy.start()
    target = decode(ids_ref[...]) - place[2]
    t = None
    for slot, copy in enumerate(copies):
        columns = lax.broadcasted_iota(jnp.int32, (target.shape[0], step), 1) + slot * step
        onehot = jnp.where(columns == target, 1.0, 0.0).astype(jnp.bfloat16)
        copy.wait()
        d = jnp.dot(onehot, held[slot * step : (slot + 1) * step], preferred_element_type=jnp.float32)
        t = d if t is None else t + d
    t_ref[...] = t.astype(jnp.bfloat16)


def picks_of(place, gathered, weight, tokens):
    width = weight.shape[1]
    last = gathered.shape[1] // 128 - 1
    return pl.pallas_call(
        picks_kernel,
        grid_spec=pltpu.PrefetchScalarGridSpec(
            num_scalar_prefetch=1,
            grid=(1,),
            in_specs=[
                pl.BlockSpec((tokens, 128), lambda i, s: (0, last)),
                pl.BlockSpec(memory_space=pltpu.HBM),
            ],
            out_specs=pl.BlockSpec((tokens, width), lambda i, s: (0, 0)),
            scratch_shapes=[pltpu.VMEM(weight.shape, weight.dtype), pltpu.SemaphoreType.DMA((4,))],
        ),
        out_shape=pltpu.HBM((tokens, width), jnp.bfloat16),
        compiler_params=params(24),
        cost_estimate=pl.CostEstimate(
            flops=2 * tokens * weight.size, bytes_accessed=2 * weight.size, transcendentals=0
        ),
    )(place, gathered, far(weight))


def product_kernel(place, own_ref, oth_ref, w_ref, u_ref, held, other, sems, sem):
    half = held.shape[0] // 2
    step, copies = row_blocks(place, w_ref, held, sems)
    fetch = pltpu.make_async_copy(oth_ref, other, sem)
    copies[0].start()
    copies[1].start()
    fetch.start()
    per_half = len(copies) // 2
    for which, p_ref in enumerate((own_ref, other)):
        u = None
        for k in range(per_half):
            slot = which * per_half + k
            copies[slot].wait()
            if slot + 2 < len(copies):
                copies[slot + 2].start()
            if slot == per_half:
                fetch.wait()
            d = jnp.dot(
                p_ref[:, k * step : (k + 1) * step],
                held[slot * step : (slot + 1) * step],
                preferred_element_type=jnp.float32,
            )
            u = d if u is None else u + d
        u_ref[which] = u


def products(place, own, oth, weight):
    tokens, width = own.shape[0], weight.shape[1]
    return pl.pallas_call(
        product_kernel,
        grid_spec=pltpu.PrefetchScalarGridSpec(
            num_scalar_prefetch=1,
            grid=(1,),
            in_specs=[
                pl.BlockSpec(own.shape, lambda i, s: (0, 0)),
                pl.BlockSpec(memory_space=pltpu.HBM),
                pl.BlockSpec(memory_space=pltpu.HBM),
            ],
            out_specs=pl.BlockSpec((2, tokens, width), lambda i, s: (0, 0, 0)),
            scratch_shapes=[
                pltpu.VMEM(weight.shape, weight.dtype),
                pltpu.VMEM(oth.shape, oth.dtype),
                pltpu.SemaphoreType.DMA((4,)),
                pltpu.SemaphoreType.DMA,
            ],
        ),
        out_shape=jax.ShapeDtypeStruct((2, tokens, width), jnp.float32),
        compiler_params=params(24),
        cost_estimate=pl.CostEstimate(
            flops=2 * tokens * weight.size, bytes_accessed=2 * weight.size, transcendentals=0
        ),
    )(place, own, far(oth), far(weight))


def weight_grad_kernel(steps, place, own_ref, oth_ref, hidden_ref, ids_ref, scale_ref, out_ref):
    i = pl.program_id(0)

    def tile(p_ref, which, j):
        columns = lax.broadcasted_iota(jnp.int32, p_ref.shape, 1) + (place[1 + which] + j * TILE)
        onehot = (columns == decode(ids_ref[...])).astype(jnp.float32)
        scale = scale_ref[:, which : which + 1]
        g = (4.0 * (p_ref[...].astype(jnp.float32) * scale - onehot)).astype(jnp.bfloat16)
        out_ref[...] = lax.dot_general(
            g, hidden_ref[...], (((0,), (0,)), ((), ())), preferred_element_type=jnp.float32
        ).astype(jnp.bfloat16)

    @pl.when(i < steps)
    def _():
        tile(own_ref, 0, i)

    @pl.when(i >= steps)
    def _():
        tile(oth_ref, 1, i - steps)


def weight_gradient(place, own, oth, gathered, scales, half, width):
    tokens = own.shape[0]
    last = gathered.shape[1] // 128 - 1
    steps = half // TILE
    return pl.pallas_call(
        functools.partial(weight_grad_kernel, steps),
        grid_spec=pltpu.PrefetchScalarGridSpec(
            num_scalar_prefetch=1,
            grid=(2 * steps,),
            in_specs=[
                pl.BlockSpec((tokens, TILE), lambda i, s: (0, jnp.minimum(i, steps - 1))),
                pl.BlockSpec((tokens, TILE), lambda i, s: (0, jnp.maximum(i - steps, 0))),
                pl.BlockSpec((tokens, width), lambda i, s: (0, 0)),
                pl.BlockSpec((tokens, 128), lambda i, s: (0, last)),
                pl.BlockSpec((tokens, 128), lambda i, s: (0, 0)),
            ],
            out_specs=pl.BlockSpec(
                (TILE, width), lambda i, s: (lax.rem(i + s[0] * steps, 2 * steps), 0)
            ),
        ),
        out_shape=jax.ShapeDtypeStruct((2 * half, width), jnp.bfloat16),
        compiler_params=pltpu.CompilerParams(vmem_limit_bytes=24 << 20),
        cost_estimate=pl.CostEstimate(
            flops=4 * tokens * half * width, bytes_accessed=4 * half * (width + tokens), transcendentals=0
        ),
    )(place, own, far(oth), gathered, gathered, scales)


def shards(hidden, targets, weight):
    rows, width = hidden.shape
    vocab = weight.shape[0]
    half = vocab // 2
    section = lax.axis_index(PIPE)
    core = lax.axis_index("core")
    chip = lax.axis_index(CHIPS)
    base_own = section * vocab + core * half
    base_oth = section * vocab + (1 - core) * half

    gathered = lax.all_to_all(pack(hidden, targets, 16), PIPE, 0, 0).reshape(16 * rows, width + 128)
    tokens = gathered.shape[0]
    per_chip = tokens // 8
    full = gathered[:, :width]

    w_own = lax.dynamic_slice_in_dim(weight, core * half, half, 0)
    w_oth = lax.dynamic_slice_in_dim(weight, (1 - core) * half, half, 0)
    dims = (((1,), (1,)), ((), ()))
    send = lax.dot_general(full, w_oth, dims, preferred_element_type=jnp.float32)
    got = lax.ppermute(send.astype(jnp.float16), "core", SWAP)
    keep = lax.dot_general(full, w_own, dims, preferred_element_type=jnp.float32)
    keep = lax.optimization_barrier(keep)
    keep = (keep + got.astype(jnp.float32)).astype(jnp.float16)
    parts = lax.all_to_all(keep.reshape(8, per_chip, half), CHIPS, 0, 0)
    logits = jnp.sum(parts.astype(jnp.float32), axis=0)
    picks = picks_of(jnp.stack([0, half, section * vocab]), gathered, weight, tokens)

    block = softmax(jnp.stack([chip, base_own]), logits, gathered, picks, 8)
    own = lax.all_to_all(block, CHIPS, 0, 0).reshape(tokens, half + 128)
    st_own = stat_rows(own)
    st_oth = lax.ppermute(st_own, "core", SWAP)
    own, st_oth = lax.optimization_barrier((own, st_oth))
    oth = lax.ppermute(own, "core", SWAP)
    everyone = lax.all_to_all(join_stats(st_own, st_oth, 16), PIPE, 0, 0)

    u = products(jnp.stack([core * half, (1 - core) * half]), own, oth, weight)

    scales, every_loss = scale_columns(everyone, st_own, st_oth, u)
    hg = scales[:, 0:1] * u[0] + scales[:, 1:2] * u[1] - picks.astype(jnp.float32)
    sent = (hg * 16384.0).astype(jnp.float16).reshape(16, rows, width)
    parts = lax.all_to_all(sent, PIPE, 0, 0)
    hidden_grad = (jnp.sum(parts.astype(jnp.float32), axis=0) * (1.0 / 4096.0)).astype(jnp.bfloat16)

    losses = lax.dynamic_slice_in_dim(every_loss[0], section * rows, rows, 0)
    weight_grad = weight_gradient(
        jnp.stack([core, base_own, base_oth]), own, oth, gathered, scales, half, width
    )
    return (losses, hidden_grad, weight_grad)


def solution(mesh):
    fine = Mesh(mesh.devices.reshape(4, 4, 4, 2, 2), PIPE + TENSOR)
    return jax.shard_map(
        shards,
        mesh=fine,
        in_specs=(P(PIPE, TENSOR), P(PIPE), P(PIPE, TENSOR)),
        out_specs=(P(PIPE), P(PIPE, TENSOR), P(PIPE, TENSOR)),
        check_vma=False,
    )
```

time: 130 us -> 119 us (0.915)
  Pallas kernels: 0 us -> 23.5 us
  waiting for transfers between devices: 52.8 us -> 36 us
  matrix products: 20.8 us -> 5.79 us
  local copies, waits for them, and re-layouts: 3.33 us -> 1.37 us
    pallas_call x0 -> x8, Pallas kernels: none -> 23.5 us  [the longest x1 8.98 us: weight_gradient(): pl.pallas_call(functools.partial(weight_grad_kernel, steps), grid_spec=pl...]
    dot_general x3 -> x0, matrix products: 13.8 us -> none  [the longest x1 6.71 us: shards(): lax.dot_general(g_full, full, (((0,), (0,)), ((), ())), preferred_element...]
    all_to_all x2, waiting for transfers between devices: 25.7 us -> 20.2 us  [the longest x1 15.4 us: shards(): lax.all_to_all(pack(hidden, targets, 16), PIPE, 0, 0)]
    all_to_all x1, waiting for transfers between devices: 14.8 us -> 9.77 us  [shards(): parts = lax.all_to_all(keep.reshape(8, per_chip, half), CHIPS, 0, 0)]
    all_to_all x1, waiting for transfers between devices: 7.68 us -> 5.2 us  [shards(): parts = lax.all_to_all(sent, PIPE, 0, 0)]
    ppermute x1, waiting for transfers between devices: 2.29 us -> 0.01 us  [shards(): got = lax.ppermute(send.astype(jnp.float16), 'core', SWAP)]
    ppermute x1, waiting for transfers between devices: 2.26 us -> 0.01 us  [shards(): oth = lax.ppermute(own, 'core', SWAP)]
    ppermute x0 -> x1, starting transfers between devices: none -> 1.77 us  [shards(): st_oth = lax.ppermute(st_own, 'core', SWAP)]
  transfers between devices with their start and end apart: 6 -> 7, of which waited for: 6 -> 5; matrix products, arithmetic and copies ran while one was open for 6% -> 3% of each run, Pallas kernels for 0% -> 18%
where the time goes in v2:
time: 119 us; the launch traced here: 118 us
  waiting for transfers between devices  36 us (30%)
  starting transfers between devices  28.7 us (24%)
  Pallas kernels  23.5 us (20%)
  blocking collectives  18.7 us (16%)
  matrix products  5.79 us (5%)
  other arithmetic  3.53 us (3%)
  local copies, waits for them, and re-layouts  1.37 us (1%)
    all_to_all x1, blocking collectives, shards(): own = lax.all_to_all(block, CHIPS, 0, 0).reshape(tokens, half + 128)  18.7 us
    all_to_all x1, waiting for transfers between devices, shards(): lax.all_to_all(pack(hidden, targets, 16), PIPE, 0, 0)  15.4 us
    all_to_all x1, starting transfers between devices, shards(): lax.all_to_all(pack(hidden, targets, 16), PIPE, 0, 0)  11.7 us
    all_to_all x1, waiting for transfers between devices, shards(): parts = lax.all_to_all(keep.reshape(8, per_chip, half), CHIPS, 0, 0)  9.77 us
    pallas_call x1, Pallas kernels, weight_gradient(): pl.pallas_call(functools.partial(weight_grad_kernel, steps), grid_spec=pl...  8.98 us
    pallas_call x1, Pallas kernels, picks_of(): pl.pallas_call(picks_kernel, grid_spec=pltpu.PrefetchScalarGridSpec(num_s...  5.65 us
    pallas_call x1, Pallas kernels, products(): pl.pallas_call(product_kernel, grid_spec=pltpu.PrefetchScalarGridSpec(num...  5.54 us
    all_to_all x1, waiting for transfers between devices, shards(): parts = lax.all_to_all(sent, PIPE, 0, 0)  5.2 us
  transfers between devices with their start and end apart: 7, of which 5 were waited for; matrix products, arithmetic and copies ran while one was open for 3% of the time, Pallas kernels for 18%

profile of v2, /device:TPU:1, one launch (start us, length us, event | category | flops | bytes accessed | tf_op | source)
XLA Modules:
  0.0 118.4 jit_solution(6945050285021609973)
XLA Ops:
  0.6 1.6 %shard_map.58 = bf16[16,16,896]{2,1,0:T(8,128)(2,1)} custom-call(s32[16]{0:T(128)} %targets.1, bf16[16,768]{1,0:T(8,128)(2,1)} %hidden_ref.1), custom_call_target="tpu_custom_call" | custom-call | tf_op jit(solution)/shard_map/pallas_call | solution.py:57
  2.2 11.7 %all-to-all-start = ((bf16[16,16,896]{2,1,0:T(8,128)(2,1)}), bf16[16,16,896]{2,1,0:T(8,128)(2,1)S(1)}, u32[]{:S(2)}, u32[]{:S(2)}) async-start(bf16[16,16,896]{2,1,0:T(8,128)(2,1)} %shard_map.58), calls=%async_computation | async-start | bytes 917504 | tf_op jit(solution)/shard_map/all_to_all | solution.py:327
  14.0 15.4 %all-to-all-done = bf16[16,16,896]{2,1,0:T(8,128)(2,1)S(1)} async-done(((bf16[16,16,896]{2,1,0:T(8,128)(2,1)}), bf16[16,16,896]{2,1,0:T(8,128)(2,1)S(1)}, u32[]{:S(2)}, u32[]{:S(2)}) %all-to-all-start) | async-done | bytes 458784 | tf_op jit(solution)/shard_map/all_to_all | solution.py:327
  29.3 2.9 %fusion.4 = f16[256,2048]{1,0:T(8,128)(2,1)S(1)} fusion(bf16[4096,768]{1,0:T(8,128)(2,1)} %w_ref.3, s32[]{:T(128)S(6)} %select_n.10, bf16[256,896]{1,0:T(8,128)(2,1)S(1)} %bitcast.35), kind=kOutput, calls=%fused_computation.4 | convolution fusion | flops 805830656 | bytes 4587524 | tf_op jit(solution)/shard_map/dot_general | solution.py:335
  32.3 2.9 %collective-permute-start = (f16[256,2048]{1,0:T(8,128)(2,1)S(1)}, f16[256,2048]{1,0:T(8,128)(2,1)S(1)}, u32[]{:S(2)}, u32[]{:S(2)}) collective-permute-start(f16[256,2048]{1,0:T(8,128)(2,1)S(1)} %fusion.4), channel_id=1, source_target_pairs={{0,1},{1,0},{2,3},{3,2},{4,5},{5,4},{6,7},{7,6},{8,9},{9,8},{10,11... | collective-permute-start | bytes 3145736 | tf_op jit(solution)/shard_map/ppermute | solution.py:336
  35.1 2.9 %fusion.2 = f32[256,2048]{1,0:T(8,128)S(1)} fusion(bf16[4096,768]{1,0:T(8,128)(2,1)} %w_ref.3, s32[]{:T(128)S(6)} %select_n.9, bf16[256,896]{1,0:T(8,128)(2,1)S(1)} %bitcast.36), kind=kOutput, calls=%fused_computation.2 | convolution fusion | flops 805306368 | bytes 5636100 | tf_op jit(solution)/shard_map/dot_general | solution.py:337
  38.0 0.0 collective-permute-done
  38.0 1.3 %add_convert_fusion = f16[256,2048]{1,0:T(8,128)(2,1)} fusion(f32[256,2048]{1,0:T(8,128)S(1)} %fusion.2, f16[256,2048]{1,0:T(8,128)(2,1)S(1)} %collective-permute-done), kind=kLoop, calls=%fused_computation.6 | loop fusion | flops 1572864 | bytes 4194304 | tf_op jit(solution)/shard_map/convert_element_type | solution.py:339
  39.4 4.3 %all-to-all-start.1 = ((f16[8,32,2048]{2,1,0:T(8,128)(2,1)}), f16[8,32,2048]{2,1,0:T(8,128)(2,1)S(1)}, u32[]{:S(2)}, u32[]{:S(2)}) async-start(f16[8,32,2048]{2,1,0:T(8,128)(2,1)} %bitcast.3), calls=%async_computation.1 | async-start | bytes 2097152 | tf_op jit(solution)/shard_map/all_to_all | solution.py:340
  43.7 0.1 pad_add_fusion.place
  43.8 0.1 pad_add_fusion.1.place
  43.8 5.7 %shard_map.59.picks_ref = bf16[256,768]{1,0:T(8,128)(2,1)} custom-call(s32[3]{0:T(128)S(1)} %pad_add_fusion.1.place, bf16[256,896]{1,0:T(8,128)(2,1)S(1)} %bitcast.37, bf16[4096,768]{1,0:T(8,128)(2,1)} %w_ref.3), custom_call_target="tpu_custom_call" | custom-call | flops 1610612736 | bytes 6291456 | tf_op jit(solution)/shard_map/pallas_call | solution.py:194
  49.5 9.8 %all-to-all-done.1 = f16[8,32,2048]{2,1,0:T(8,128)(2,1)S(1)} async-done(((f16[8,32,2048]{2,1,0:T(8,128)(2,1)}), f16[8,32,2048]{2,1,0:T(8,128)(2,1)S(1)}, u32[]{:S(2)}, u32[]{:S(2)}) %all-to-all-start.1) | async-done | bytes 1048608 | tf_op jit(solution)/shard_map/all_to_all | solution.py:340
  59.3 0.2 convert_reduce_fusion.logits_ref
  59.5 0.8 shard_map.60
  60.3 18.7 %all_to_all.25 = bf16[8,32,2176]{2,1,0:T(8,128)(2,1)S(1)} all-to-all(bf16[8,32,2176]{2,1,0:T(8,128)(2,1)S(1)} %shard_map.60), channel_id=1, replica_groups=mesh['y'=4,'zh'=4,'x'=4,'zl'=2,'core'=2] {'x','zl'}, dimensions={0} | all-to-all | bytes 2228224 | tf_op jit(solution)/shard_map/all_to_all | solution.py:345
  79.0 0.1 shard_map.61.own_ref
  79.1 1.8 %collective-permute-start.1 = (f32[8,256]{1,0:T(8,128)S(1)}, f32[8,256]{1,0:T(8,128)S(1)}, u32[]{:S(2)}, u32[]{:S(2)}) collective-permute-start(f32[8,256]{1,0:T(8,128)S(1)} %shard_map.61.own_ref), channel_id=1, source_target_pairs={{0,1},{1,0},{2,3},{3,2},{4,5},{5,4},{6,7},{7,6},{8,9},{9,8},{10,11... | collective-permute-start | bytes 24584 | tf_op jit(solution)/shard_map/ppermute | solution.py:347
  80.9 0.8 collective-permute-done.1.oth_ref
  81.7 0.3 collective-permute-start.2
  82.0 0.7 shard_map.62
  82.7 3.5 %all-to-all-start.3 = ((f32[16,8,256]{2,1,0:T(8,128)}), f32[16,8,256]{2,1,0:T(8,128)S(1)}, u32[]{:S(2)}, u32[]{:S(2)}) async-start(f32[16,8,256]{2,1,0:T(8,128)} %shard_map.62), calls=%async_computation.3 | async-start | bytes 262144 | tf_op jit(solution)/shard_map/all_to_all | solution.py:350
  86.2 0.1 pad_add_fusion.2.place
  86.3 0.0 collective-permute-done.2.oth_ref
  86.3 5.5 %shard_map.63.u_ref = f32[2,256,768]{2,1,0:T(8,128)S(1)} custom-call(s32[2]{0:T(128)S(1)} %pad_add_fusion.2.place, bf16[256,2176]{1,0:T(8,128)(2,1)S(1)} %bitcast.33, bf16[256,2176]{1,0:T(8,128)(2,1)} %collective-permute-done.2.oth_ref, bf16[4096,768]{1,0:T(8,128)(2,1)} %w_ref.3), custom_call_target="tpu_custom_call" | custom-call | flops 1610612736 | bytes 6291456 | tf_op jit(solution)/shard_map/pallas_call | solution.py:242
  91.8 4.8 %all-to-all-done.3.every_ref = f32[16,8,256]{2,1,0:T(8,128)S(1)} async-done(((f32[16,8,256]{2,1,0:T(8,128)}), f32[16,8,256]{2,1,0:T(8,128)S(1)}, u32[]{:S(2)}, u32[]{:S(2)}) %all-to-all-start.3) | async-done | bytes 131104 | tf_op jit(solution)/shard_map/all_to_all | solution.py:350
  96.6 0.0 copy-start
  96.6 0.2 shard_map.64
  96.9 0.2 slice_reduce_fusion.1
  97.1 0.6 copy-done
  97.6 1.0 fusion.11
  98.7 4.2 %all-to-all-start.4 = ((f16[16,16,768]{2,1,0:T(8,128)(2,1)}), f16[16,16,768]{2,1,0:T(8,128)(2,1)S(1)}, u32[]{:S(2)}, u32[]{:S(2)}) async-start(f16[16,16,768]{2,1,0:T(8,128)(2,1)} %bitcast.41), calls=%async_computation.4 | async-start | bytes 786432 | tf_op jit(solution)/shard_map/all_to_all | solution.py:357
  102.9 0.1 pad_add_fusion.3.place
  103.0 0.6 fusion.17
  103.5 9.0 %shard_map.65 = bf16[4096,768]{1,0:T(8,128)(2,1)} custom-call(s32[3]{0:T(128)S(1)} %pad_add_fusion.3.place, bf16[256,2176]{1,0:T(8,128)(2,1)S(1)} %bitcast.34, bf16[256,2176]{1,0:T(8,128)(2,1)} %collective-permute-done.2.oth_ref, bf16[256,896]{1,0:T(8,128)(2,1)S(1)} %bitcast.39, bf16[256,896]{1,0:T(8,128)(2,1)S(1)} %bitcast.40, ...), custom_call_target="tpu_custom_call" | custom-call | flops 1610612736 | bytes 8388608 | tf_op jit(solution)/shard_map/pallas_call | solution.py:293
  112.5 5.2 %all-to-all-done.4 = f16[16,16,768]{2,1,0:T(8,128)(2,1)S(1)} async-done(((f16[16,16,768]{2,1,0:T(8,128)(2,1)}), f16[16,16,768]{2,1,0:T(8,128)(2,1)S(1)}, u32[]{:S(2)}, u32[]{:S(2)}) %all-to-all-start.4) | async-done | bytes 393248 | tf_op jit(solution)/shard_map/all_to_all | solution.py:357
  117.7 0.1 convert_reduce_fusion.1
  117.8 0.6 multiply_convert_fusion
Async XLA Ops:
  2.2 27.2 %all-to-all-start = ((bf16[16,16,896]{2,1,0:T(8,128)(2,1)}), bf16[16,16,896]{2,1,0:T(8,128)(2,1)S(1)}, u32[]{:S(2)}, u32[]{:S(2)}) async-start(bf16[16,16,896]{2,1,0:T(8,128)(2,1)} %shard_map.58), calls=%async_computation | async-start | bytes 917504 | tf_op jit(solution)/shard_map/all_to_all | solution.py:327
  32.3 5.8 %collective-permute-start = (f16[256,2048]{1,0:T(8,128)(2,1)S(1)}, f16[256,2048]{1,0:T(8,128)(2,1)S(1)}, u32[]{:S(2)}, u32[]{:S(2)}) collective-permute-start(f16[256,2048]{1,0:T(8,128)(2,1)S(1)} %fusion.4), channel_id=1, source_target_pairs={{0,1},{1,0},{2,3},{3,2},{4,5},{5,4},{6,7},{7,6},{8,9},{9,8},{10,11... | collective-permute-start | bytes 3145736 | tf_op jit(solution)/shard_map/ppermute | solution.py:336
  39.4 19.9 %all-to-all-start.1 = ((f16[8,32,2048]{2,1,0:T(8,128)(2,1)}), f16[8,32,2048]{2,1,0:T(8,128)(2,1)S(1)}, u32[]{:S(2)}, u32[]{:S(2)}) async-start(f16[8,32,2048]{2,1,0:T(8,128)(2,1)} %bitcast.3), calls=%async_computation.1 | async-start | bytes 2097152 | tf_op jit(solution)/shard_map/all_to_all | solution.py:340
  79.1 2.6 %collective-permute-start.1 = (f32[8,256]{1,0:T(8,128)S(1)}, f32[8,256]{1,0:T(8,128)S(1)}, u32[]{:S(2)}, u32[]{:S(2)}) collective-permute-start(f32[8,256]{1,0:T(8,128)S(1)} %shard_map.61.own_ref), channel_id=1, source_target_pairs={{0,1},{1,0},{2,3},{3,2},{4,5},{5,4},{6,7},{7,6},{8,9},{9,8},{10,11... | collective-permute-start | bytes 24584 | tf_op jit(solution)/shard_map/ppermute | solution.py:347
  81.7 4.6 %collective-permute-start.2 = (bf16[256,2176]{1,0:T(8,128)(2,1)S(1)}, bf16[256,2176]{1,0:T(8,128)(2,1)}, u32[]{:S(2)}, u32[]{:S(2)}) collective-permute-start(bf16[256,2176]{1,0:T(8,128)(2,1)S(1)} %bitcast.32), channel_id=1, source_target_pairs={{0,1},{1,0},{2,3},{3,2},{4,5},{5,4},{6,7},{7,6},{8,9},{9,8},{10,11... | collective-permute-start | bytes 3342344 | tf_op jit(solution)/shard_map/ppermute | solution.py:349
  82.7 13.9 %all-to-all-start.3 = ((f32[16,8,256]{2,1,0:T(8,128)}), f32[16,8,256]{2,1,0:T(8,128)S(1)}, u32[]{:S(2)}, u32[]{:S(2)}) async-start(f32[16,8,256]{2,1,0:T(8,128)} %shard_map.62), calls=%async_computation.3 | async-start | bytes 262144 | tf_op jit(solution)/shard_map/all_to_all | solution.py:350
  96.6 1.0 copy-start
  98.7 19.1 %all-to-all-start.4 = ((f16[16,16,768]{2,1,0:T(8,128)(2,1)}), f16[16,16,768]{2,1,0:T(8,128)(2,1)S(1)}, u32[]{:S(2)}, u32[]{:S(2)}) async-start(f16[16,16,768]{2,1,0:T(8,128)(2,1)} %bitcast.41), calls=%async_computation.4 | async-start | bytes 786432 | tf_op jit(solution)/shard_map/all_to_all | solution.py:357

commit v3 on v2

--- a/solution.py
+++ b/solution.py
@@ -11,6 +11,7 @@
 CHIPS = ("x", "zl")
 TENSOR = ("x", "zl", "core")
 SWAP = [(0, 1), (1, 0)]
+STEPS = [(1, 0), (3, 0), (0, 1), (2, 1), (2, 0), (1, 1), (3, 1)]
 TILE = 512
 
 
@@ -25,6 +26,12 @@
 
 def spread(v, axes, n):
     return lax.all_to_all(jnp.broadcast_to(v[None], (n,) + v.shape), axes, 0, 0)
+
+
+def to_chip(v, step):
+    dx, dz = step
+    pairs = [(2 * x + z, 2 * ((x + dx) % 4) + (z ^ dz)) for x in range(4) for z in range(2)]
+    return lax.ppermute(v, CHIPS, pairs)
 
 
 def far(v):
@@ -63,7 +70,7 @@
     )(targets, hidden)
 
 
-def softmax_kernel(place, logits_ref, ids_ref, picks_ref, out_ref):
+def softmax_kernel(place, logits_ref, ids_ref, out_ref):
     rows, half = logits_ref.shape
     logits = logits_ref[...]
     top = jnp.max(logits, axis=1, keepdims=True)
@@ -78,15 +85,12 @@
             rounded = v.astype(jnp.bfloat16).astype(jnp.float32)
             stats = jnp.where(lane == 3 * k + part, rounded, stats)
             v = v - rounded
-    e, stats = e.astype(jnp.bfloat16), stats.astype(jnp.bfloat16)
-    for d in range(out_ref.shape[0]):
-        out_ref[d, :, :half] = e
-        out_ref[d, :, half:] = stats
-
-
-def softmax(place, logits, gathered, picks, copies):
+    out_ref[:, :half] = e.astype(jnp.bfloat16)
+    out_ref[:, half:] = stats.astype(jnp.bfloat16)
+
+
+def softmax(place, logits, ids):
     rows, half = logits.shape
-    last = gathered.shape[1] // 128 - 1
     return pl.pallas_call(
         softmax_kernel,
         grid_spec=pltpu.PrefetchScalarGridSpec(
@@ -94,31 +98,44 @@
             grid=(1,),
             in_specs=[
                 pl.BlockSpec((rows, half), lambda i, s: (0, 0)),
-                pl.BlockSpec((rows, 128), lambda i, s: (s[0], last)),
-                pl.BlockSpec(memory_space=pltpu.HBM),
-            ],
-            out_specs=pl.BlockSpec((copies, rows, half + 128), lambda i, s: (0, 0, 0)),
-        ),
-        out_shape=jax.ShapeDtypeStruct((copies, rows, half + 128), jnp.bfloat16),
+                pl.BlockSpec((rows, 128), lambda i, s: (s[0], 0)),
+            ],
+            out_specs=pl.BlockSpec((rows, half + 128), lambda i, s: (0, 0)),
+        ),
+        out_shape=jax.ShapeDtypeStruct((rows, half + 128), jnp.bfloat16),
         compiler_params=params(8),
-    )(place, logits, gathered, far(picks))
-
-
-def rows_kernel(block_ref, out_ref):
-    v = block_ref[...].astype(jnp.float32).T
-    out_ref[...] = jnp.concatenate([join3(v, 0), join3(v, 1), join3(v, 2), v[16:21]], axis=0)
-
-
-def stat_rows(own):
-    tokens, width = own.shape
-    return pl.pallas_call(
-        rows_kernel,
-        grid=(1,),
-        in_specs=[pl.BlockSpec((tokens, 128), lambda i: (0, width // 128 - 1))],
-        out_specs=pl.BlockSpec((8, tokens), lambda i: (0, 0)),
-        out_shape=jax.ShapeDtypeStruct((8, tokens), jnp.float32),
-        compiler_params=params(4),
-    )(own)
+    )(place, logits, ids)
+
+
+def assemble_kernel(place, *refs):
+    blocks, (out_ref, stat_ref) = refs[:-2], refs[-2:]
+    rows = blocks[0].shape[0]
+    for r, block in enumerate(blocks):
+        out_ref[pl.ds(pl.multiple_of(place[r] * rows, rows), rows)] = block[...]
+    v = out_ref[:, out_ref.shape[1] - 128 :].astype(jnp.float32).T
+    stat_ref[...] = jnp.concatenate([join3(v, 0), join3(v, 1), join3(v, 2), v[16:21]], axis=0)
+
+
+def assemble(place, blocks):
+    rows, width = blocks[0].shape
+    tokens = rows * len(blocks)
+    return pl.pallas_call(
+        assemble_kernel,
+        grid_spec=pltpu.PrefetchScalarGridSpec(
+            num_scalar_prefetch=1,
+            grid=(1,),
+            in_specs=[pl.BlockSpec((rows, width), lambda i, s: (0, 0))] * len(blocks),
+            out_specs=[
+                pl.BlockSpec((tokens, width), lambda i, s: (0, 0)),
+                pl.BlockSpec((8, tokens), lambda i, s: (0, 0)),
+            ],
+        ),
+        out_shape=[
+            jax.ShapeDtypeStruct((tokens, width), jnp.bfloat16),
+            jax.ShapeDtypeStruct((8, tokens), jnp.float32),
+        ],
+        compiler_params=params(12),
+    )(place, *blocks)
 
 
 def join_kernel(own_ref, oth_ref, out_ref):
@@ -173,71 +190,36 @@
     return step, copies
 
 
-def picks_kernel(place, ids_ref, w_ref, t_ref, held, sems):
-    step, copies = row_blocks(place, w_ref, held, sems)
-    for copy in copies:
-        copy.start()
-    target = decode(ids_ref[...]) - place[2]
-    t = None
-    for slot, copy in enumerate(copies):
-        columns = lax.broadcasted_iota(jnp.int32, (target.shape[0], step), 1) + slot * step
-        onehot = jnp.where(columns == target, 1.0, 0.0).astype(jnp.bfloat16)
-        copy.wait()
-        d = jnp.dot(onehot, held[slot * step : (slot + 1) * step], preferred_element_type=jnp.float32)
-        t = d if t is None else t + d
-    t_ref[...] = t.astype(jnp.bfloat16)
-
-
-def picks_of(place, gathered, weight, tokens):
-    width = weight.shape[1]
-    last = gathered.shape[1] // 128 - 1
-    return pl.pallas_call(
-        picks_kernel,
-        grid_spec=pltpu.PrefetchScalarGridSpec(
-            num_scalar_prefetch=1,
-            grid=(1,),
-            in_specs=[
-                pl.BlockSpec((tokens, 128), lambda i, s: (0, last)),
-                pl.BlockSpec(memory_space=pltpu.HBM),
-            ],
-            out_specs=pl.BlockSpec((tokens, width), lambda i, s: (0, 0)),
-            scratch_shapes=[pltpu.VMEM(weight.shape, weight.dtype), pltpu.SemaphoreType.DMA((4,))],
-        ),
-        out_shape=pltpu.HBM((tokens, width), jnp.bfloat16),
-        compiler_params=params(24),
-        cost_estimate=pl.CostEstimate(
-            flops=2 * tokens * weight.size, bytes_accessed=2 * weight.size, transcendentals=0
-        ),
-    )(place, gathered, far(weight))
-
-
-def product_kernel(place, own_ref, oth_ref, w_ref, u_ref, held, other, sems, sem):
-    half = held.shape[0] // 2
+def product_kernel(place, own_ref, ids_ref, oth_ref, w_ref, u_ref, t_ref, held, other, sems, sem):
     step, copies = row_blocks(place, w_ref, held, sems)
     fetch = pltpu.make_async_copy(oth_ref, other, sem)
     copies[0].start()
     copies[1].start()
     fetch.start()
     per_half = len(copies) // 2
+    target = decode(ids_ref[...])
+    tokens = target.shape[0]
+    t = None
     for which, p_ref in enumerate((own_ref, other)):
         u = None
         for k in range(per_half):
             slot = which * per_half + k
+            if slot == per_half:
+                fetch.wait()
+            columns = lax.broadcasted_iota(jnp.int32, (tokens, step), 1) + (place[2] + place[which] + k * step)
+            onehot = jnp.where(columns == target, 1.0, 0.0).astype(jnp.bfloat16)
+            both = jnp.concatenate([p_ref[:, k * step : (k + 1) * step], onehot], axis=0)
             copies[slot].wait()
             if slot + 2 < len(copies):
                 copies[slot + 2].start()
-            if slot == per_half:
-                fetch.wait()
-            d = jnp.dot(
-                p_ref[:, k * step : (k + 1) * step],
-                held[slot * step : (slot + 1) * step],
-                preferred_element_type=jnp.float32,
-            )
-            u = d if u is None else u + d
+            d = jnp.dot(both, held[slot * step : (slot + 1) * step], preferred_element_type=jnp.float32)
+            u = d[:tokens] if u is None else u + d[:tokens]
+            t = d[tokens:] if t is None else t + d[tokens:]
         u_ref[which] = u
-
-
-def products(place, own, oth, weight):
+    t_ref[...] = t.astype(jnp.bfloat16)
+
+
+def products(place, own, oth, ids, weight):
     tokens, width = own.shape[0], weight.shape[1]
     return pl.pallas_call(
         product_kernel,
@@ -246,10 +228,14 @@
             grid=(1,),
             in_specs=[
                 pl.BlockSpec(own.shape, lambda i, s: (0, 0)),
+                pl.BlockSpec(ids.shape, lambda i, s: (0, 0)),
                 pl.BlockSpec(memory_space=pltpu.HBM),
                 pl.BlockSpec(memory_space=pltpu.HBM),
             ],
-            out_specs=pl.BlockSpec((2, tokens, width), lambda i, s: (0, 0, 0)),
+            out_specs=[
+                pl.BlockSpec((2, tokens, width), lambda i, s: (0, 0, 0)),
+                pl.BlockSpec((tokens, width), lambda i, s: (0, 0)),
+            ],
             scratch_shapes=[
                 pltpu.VMEM(weight.shape, weight.dtype),
                 pltpu.VMEM(oth.shape, oth.dtype),
@@ -257,12 +243,15 @@
                 pltpu.SemaphoreType.DMA,
             ],
         ),
-        out_shape=jax.ShapeDtypeStruct((2, tokens, width), jnp.float32),
-        compiler_params=params(24),
+        out_shape=[
+            jax.ShapeDtypeStruct((2, tokens, width), jnp.float32),
+            jax.ShapeDtypeStruct((tokens, width), jnp.bfloat16),
+        ],
+        compiler_params=params(28),
         cost_estimate=pl.CostEstimate(
-            flops=2 * tokens * weight.size, bytes_accessed=2 * weight.size, transcendentals=0
-        ),
-    )(place, own, far(oth), far(weight))
+            flops=4 * tokens * weight.size, bytes_accessed=2 * weight.size, transcendentals=0
+        ),
+    )(place, own, ids, far(oth), far(weight))
 
 
 def weight_grad_kernel(steps, place, own_ref, oth_ref, hidden_ref, ids_ref, scale_ref, out_ref):
@@ -286,9 +275,8 @@
         tile(oth_ref, 1, i - steps)
 
 
-def weight_gradient(place, own, oth, gathered, scales, half, width):
+def weight_gradient(place, own, oth, gathered, ids, scales, half, width):
     tokens = own.shape[0]
-    last = gathered.shape[1] // 128 - 1
     steps = half // TILE
     return pl.pallas_call(
         functools.partial(weight_grad_kernel, steps),
@@ -299,7 +287,7 @@
                 pl.BlockSpec((tokens, TILE), lambda i, s: (0, jnp.minimum(i, steps - 1))),
                 pl.BlockSpec((tokens, TILE), lambda i, s: (0, jnp.maximum(i - steps, 0))),
                 pl.BlockSpec((tokens, width), lambda i, s: (0, 0)),
-                pl.BlockSpec((tokens, 128), lambda i, s: (0, last)),
+                pl.BlockSpec((tokens, 128), lambda i, s: (0, 0)),
                 pl.BlockSpec((tokens, 128), lambda i, s: (0, 0)),
             ],
             out_specs=pl.BlockSpec(
@@ -311,7 +299,7 @@
         cost_estimate=pl.CostEstimate(
             flops=4 * tokens * half * width, bytes_accessed=4 * half * (width + tokens), transcendentals=0
         ),
-    )(place, own, far(oth), gathered, gathered, scales)
+    )(place, own, far(oth), far(gathered), ids, scales)
 
 
 def shards(hidden, targets, weight):
@@ -327,7 +315,7 @@
     gathered = lax.all_to_all(pack(hidden, targets, 16), PIPE, 0, 0).reshape(16 * rows, width + 128)
     tokens = gathered.shape[0]
     per_chip = tokens // 8
-    full = gathered[:, :width]
+    full, ids = gathered[:, :width], gathered[:, width:]
 
     w_own = lax.dynamic_slice_in_dim(weight, core * half, half, 0)
     w_oth = lax.dynamic_slice_in_dim(weight, (1 - core) * half, half, 0)
@@ -336,30 +324,39 @@
     got = lax.ppermute(send.astype(jnp.float16), "core", SWAP)
     keep = lax.dot_general(full, w_own, dims, preferred_element_type=jnp.float32)
     keep = lax.optimization_barrier(keep)
-    keep = (keep + got.astype(jnp.float32)).astype(jnp.float16)
-    parts = lax.all_to_all(keep.reshape(8, per_chip, half), CHIPS, 0, 0)
-    logits = jnp.sum(parts.astype(jnp.float32), axis=0)
-    picks = picks_of(jnp.stack([0, half, section * vocab]), gathered, weight, tokens)
-
-    block = softmax(jnp.stack([chip, base_own]), logits, gathered, picks, 8)
-    own = lax.all_to_all(block, CHIPS, 0, 0).reshape(tokens, half + 128)
-    st_own = stat_rows(own)
+    x, z = lax.axis_index("x"), lax.axis_index("zl")
+    chips = [2 * lax.rem(x + dx, 4) + (z + dz) % 2 for dx, dz in STEPS]
+
+    def part(j):
+        mine = lax.dynamic_slice_in_dim(keep, j * per_chip, per_chip, 0)
+        theirs = lax.dynamic_slice_in_dim(got, j * per_chip, per_chip, 0)
+        return mine + theirs.astype(jnp.float32)
+
+    parts = [to_chip(part(j).astype(jnp.float16), step) for j, step in zip(chips, STEPS)]
+    logits = lax.optimization_barrier(part(chip))
+    for v in parts:
+        logits = logits + v.astype(jnp.float32)
+
+    block = softmax(jnp.stack([chip, base_own]), logits, ids)
+    sources = [2 * lax.rem(x + 4 - dx, 4) + (z + dz) % 2 for dx, dz in STEPS]
+    own, st_own = assemble(jnp.stack([chip] + sources), [block] + [to_chip(block, step) for step in STEPS])
     st_oth = lax.ppermute(st_own, "core", SWAP)
     own, st_oth = lax.optimization_barrier((own, st_oth))
     oth = lax.ppermute(own, "core", SWAP)
     everyone = lax.all_to_all(join_stats(st_own, st_oth, 16), PIPE, 0, 0)
 
-    u = products(jnp.stack([core * half, (1 - core) * half]), own, oth, weight)
+    place = jnp.stack([core * half, (1 - core) * half, section * vocab])
+    u, picks = products(place, own, oth, ids, weight)
 
     scales, every_loss = scale_columns(everyone, st_own, st_oth, u)
     hg = scales[:, 0:1] * u[0] + scales[:, 1:2] * u[1] - picks.astype(jnp.float32)
     sent = (hg * 16384.0).astype(jnp.float16).reshape(16, rows, width)
     parts = lax.all_to_all(sent, PIPE, 0, 0)
-    hidden_grad = (jnp.sum(parts.astype(jnp.float32), axis=0) * (1.0 / 4096.0)).astype(jnp.bfloat16)
+    hidden_grad = jnp.sum(parts.astype(jnp.float32) * (1.0 / 4096.0), axis=0).astype(jnp.bfloat16)
 
     losses = lax.dynamic_slice_in_dim(every_loss[0], section * rows, rows, 0)
     weight_grad = weight_gradient(
-        jnp.stack([core, base_own, base_oth]), own, oth, gathered, scales, half, width
+        jnp.stack([core, base_own, base_oth]), own, oth, gathered, ids, scales, half, width
     )
     return (losses, hidden_grad, weight_grad)
 

time: 119 us -> 116 us (0.975)
  starting transfers between devices: 28.7 us -> 48.2 us
  blocking collectives: 18.7 us -> 0 us
  Pallas kernels: 23.5 us -> 20.8 us
    ppermute x0 -> x14, starting transfers between devices: none -> 21.9 us  [to_chip(): return lax.ppermute(v, CHIPS, pairs)]
    all_to_all x1 -> x0, blocking collectives: 18.7 us -> none  [shards(): own = lax.all_to_all(block, CHIPS, 0, 0).reshape(tokens, half + 128)]
    ppermute x0 -> x14, waiting for transfers between devices: none -> 12.6 us  [to_chip(): return lax.ppermute(v, CHIPS, pairs)]
    all_to_all x1 -> x0, waiting for transfers between devices: 9.77 us -> none  [shards(): parts = lax.all_to_all(keep.reshape(8, per_chip, half), CHIPS, 0, 0)]
    pallas_call x2 -> x1, Pallas kernels: 5.72 us -> 0.68 us  [assemble(): pl.pallas_call(assemble_kernel, grid_spec=pltpu.PrefetchScalarGridSpec(nu...]
    all_to_all x1 -> x0, starting transfers between devices: 4.32 us -> none  [shards(): parts = lax.all_to_all(keep.reshape(8, per_chip, half), CHIPS, 0, 0)]
    pallas_call x1, Pallas kernels: 5.54 us -> 7.76 us  [products(): pl.pallas_call(product_kernel, grid_spec=pltpu.PrefetchScalarGridSpec(num...]
    all_to_all x1, waiting for transfers between devices: 4.8 us -> 2.72 us  [shards(): everyone = lax.all_to_all(join_stats(st_own, st_oth, 16), PIPE, 0, 0)]
  transfers between devices with their start and end apart: 7 -> 20, of which waited for: 5 -> 12; matrix products, arithmetic and copies ran while one was open for 3% -> 3% of each run, Pallas kernels for 18% -> 15%
where the time goes in v3:
time: 116 us; the launch traced here: 115 us
  starting transfers between devices  48.2 us (42%)
  waiting for transfers between devices  36 us (31%)
  Pallas kernels  20.8 us (18%)
  matrix products  5.99 us (5%)
  other arithmetic  2.46 us (2%)
    ppermute x14, starting transfers between devices, to_chip(): return lax.ppermute(v, CHIPS, pairs)  21.9 us
    all_to_all x1, waiting for transfers between devices, shards(): lax.all_to_all(pack(hidden, targets, 16), PIPE, 0, 0)  15.4 us
    ppermute x14, waiting for transfers between devices, to_chip(): return lax.ppermute(v, CHIPS, pairs)  12.6 us
    all_to_all x1, starting transfers between devices, shards(): lax.all_to_all(pack(hidden, targets, 16), PIPE, 0, 0)  11.7 us
    pallas_call x1, Pallas kernels, weight_gradient(): pl.pallas_call(functools.partial(weight_grad_kernel, steps), grid_spec=pl...  9.11 us
    pallas_call x1, Pallas kernels, products(): pl.pallas_call(product_kernel, grid_spec=pltpu.PrefetchScalarGridSpec(num...  7.76 us
    all_to_all x1, starting transfers between devices, shards(): parts = lax.all_to_all(sent, PIPE, 0, 0)  6.29 us
    all_to_all x1, waiting for transfers between devices, shards(): parts = lax.all_to_all(sent, PIPE, 0, 0)  4.42 us
  transfers between devices with their start and end apart: 20, of which 12 were waited for; matrix products, arithmetic and copies ran while one was open for 3% of the time, Pallas kernels for 15%

profile of v3, /device:TPU:1, one launch (start us, length us, event | category | flops | bytes accessed | tf_op | source)
XLA Modules:
  0.0 115.1 jit_solution(733096461887540297)
XLA Ops:
  0.6 1.6 %shard_map.58 = bf16[16,16,896]{2,1,0:T(8,128)(2,1)} custom-call(s32[16]{0:T(128)} %targets.1, bf16[16,768]{1,0:T(8,128)(2,1)} %hidden_ref.1), custom_call_target="tpu_custom_call" | custom-call | tf_op jit(solution)/shard_map/pallas_call | solution.py:64
  2.2 11.7 %all-to-all-start = ((bf16[16,16,896]{2,1,0:T(8,128)(2,1)}), bf16[16,16,896]{2,1,0:T(8,128)(2,1)S(1)}, u32[]{:S(2)}, u32[]{:S(2)}) async-start(bf16[16,16,896]{2,1,0:T(8,128)(2,1)} %shard_map.58), calls=%async_computation | async-start | bytes 917504 | tf_op jit(solution)/shard_map/all_to_all | solution.py:315
  14.0 15.4 %all-to-all-done = bf16[16,16,896]{2,1,0:T(8,128)(2,1)S(1)} async-done(((bf16[16,16,896]{2,1,0:T(8,128)(2,1)}), bf16[16,16,896]{2,1,0:T(8,128)(2,1)S(1)}, u32[]{:S(2)}, u32[]{:S(2)}) %all-to-all-start) | async-done | bytes 458784 | tf_op jit(solution)/shard_map/all_to_all | solution.py:315
  29.3 0.0 copy-start
  29.4 3.1 %fusion.4 = f16[256,2048]{1,0:T(8,128)(2,1)S(1)} fusion(bf16[4096,768]{1,0:T(8,128)(2,1)} %w_ref.1, s32[]{:T(128)S(6)} %select_n.80, bf16[256,896]{1,0:T(8,128)(2,1)S(1)} %bitcast.32), kind=kOutput, calls=%fused_computation.4 | convolution fusion | flops 805830656 | bytes 4587524 | tf_op jit(solution)/shard_map/dot_general | solution.py:323
  32.4 2.9 %collective-permute-start = (f16[256,2048]{1,0:T(8,128)(2,1)S(1)}, f16[256,2048]{1,0:T(8,128)(2,1)S(1)}, u32[]{:S(2)}, u32[]{:S(2)}) collective-permute-start(f16[256,2048]{1,0:T(8,128)(2,1)S(1)} %fusion.4), channel_id=1, source_target_pairs={{0,1},{1,0},{2,3},{3,2},{4,5},{5,4},{6,7},{7,6},{8,9},{9,8},{10,11... | collective-permute-start | bytes 3145736 | tf_op jit(solution)/shard_map/ppermute | solution.py:324
  35.3 2.9 %fusion.2 = f32[256,2048]{1,0:T(8,128)S(1)} fusion(bf16[4096,768]{1,0:T(8,128)(2,1)} %w_ref.1, s32[]{:T(128)S(6)} %select_n.78, bf16[256,896]{1,0:T(8,128)(2,1)S(1)} %bitcast.33), kind=kOutput, calls=%fused_computation.2 | convolution fusion | flops 805306368 | bytes 5636100 | tf_op jit(solution)/shard_map/dot_general | solution.py:325
  38.2 0.0 collective-permute-done
  38.2 0.4 add_convert_fusion.6
  38.6 1.3 %collective-permute-start.1 = (f16[32,2048]{1,0:T(8,128)(2,1)S(1)}, f16[32,2048]{1,0:T(8,128)(2,1)S(1)}, u32[]{:S(2)}, u32[]{:S(2)}) collective-permute-start(f16[32,2048]{1,0:T(8,128)(2,1)S(1)} %get-tuple-element.21), channel_id=1, source_target_pairs={{0,4},{2,6},{4,8},{6,10},{8,12},{10,14},{12,0},{14,2},{1,5},{3,7},... | collective-permute-start | bytes 393224 | tf_op jit(solution)/shard_map/ppermute | solution.py:34
  39.9 1.7 %collective-permute-start.7 = (f16[32,2048]{1,0:T(8,128)(2,1)S(1)}, f16[32,2048]{1,0:T(8,128)(2,1)S(1)}, u32[]{:S(2)}, u32[]{:S(2)}) collective-permute-start(f16[32,2048]{1,0:T(8,128)(2,1)S(1)} %get-tuple-element.22), channel_id=1, source_target_pairs={{0,14},{2,12},{4,2},{6,0},{8,6},{10,4},{12,10},{14,8},{1,15},{3,13... | collective-permute-start | bytes 393224 | tf_op jit(solution)/shard_map/ppermute | solution.py:34
  41.7 0.6 collective-permute-start.6
  42.3 2.4 %collective-permute-start.5 = (f16[32,2048]{1,0:T(8,128)(2,1)S(1)}, f16[32,2048]{1,0:T(8,128)(2,1)S(1)}, u32[]{:S(2)}, u32[]{:S(2)}) collective-permute-start(f16[32,2048]{1,0:T(8,128)(2,1)S(1)} %get-tuple-element.24), channel_id=1, source_target_pairs={{0,8},{2,10},{4,12},{6,14},{8,0},{10,2},{12,4},{14,6},{1,9},{3,11}... | collective-permute-start | bytes 393224 | tf_op jit(solution)/shard_map/ppermute | solution.py:34
  44.7 0.8 collective-permute-start.4
  45.5 0.0 collective-permute-done.1
  45.5 0.9 collective-permute-start.3
  46.4 0.0 collective-permute-done.7
  46.4 2.7 %collective-permute-start.2 = (f16[32,2048]{1,0:T(8,128)(2,1)S(1)}, f16[32,2048]{1,0:T(8,128)(2,1)S(1)}, u32[]{:S(2)}, u32[]{:S(2)}) collective-permute-start(f16[32,2048]{1,0:T(8,128)(2,1)S(1)} %get-tuple-element.27), channel_id=1, source_target_pairs={{0,12},{2,14},{4,0},{6,2},{8,4},{10,6},{12,8},{14,10},{1,13},{3,15... | collective-permute-start | bytes 393224 | tf_op jit(solution)/shard_map/ppermute | solution.py:34
  49.1 0.1 pad_add_fusion.place
  49.2 0.0 copy-done
  49.2 0.6 collective-permute-done.6
  49.8 3.7 %collective-permute-done.5 = f16[32,2048]{1,0:T(8,128)(2,1)S(1)} collective-permute-done((f16[32,2048]{1,0:T(8,128)(2,1)S(1)}, f16[32,2048]{1,0:T(8,128)(2,1)S(1)}, u32[]{:S(2)}, u32[]{:S(2)}) %collective-permute-start.5) | collective-permute-done | bytes 131104 | tf_op jit(solution)/shard_map/ppermute | solution.py:34
  53.5 0.0 collective-permute-done.4
  53.5 0.8 collective-permute-done.3
  54.3 0.3 collective-permute-done.2
  54.5 0.1 convert_add_fusion.logits_ref
  54.7 0.8 shard_map.59.refs_0_
  55.5 3.4 %collective-permute-start.14 = (bf16[32,2176]{1,0:T(8,128)(2,1)S(1)}, bf16[32,2176]{1,0:T(8,128)(2,1)S(1)}, u32[]{:S(2)}, u32[]{:S(2)}) collective-permute-start(bf16[32,2176]{1,0:T(8,128)(2,1)S(1)} %shard_map.59.refs_0_), channel_id=1, source_target_pairs={{0,14},{2,12},{4,2},{6,0},{8,6},{10,4},{12,10},{14,8},{1,15},{3,13... | collective-permute-start | bytes 417800 | tf_op jit(solution)/shard_map/ppermute | solution.py:34
  58.9 0.0 collective-permute-start.13
  58.9 1.5 %collective-permute-start.12 = (bf16[32,2176]{1,0:T(8,128)(2,1)S(1)}, bf16[32,2176]{1,0:T(8,128)(2,1)S(1)}, u32[]{:S(2)}, u32[]{:S(2)}) collective-permute-start(bf16[32,2176]{1,0:T(8,128)(2,1)S(1)} %shard_map.59.refs_0_), channel_id=1, source_target_pairs={{0,8},{2,10},{4,12},{6,14},{8,0},{10,2},{12,4},{14,6},{1,9},{3,11}... | collective-permute-start | bytes 417800 | tf_op jit(solution)/shard_map/ppermute | solution.py:34
  60.5 2.0 %collective-permute-start.11 = (bf16[32,2176]{1,0:T(8,128)(2,1)S(1)}, bf16[32,2176]{1,0:T(8,128)(2,1)S(1)}, u32[]{:S(2)}, u32[]{:S(2)}) collective-permute-start(bf16[32,2176]{1,0:T(8,128)(2,1)S(1)} %shard_map.59.refs_0_), channel_id=1, source_target_pairs={{0,10},{2,8},{4,14},{6,12},{8,2},{10,0},{12,6},{14,4},{1,11},{3,9}... | collective-permute-start | bytes 417800 | tf_op jit(solution)/shard_map/ppermute | solution.py:34
  62.5 0.6 collective-permute-start.10
  63.1 0.0 collective-permute-done.14.refs_7_
  63.1 3.3 %collective-permute-start.9 = (bf16[32,2176]{1,0:T(8,128)(2,1)S(1)}, bf16[32,2176]{1,0:T(8,128)(2,1)S(1)}, u32[]{:S(2)}, u32[]{:S(2)}) collective-permute-start(bf16[32,2176]{1,0:T(8,128)(2,1)S(1)} %shard_map.59.refs_0_), channel_id=1, source_target_pairs={{0,12},{2,14},{4,0},{6,2},{8,4},{10,6},{12,8},{14,10},{1,13},{3,15... | collective-permute-start | bytes 417800 | tf_op jit(solution)/shard_map/ppermute | solution.py:34
  66.4 0.0 collective-permute-done.13.refs_6_
  66.4 0.5 collective-permute-start.8
  66.8 0.1 stack.64.place
  66.9 4.3 %collective-permute-done.12.refs_5_ = bf16[32,2176]{1,0:T(8,128)(2,1)S(1)} collective-permute-done((bf16[32,2176]{1,0:T(8,128)(2,1)S(1)}, bf16[32,2176]{1,0:T(8,128)(2,1)S(1)}, u32[]{:S(2)}, u32[]{:S(2)}) %collective-permute-start.12) | collective-permute-done | bytes 139296 | tf_op jit(solution)/shard_map/ppermute | solution.py:34
  71.2 0.0 collective-permute-done.11.refs_4_
  71.2 0.4 collective-permute-done.10.refs_3_
  71.7 0.7 collective-permute-done.9.refs_2_
  72.4 1.8 %collective-permute-done.8.refs_1_ = bf16[32,2176]{1,0:T(8,128)(2,1)S(1)} collective-permute-done((bf16[32,2176]{1,0:T(8,128)(2,1)S(1)}, bf16[32,2176]{1,0:T(8,128)(2,1)S(1)}, u32[]{:S(2)}, u32[]{:S(2)}) %collective-permute-start.8) | collective-permute-done | bytes 139296 | tf_op jit(solution)/shard_map/ppermute | solution.py:34
  74.2 0.7 shard_map.60
  74.9 1.6 %collective-permute-start.15 = (f32[8,256]{1,0:T(8,128)S(1)}, f32[8,256]{1,0:T(8,128)S(1)}, u32[]{:S(2)}, u32[]{:S(2)}) collective-permute-start(f32[8,256]{1,0:T(8,128)S(1)} %get-tuple-element.11.own_ref), channel_id=1, source_target_pairs={{0,1},{1,0},{2,3},{3,2},{4,5},{5,4},{6,7},{7,6},{8,9},{9,8},{10,11... | collective-permute-start | bytes 24584 | tf_op jit(solution)/shard_map/ppermute | solution.py:343
  76.5 0.8 collective-permute-done.15.oth_ref
  77.3 0.3 collective-permute-start.16
  77.7 0.1 pad_add_fusion.1.place
  77.7 0.7 shard_map.61
  78.4 3.5 %all-to-all-start.1 = ((f32[16,8,256]{2,1,0:T(8,128)}), f32[16,8,256]{2,1,0:T(8,128)S(1)}, u32[]{:S(2)}, u32[]{:S(2)}) async-start(f32[16,8,256]{2,1,0:T(8,128)} %shard_map.61), calls=%async_computation.1 | async-start | bytes 262144 | tf_op jit(solution)/shard_map/all_to_all | solution.py:346
  81.9 0.0 collective-permute-done.16.oth_ref
  81.9 7.8 %shard_map.62 = (f32[2,256,768]{2,1,0:T(8,128)S(1)}, bf16[256,768]{1,0:T(8,128)(2,1)S(1)}) custom-call(s32[3]{0:T(128)S(1)} %pad_add_fusion.1.place, bf16[256,2176]{1,0:T(8,128)(2,1)S(1)} %get-tuple-element.14.own_ref, bf16[256,128]{1,0:T(8,128)(2,1)S(1)} %slice.25.ids_ref, bf16[256,2176]{1,0:T(8,128)(2,1)} %collective-permute-done.16.oth_ref, ...), custom_call_target="tpu_custom_call" | custom-call | flops 3221225472 | bytes 6291456 | tf_op jit(solution)/shard_map/pallas_call | solution.py:224
  89.7 2.7 %all-to-all-done.1.every_ref = f32[16,8,256]{2,1,0:T(8,128)S(1)} async-done(((f32[16,8,256]{2,1,0:T(8,128)}), f32[16,8,256]{2,1,0:T(8,128)S(1)}, u32[]{:S(2)}, u32[]{:S(2)}) %all-to-all-start.1) | async-done | bytes 131104 | tf_op jit(solution)/shard_map/all_to_all | solution.py:346
  92.4 0.2 shard_map.63
  92.6 0.2 slice_reduce_fusion.1
  92.8 1.0 fusion.10
  93.9 6.3 %all-to-all-start.2 = ((f16[16,16,768]{2,1,0:T(8,128)(2,1)}), f16[16,16,768]{2,1,0:T(8,128)(2,1)S(1)}, u32[]{:S(2)}, u32[]{:S(2)}) async-start(f16[16,16,768]{2,1,0:T(8,128)(2,1)} %bitcast.36), calls=%async_computation.2 | async-start | bytes 786432 | tf_op jit(solution)/shard_map/all_to_all | solution.py:354
  100.2 0.1 pad_add_fusion.2.place
  100.3 0.6 fusion.15
  100.8 9.1 %shard_map.64 = bf16[4096,768]{1,0:T(8,128)(2,1)} custom-call(s32[3]{0:T(128)S(1)} %pad_add_fusion.2.place, bf16[256,2176]{1,0:T(8,128)(2,1)S(1)} %get-tuple-element.14.own_ref, bf16[256,2176]{1,0:T(8,128)(2,1)} %collective-permute-done.16.oth_ref, bf16[256,896]{1,0:T(8,128)(2,1)} %bitcast.35, bf16[256,128]{1,0:T(8,128)(2,1)S(1)} %slice.25.ids_ref, ...), custom_call_target="tpu_custom_call" | custom-call | flops 1610612736 | bytes 8388608 | tf_op jit(solution)/shard_map/pallas_call | solution.py:281
  110.0 4.4 %all-to-all-done.2 = f16[16,16,768]{2,1,0:T(8,128)(2,1)S(1)} async-done(((f16[16,16,768]{2,1,0:T(8,128)(2,1)}), f16[16,16,768]{2,1,0:T(8,128)(2,1)S(1)}, u32[]{:S(2)}, u32[]{:S(2)}) %all-to-all-start.2) | async-done | bytes 393248 | tf_op jit(solution)/shard_map/all_to_all | solution.py:354
  114.4 0.7 multiply_reduce_fusion
  (1 shorter events, 0.0 us)
Async XLA Ops:
  2.2 27.2 %all-to-all-start = ((bf16[16,16,896]{2,1,0:T(8,128)(2,1)}), bf16[16,16,896]{2,1,0:T(8,128)(2,1)S(1)}, u32[]{:S(2)}, u32[]{:S(2)}) async-start(bf16[16,16,896]{2,1,0:T(8,128)(2,1)} %shard_map.58), calls=%async_computation | async-start | bytes 917504 | tf_op jit(solution)/shard_map/all_to_all | solution.py:315
  29.3 19.8 %copy-start = (bf16[16,16,896]{2,1,0:T(8,128)(2,1)}, bf16[16,16,896]{2,1,0:T(8,128)(2,1)S(1)}, u32[]{:S(2)}) copy-start(bf16[16,16,896]{2,1,0:T(8,128)(2,1)S(1)} %all-to-all-done) | copy-start | bytes 1376260
  32.4 5.8 %collective-permute-start = (f16[256,2048]{1,0:T(8,128)(2,1)S(1)}, f16[256,2048]{1,0:T(8,128)(2,1)S(1)}, u32[]{:S(2)}, u32[]{:S(2)}) collective-permute-start(f16[256,2048]{1,0:T(8,128)(2,1)S(1)} %fusion.4), channel_id=1, source_target_pairs={{0,1},{1,0},{2,3},{3,2},{4,5},{5,4},{6,7},{7,6},{8,9},{9,8},{10,11... | collective-permute-start | bytes 3145736 | tf_op jit(solution)/shard_map/ppermute | solution.py:324
  38.6 6.9 %collective-permute-start.1 = (f16[32,2048]{1,0:T(8,128)(2,1)S(1)}, f16[32,2048]{1,0:T(8,128)(2,1)S(1)}, u32[]{:S(2)}, u32[]{:S(2)}) collective-permute-start(f16[32,2048]{1,0:T(8,128)(2,1)S(1)} %get-tuple-element.21), channel_id=1, source_target_pairs={{0,4},{2,6},{4,8},{6,10},{8,12},{10,14},{12,0},{14,2},{1,5},{3,7},... | collective-permute-start | bytes 393224 | tf_op jit(solution)/shard_map/ppermute | solution.py:34
  39.9 6.5 %collective-permute-start.7 = (f16[32,2048]{1,0:T(8,128)(2,1)S(1)}, f16[32,2048]{1,0:T(8,128)(2,1)S(1)}, u32[]{:S(2)}, u32[]{:S(2)}) collective-permute-start(f16[32,2048]{1,0:T(8,128)(2,1)S(1)} %get-tuple-element.22), channel_id=1, source_target_pairs={{0,14},{2,12},{4,2},{6,0},{8,6},{10,4},{12,10},{14,8},{1,15},{3,13... | collective-permute-start | bytes 393224 | tf_op jit(solution)/shard_map/ppermute | solution.py:34
  41.7 8.1 %collective-permute-start.6 = (f16[32,2048]{1,0:T(8,128)(2,1)S(1)}, f16[32,2048]{1,0:T(8,128)(2,1)S(1)}, u32[]{:S(2)}, u32[]{:S(2)}) collective-permute-start(f16[32,2048]{1,0:T(8,128)(2,1)S(1)} %get-tuple-element.23), channel_id=1, source_target_pairs={{0,6},{2,4},{4,10},{6,8},{8,14},{10,12},{12,2},{14,0},{1,7},{3,5},... | collective-permute-start | bytes 393224 | tf_op jit(solution)/shard_map/ppermute | solution.py:34
  42.3 11.2 %collective-permute-start.5 = (f16[32,2048]{1,0:T(8,128)(2,1)S(1)}, f16[32,2048]{1,0:T(8,128)(2,1)S(1)}, u32[]{:S(2)}, u32[]{:S(2)}) collective-permute-start(f16[32,2048]{1,0:T(8,128)(2,1)S(1)} %get-tuple-element.24), channel_id=1, source_target_pairs={{0,8},{2,10},{4,12},{6,14},{8,0},{10,2},{12,4},{14,6},{1,9},{3,11}... | collective-permute-start | bytes 393224 | tf_op jit(solution)/shard_map/ppermute | solution.py:34
  44.7 8.8 %collective-permute-start.4 = (f16[32,2048]{1,0:T(8,128)(2,1)S(1)}, f16[32,2048]{1,0:T(8,128)(2,1)S(1)}, u32[]{:S(2)}, u32[]{:S(2)}) collective-permute-start(f16[32,2048]{1,0:T(8,128)(2,1)S(1)} %get-tuple-element.25), channel_id=1, source_target_pairs={{0,10},{2,8},{4,14},{6,12},{8,2},{10,0},{12,6},{14,4},{1,11},{3,9}... | collective-permute-start | bytes 393224 | tf_op jit(solution)/shard_map/ppermute | solution.py:34
  45.5 8.7 %collective-permute-start.3 = (f16[32,2048]{1,0:T(8,128)(2,1)S(1)}, f16[32,2048]{1,0:T(8,128)(2,1)S(1)}, u32[]{:S(2)}, u32[]{:S(2)}) collective-permute-start(f16[32,2048]{1,0:T(8,128)(2,1)S(1)} %get-tuple-element.26), channel_id=1, source_target_pairs={{0,2},{2,0},{4,6},{6,4},{8,10},{10,8},{12,14},{14,12},{1,3},{3,1},... | collective-permute-start | bytes 393224 | tf_op jit(solution)/shard_map/ppermute | solution.py:34
  46.4 8.1 %collective-permute-start.2 = (f16[32,2048]{1,0:T(8,128)(2,1)S(1)}, f16[32,2048]{1,0:T(8,128)(2,1)S(1)}, u32[]{:S(2)}, u32[]{:S(2)}) collective-permute-start(f16[32,2048]{1,0:T(8,128)(2,1)S(1)} %get-tuple-element.27), channel_id=1, source_target_pairs={{0,12},{2,14},{4,0},{6,2},{8,4},{10,6},{12,8},{14,10},{1,13},{3,15... | collective-permute-start | bytes 393224 | tf_op jit(solution)/shard_map/ppermute | solution.py:34
  55.5 7.6 %collective-permute-start.14 = (bf16[32,2176]{1,0:T(8,128)(2,1)S(1)}, bf16[32,2176]{1,0:T(8,128)(2,1)S(1)}, u32[]{:S(2)}, u32[]{:S(2)}) collective-permute-start(bf16[32,2176]{1,0:T(8,128)(2,1)S(1)} %shard_map.59.refs_0_), channel_id=1, source_target_pairs={{0,14},{2,12},{4,2},{6,0},{8,6},{10,4},{12,10},{14,8},{1,15},{3,13... | collective-permute-start | bytes 417800 | tf_op jit(solution)/shard_map/ppermute | solution.py:34
  58.9 7.4 %collective-permute-start.13 = (bf16[32,2176]{1,0:T(8,128)(2,1)S(1)}, bf16[32,2176]{1,0:T(8,128)(2,1)S(1)}, u32[]{:S(2)}, u32[]{:S(2)}) collective-permute-start(bf16[32,2176]{1,0:T(8,128)(2,1)S(1)} %shard_map.59.refs_0_), channel_id=1, source_target_pairs={{0,6},{2,4},{4,10},{6,8},{8,14},{10,12},{12,2},{14,0},{1,7},{3,5},... | collective-permute-start | bytes 417800 | tf_op jit(solution)/shard_map/ppermute | solution.py:34
  58.9 12.3 %collective-permute-start.12 = (bf16[32,2176]{1,0:T(8,128)(2,1)S(1)}, bf16[32,2176]{1,0:T(8,128)(2,1)S(1)}, u32[]{:S(2)}, u32[]{:S(2)}) collective-permute-start(bf16[32,2176]{1,0:T(8,128)(2,1)S(1)} %shard_map.59.refs_0_), channel_id=1, source_target_pairs={{0,8},{2,10},{4,12},{6,14},{8,0},{10,2},{12,4},{14,6},{1,9},{3,11}... | collective-permute-start | bytes 417800 | tf_op jit(solution)/shard_map/ppermute | solution.py:34
  60.5 10.8 %collective-permute-start.11 = (bf16[32,2176]{1,0:T(8,128)(2,1)S(1)}, bf16[32,2176]{1,0:T(8,128)(2,1)S(1)}, u32[]{:S(2)}, u32[]{:S(2)}) collective-permute-start(bf16[32,2176]{1,0:T(8,128)(2,1)S(1)} %shard_map.59.refs_0_), channel_id=1, source_target_pairs={{0,10},{2,8},{4,14},{6,12},{8,2},{10,0},{12,6},{14,4},{1,11},{3,9}... | collective-permute-start | bytes 417800 | tf_op jit(solution)/shard_map/ppermute | solution.py:34
  62.5 9.2 %collective-permute-start.10 = (bf16[32,2176]{1,0:T(8,128)(2,1)S(1)}, bf16[32,2176]{1,0:T(8,128)(2,1)S(1)}, u32[]{:S(2)}, u32[]{:S(2)}) collective-permute-start(bf16[32,2176]{1,0:T(8,128)(2,1)S(1)} %shard_map.59.refs_0_), channel_id=1, source_target_pairs={{0,2},{2,0},{4,6},{6,4},{8,10},{10,8},{12,14},{14,12},{1,3},{3,1},... | collective-permute-start | bytes 417800 | tf_op jit(solution)/shard_map/ppermute | solution.py:34
  63.1 9.3 %collective-permute-start.9 = (bf16[32,2176]{1,0:T(8,128)(2,1)S(1)}, bf16[32,2176]{1,0:T(8,128)(2,1)S(1)}, u32[]{:S(2)}, u32[]{:S(2)}) collective-permute-start(bf16[32,2176]{1,0:T(8,128)(2,1)S(1)} %shard_map.59.refs_0_), channel_id=1, source_target_pairs={{0,12},{2,14},{4,0},{6,2},{8,4},{10,6},{12,8},{14,10},{1,13},{3,15... | collective-permute-start | bytes 417800 | tf_op jit(solution)/shard_map/ppermute | solution.py:34
  66.4 7.8 %collective-permute-start.8 = (bf16[32,2176]{1,0:T(8,128)(2,1)S(1)}, bf16[32,2176]{1,0:T(8,128)(2,1)S(1)}, u32[]{:S(2)}, u32[]{:S(2)}) collective-permute-start(bf16[32,2176]{1,0:T(8,128)(2,1)S(1)} %shard_map.59.refs_0_), channel_id=1, source_target_pairs={{0,4},{2,6},{4,8},{6,10},{8,12},{10,14},{12,0},{14,2},{1,5},{3,7},... | collective-permute-start | bytes 417800 | tf_op jit(solution)/shard_map/ppermute | solution.py:34
  74.9 2.5 %collective-permute-start.15 = (f32[8,256]{1,0:T(8,128)S(1)}, f32[8,256]{1,0:T(8,128)S(1)}, u32[]{:S(2)}, u32[]{:S(2)}) collective-permute-start(f32[8,256]{1,0:T(8,128)S(1)} %get-tuple-element.11.own_ref), channel_id=1, source_target_pairs={{0,1},{1,0},{2,3},{3,2},{4,5},{5,4},{6,7},{7,6},{8,9},{9,8},{10,11... | collective-permute-start | bytes 24584 | tf_op jit(solution)/shard_map/ppermute | solution.py:343
  77.3 4.6 %collective-permute-start.16 = (bf16[256,2176]{1,0:T(8,128)(2,1)S(1)}, bf16[256,2176]{1,0:T(8,128)(2,1)}, u32[]{:S(2)}, u32[]{:S(2)}) collective-permute-start(bf16[256,2176]{1,0:T(8,128)(2,1)S(1)} %get-tuple-element.14.own_ref), channel_id=1, source_target_pairs={{0,1},{1,0},{2,3},{3,2},{4,5},{5,4},{6,7},{7,6},{8,9},{9,8},{10,11... | collective-permute-start | bytes 3342344 | tf_op jit(solution)/shard_map/ppermute | solution.py:345
  78.4 14.0 %all-to-all-start.1 = ((f32[16,8,256]{2,1,0:T(8,128)}), f32[16,8,256]{2,1,0:T(8,128)S(1)}, u32[]{:S(2)}, u32[]{:S(2)}) async-start(f32[16,8,256]{2,1,0:T(8,128)} %shard_map.61), calls=%async_computation.1 | async-start | bytes 262144 | tf_op jit(solution)/shard_map/all_to_all | solution.py:346
  93.9 20.5 %all-to-all-start.2 = ((f16[16,16,768]{2,1,0:T(8,128)(2,1)}), f16[16,16,768]{2,1,0:T(8,128)(2,1)S(1)}, u32[]{:S(2)}, u32[]{:S(2)}) async-start(f16[16,16,768]{2,1,0:T(8,128)(2,1)} %bitcast.36), calls=%async_computation.2 | async-start | bytes 786432 | tf_op jit(solution)/shard_map/all_to_all | solution.py:354

commit v4 on v3

--- a/solution.py
+++ b/solution.py
@@ -42,8 +42,11 @@
     return pltpu.CompilerParams(vmem_limit_bytes=mib << 20)
 
 
-def pack_kernel(targets, hidden_ref, out_ref):
+def pack_kernel(targets_ref, hidden_ref, out_ref, targets, sem):
+    copy = pltpu.make_async_copy(targets_ref, targets, sem)
+    copy.start()
     rows, width = hidden_ref.shape
+    copy.wait()
     row = lax.broadcasted_iota(jnp.int32, (rows, 128), 0)
     lane = lax.broadcasted_iota(jnp.int32, (rows, 128), 1)
     ids = jnp.zeros((rows, 128), jnp.int32)
@@ -54,20 +57,45 @@
         ids = jnp.where((row == r) & (lane == 0), high, ids)
         ids = jnp.where((row == r) & (lane == 1), low, ids)
     ids = ids.astype(jnp.float32).astype(jnp.bfloat16)
-    for d in range(out_ref.shape[0]):
-        out_ref[d, :, :width] = hidden_ref[...]
-        out_ref[d, :, width:] = ids
-
-
-def pack(hidden, targets, copies):
+    out_ref[:, :width] = hidden_ref[...]
+    out_ref[:, width:] = ids
+
+
+def pack(hidden, targets):
     rows, width = hidden.shape
     return pl.pallas_call(
         pack_kernel,
-        in_specs=[pl.BlockSpec(memory_space=pltpu.SMEM), pl.BlockSpec(memory_space=pltpu.VMEM)],
-        out_specs=pl.BlockSpec(memory_space=pltpu.VMEM),
-        out_shape=jax.ShapeDtypeStruct((copies, rows, width + 128), jnp.bfloat16),
-        compiler_params=params(60),
-    )(targets, hidden)
+        grid=(1,),
+        in_specs=[pl.BlockSpec(memory_space=pltpu.HBM), pl.BlockSpec((rows, width), lambda i: (0, 0))],
+        out_specs=pl.BlockSpec((rows, width + 128), lambda i: (0, 0)),
+        out_shape=jax.ShapeDtypeStruct((rows, width + 128), jnp.bfloat16),
+        scratch_shapes=[pltpu.SMEM((rows,), jnp.int32), pltpu.SemaphoreType.DMA],
+        compiler_params=params(4),
+    )(far(targets), far(hidden))
+
+
+def order_kernel(place, *refs):
+    rows = refs[0].shape[0]
+    for r, block in enumerate(refs[:-1]):
+        refs[-1][pl.ds(pl.multiple_of(place[r] * rows, rows), rows)] = block[...]
+
+
+def around(v, axis):
+    rows, width = v.shape
+    me = lax.axis_index(axis)
+    ring = [lax.ppermute(v, axis, [(i, (i + k) % 4) for i in range(4)]) for k in (1, 3, 2)]
+    place = jnp.stack([me] + [lax.rem(me + 4 - k, 4) for k in (1, 3, 2)])
+    return pl.pallas_call(
+        order_kernel,
+        grid_spec=pltpu.PrefetchScalarGridSpec(
+            num_scalar_prefetch=1,
+            grid=(1,),
+            in_specs=[pl.BlockSpec((rows, width), lambda i, s: (0, 0))] * 4,
+            out_specs=pl.BlockSpec((4 * rows, width), lambda i, s: (0, 0)),
+        ),
+        out_shape=jax.ShapeDtypeStruct((4 * rows, width), v.dtype),
+        compiler_params=params(8),
+    )(place, v, *ring)
 
 
 def softmax_kernel(place, logits_ref, ids_ref, out_ref):
@@ -190,32 +218,31 @@
     return step, copies
 
 
-def product_kernel(place, own_ref, ids_ref, oth_ref, w_ref, u_ref, t_ref, held, other, sems, sem):
+def product_kernel(place, own_ref, ids_ref, oth_ref, w_ref, u_ref, t_ref, held, other, both, sems, sem):
     step, copies = row_blocks(place, w_ref, held, sems)
     fetch = pltpu.make_async_copy(oth_ref, other, sem)
-    copies[0].start()
-    copies[1].start()
-    fetch.start()
     per_half = len(copies) // 2
+    half = step * per_half
+    for copy in copies[:per_half]:
+        copy.start()
     target = decode(ids_ref[...])
     tokens = target.shape[0]
     t = None
     for which, p_ref in enumerate((own_ref, other)):
-        u = None
-        for k in range(per_half):
-            slot = which * per_half + k
-            if slot == per_half:
-                fetch.wait()
-            columns = lax.broadcasted_iota(jnp.int32, (tokens, step), 1) + (place[2] + place[which] + k * step)
-            onehot = jnp.where(columns == target, 1.0, 0.0).astype(jnp.bfloat16)
-            both = jnp.concatenate([p_ref[:, k * step : (k + 1) * step], onehot], axis=0)
-            copies[slot].wait()
-            if slot + 2 < len(copies):
-                copies[slot + 2].start()
-            d = jnp.dot(both, held[slot * step : (slot + 1) * step], preferred_element_type=jnp.float32)
-            u = d[:tokens] if u is None else u + d[:tokens]
-            t = d[tokens:] if t is None else t + d[tokens:]
-        u_ref[which] = u
+        columns = lax.broadcasted_iota(jnp.int32, (tokens, half), 1) + (place[2] + place[which])
+        both[tokens:] = jnp.where(columns == target, 1.0, 0.0).astype(jnp.bfloat16)
+        if which == 1:
+            fetch.wait()
+        both[:tokens] = p_ref[:, :half]
+        for copy in copies[which * per_half : (which + 1) * per_half]:
+            copy.wait()
+        if which == 0:
+            fetch.start()
+            for copy in copies[per_half:]:
+                copy.start()
+        d = jnp.dot(both[...], held[which * half : (which + 1) * half], preferred_element_type=jnp.float32)
+        u_ref[which] = d[:tokens]
+        t = d[tokens:] if t is None else t + d[tokens:]
     t_ref[...] = t.astype(jnp.bfloat16)
 
 
@@ -227,8 +254,8 @@
             num_scalar_prefetch=1,
             grid=(1,),
             in_specs=[
-                pl.BlockSpec(own.shape, lambda i, s: (0, 0)),
-                pl.BlockSpec(ids.shape, lambda i, s: (0, 0)),
+                pl.BlockSpec(memory_space=pltpu.VMEM),
+                pl.BlockSpec(memory_space=pltpu.VMEM),
                 pl.BlockSpec(memory_space=pltpu.HBM),
                 pl.BlockSpec(memory_space=pltpu.HBM),
             ],
@@ -239,6 +266,7 @@
             scratch_shapes=[
                 pltpu.VMEM(weight.shape, weight.dtype),
                 pltpu.VMEM(oth.shape, oth.dtype),
+                pltpu.VMEM((2 * tokens, weight.shape[0] // 2), jnp.bfloat16),
                 pltpu.SemaphoreType.DMA((4,)),
                 pltpu.SemaphoreType.DMA,
             ],
@@ -312,7 +340,7 @@
     base_own = section * vocab + core * half
     base_oth = section * vocab + (1 - core) * half
 
-    gathered = lax.all_to_all(pack(hidden, targets, 16), PIPE, 0, 0).reshape(16 * rows, width + 128)
+    gathered = around(around(pack(hidden, targets), "zh"), "y")
     tokens = gathered.shape[0]
     per_chip = tokens // 8
     full, ids = gathered[:, :width], gathered[:, width:]

time: 116 us -> 115 us (level)
  waiting for transfers between devices: 36 us -> 30.3 us
  starting transfers between devices: 48.2 us -> 52.4 us
    all_to_all x1 -> x0, waiting for transfers between devices: 15.4 us -> none  [shards(): lax.all_to_all(pack(hidden, targets, 16), PIPE, 0, 0)]
    ppermute x0 -> x6, starting transfers between devices: none -> 14.7 us  [around(): lax.ppermute(v, axis, [(i, (i + k) % 4) for i in range(4)])]
    all_to_all x1 -> x0, starting transfers between devices: 11.7 us -> none  [shards(): lax.all_to_all(pack(hidden, targets, 16), PIPE, 0, 0)]
    ppermute x0 -> x6, waiting for transfers between devices: none -> 7.34 us  [around(): lax.ppermute(v, axis, [(i, (i + k) % 4) for i in range(4)])]
    all_to_all x1, starting transfers between devices: 3.51 us -> 5.39 us  [shards(): everyone = lax.all_to_all(join_stats(st_own, st_oth, 16), PIPE, 0, 0)]
    ppermute x14, waiting for transfers between devices: 12.6 us -> 14 us  [to_chip(): return lax.ppermute(v, CHIPS, pairs)]
    pallas_call x1 -> x3, Pallas kernels: 1.56 us -> 2.57 us  [the longest x1 1.44 us: pack(): pl.pallas_call(pack_kernel, grid=(1,), in_specs=[pl.BlockSpec(memory_spac...]
  transfers between devices with their start and end apart: 20 -> 25, of which waited for: 12 -> 13; matrix products, arithmetic and copies ran while one was open for 3% -> 3% of each run, Pallas kernels for 15% -> 15%
where the time goes in v4:
time: 115 us; the launch traced here: 114 us
  starting transfers between devices  52.4 us (46%)
  waiting for transfers between devices  30.3 us (26%)
  Pallas kernels  21.1 us (18%)
  matrix products  5.97 us (5%)
  other arithmetic  2.64 us (2%)
    ppermute x14, starting transfers between devices, to_chip(): return lax.ppermute(v, CHIPS, pairs)  21.9 us
    ppermute x6, starting transfers between devices, around(): lax.ppermute(v, axis, [(i, (i + k) % 4) for i in range(4)])  14.7 us
    ppermute x14, waiting for transfers between devices, to_chip(): return lax.ppermute(v, CHIPS, pairs)  14 us
    pallas_call x1, Pallas kernels, weight_gradient(): pl.pallas_call(functools.partial(weight_grad_kernel, steps), grid_spec=pl...  9.12 us
    ppermute x6, waiting for transfers between devices, around(): lax.ppermute(v, axis, [(i, (i + k) % 4) for i in range(4)])  7.34 us
    pallas_call x1, Pallas kernels, products(): pl.pallas_call(product_kernel, grid_spec=pltpu.PrefetchScalarGridSpec(num...  7.1 us
    all_to_all x1, starting transfers between devices, shards(): parts = lax.all_to_all(sent, PIPE, 0, 0)  5.84 us
    all_to_all x1, starting transfers between devices, shards(): everyone = lax.all_to_all(join_stats(st_own, st_oth, 16), PIPE, 0, 0)  5.39 us
  transfers between devices with their start and end apart: 25, of which 13 were waited for; matrix products, arithmetic and copies ran while one was open for 3% of the time, Pallas kernels for 15%

profile of v4, /device:TPU:1, one launch (start us, length us, event | category | flops | bytes accessed | tf_op | source)
XLA Modules:
  0.0 114.2 jit_solution(1656390978015838909)
XLA Ops:
  0.6 1.4 %shard_map.58.refs_0_ = bf16[16,896]{1,0:T(8,128)(2,1)S(1)} custom-call(s32[16]{0:T(128)} %targets_ref.1, bf16[16,768]{1,0:T(8,128)(2,1)} %hidden_ref.1), custom_call_target="tpu_custom_call" | custom-call | tf_op jit(solution)/shard_map/pallas_call | solution.py:66
  2.1 7.8 %collective-permute-start.2 = (bf16[16,896]{1,0:T(8,128)(2,1)S(1)}, bf16[16,896]{1,0:T(8,128)(2,1)S(1)}, u32[]{:S(2)}, u32[]{:S(2)}) collective-permute-start(bf16[16,896]{1,0:T(8,128)(2,1)S(1)} %shard_map.58.refs_0_), channel_id=1, source_target_pairs={{0,32},{16,48},{32,0},{48,16},{1,33},{17,49},{33,1},{49,17},{2,34}... | collective-permute-start | bytes 86024 | tf_op jit(solution)/shard_map/ppermute | solution.py:86
  9.9 0.0 collective-permute-start.1
  9.9 2.4 %collective-permute-start = (bf16[16,896]{1,0:T(8,128)(2,1)S(1)}, bf16[16,896]{1,0:T(8,128)(2,1)S(1)}, u32[]{:S(2)}, u32[]{:S(2)}) collective-permute-start(bf16[16,896]{1,0:T(8,128)(2,1)S(1)} %shard_map.58.refs_0_), channel_id=1, source_target_pairs={{0,16},{16,32},{32,48},{48,0},{1,17},{17,33},{33,49},{49,1},{2,18}... | collective-permute-start | bytes 86024 | tf_op jit(solution)/shard_map/ppermute | solution.py:86
  12.3 0.1 pad_add_fusion.2.place
  12.3 0.0 collective-permute-done.2.refs_3_
  12.3 1.2 %collective-permute-done.1.refs_2_ = bf16[16,896]{1,0:T(8,128)(2,1)S(1)} collective-permute-done((bf16[16,896]{1,0:T(8,128)(2,1)S(1)}, bf16[16,896]{1,0:T(8,128)(2,1)S(1)}, u32[]{:S(2)}, u32[]{:S(2)}) %collective-permute-start.1) | collective-permute-done | bytes 28704 | tf_op jit(solution)/shard_map/ppermute | solution.py:86
  13.5 1.3 %collective-permute-done.refs_1_ = bf16[16,896]{1,0:T(8,128)(2,1)S(1)} collective-permute-done((bf16[16,896]{1,0:T(8,128)(2,1)S(1)}, bf16[16,896]{1,0:T(8,128)(2,1)S(1)}, u32[]{:S(2)}, u32[]{:S(2)}) %collective-permute-start) | collective-permute-done | bytes 28704 | tf_op jit(solution)/shard_map/ppermute | solution.py:86
  14.8 0.6 shard_map.59.refs_0_
  15.4 3.0 %collective-permute-start.5 = (bf16[64,896]{1,0:T(8,128)(2,1)S(1)}, bf16[64,896]{1,0:T(8,128)(2,1)S(1)}, u32[]{:S(2)}, u32[]{:S(2)}) collective-permute-start(bf16[64,896]{1,0:T(8,128)(2,1)S(1)} %shard_map.59.refs_0_), channel_id=1, source_target_pairs={{0,128},{64,192},{128,0},{192,64},{1,129},{65,193},{129,1},{193,65... | collective-permute-start | bytes 344072 | tf_op jit(solution)/shard_map/ppermute | solution.py:86
  18.4 0.8 collective-permute-start.4
  19.2 0.7 collective-permute-start.3
  19.9 0.1 pad_add_fusion.1.place
  19.9 0.7 collective-permute-done.5.refs_3_
  20.6 1.9 %collective-permute-done.4.refs_2_ = bf16[64,896]{1,0:T(8,128)(2,1)S(1)} collective-permute-done((bf16[64,896]{1,0:T(8,128)(2,1)S(1)}, bf16[64,896]{1,0:T(8,128)(2,1)S(1)}, u32[]{:S(2)}, u32[]{:S(2)}) %collective-permute-start.4) | collective-permute-done | bytes 114720 | tf_op jit(solution)/shard_map/ppermute | solution.py:86
  22.5 2.3 %collective-permute-done.3.refs_1_ = bf16[64,896]{1,0:T(8,128)(2,1)S(1)} collective-permute-done((bf16[64,896]{1,0:T(8,128)(2,1)S(1)}, bf16[64,896]{1,0:T(8,128)(2,1)S(1)}, u32[]{:S(2)}, u32[]{:S(2)}) %collective-permute-start.3) | collective-permute-done | bytes 114720 | tf_op jit(solution)/shard_map/ppermute | solution.py:86
  24.8 0.6 shard_map.60.hidden_ref
  25.4 3.1 %fusion.4 = f16[256,2048]{1,0:T(8,128)(2,1)S(1)} fusion(bf16[4096,768]{1,0:T(8,128)(2,1)} %w_ref.1, s32[]{:T(128)S(6)} %select_n.80, bf16[256,896]{1,0:T(8,128)(2,1)S(1)} %shard_map.60.hidden_ref), kind=kOutput, calls=%fused_computation.4 | convolution fusion | flops 805830656 | bytes 4587524 | tf_op jit(solution)/shard_map/dot_general | solution.py:351
  28.5 3.0 %collective-permute-start.6 = (f16[256,2048]{1,0:T(8,128)(2,1)S(1)}, f16[256,2048]{1,0:T(8,128)(2,1)S(1)}, u32[]{:S(2)}, u32[]{:S(2)}) collective-permute-start(f16[256,2048]{1,0:T(8,128)(2,1)S(1)} %fusion.4), channel_id=1, source_target_pairs={{0,1},{1,0},{2,3},{3,2},{4,5},{5,4},{6,7},{7,6},{8,9},{9,8},{10,11... | collective-permute-start | bytes 3145736 | tf_op jit(solution)/shard_map/ppermute | solution.py:352
  31.5 2.9 %fusion.2 = f32[256,2048]{1,0:T(8,128)S(1)} fusion(bf16[4096,768]{1,0:T(8,128)(2,1)} %w_ref.1, s32[]{:T(128)S(6)} %select_n.78, bf16[256,896]{1,0:T(8,128)(2,1)S(1)} %shard_map.60.hidden_ref), kind=kOutput, calls=%fused_computation.2 | convolution fusion | flops 805306368 | bytes 5636100 | tf_op jit(solution)/shard_map/dot_general | solution.py:353
  34.4 0.0 collective-permute-done.6
  34.4 0.4 add_convert_fusion.6
  34.8 1.3 %collective-permute-start.7 = (f16[32,2048]{1,0:T(8,128)(2,1)S(1)}, f16[32,2048]{1,0:T(8,128)(2,1)S(1)}, u32[]{:S(2)}, u32[]{:S(2)}) collective-permute-start(f16[32,2048]{1,0:T(8,128)(2,1)S(1)} %get-tuple-element.21), channel_id=1, source_target_pairs={{0,4},{2,6},{4,8},{6,10},{8,12},{10,14},{12,0},{14,2},{1,5},{3,7},... | collective-permute-start | bytes 393224 | tf_op jit(solution)/shard_map/ppermute | solution.py:34
  36.1 2.7 %collective-permute-start.13 = (f16[32,2048]{1,0:T(8,128)(2,1)S(1)}, f16[32,2048]{1,0:T(8,128)(2,1)S(1)}, u32[]{:S(2)}, u32[]{:S(2)}) collective-permute-start(f16[32,2048]{1,0:T(8,128)(2,1)S(1)} %get-tuple-element.22), channel_id=1, source_target_pairs={{0,14},{2,12},{4,2},{6,0},{8,6},{10,4},{12,10},{14,8},{1,15},{3,13... | collective-permute-start | bytes 393224 | tf_op jit(solution)/shard_map/ppermute | solution.py:34
  38.8 0.0 collective-permute-start.12
  38.8 2.1 %collective-permute-start.11 = (f16[32,2048]{1,0:T(8,128)(2,1)S(1)}, f16[32,2048]{1,0:T(8,128)(2,1)S(1)}, u32[]{:S(2)}, u32[]{:S(2)}) collective-permute-start(f16[32,2048]{1,0:T(8,128)(2,1)S(1)} %get-tuple-element.24), channel_id=1, source_target_pairs={{0,8},{2,10},{4,12},{6,14},{8,0},{10,2},{12,4},{14,6},{1,9},{3,11}... | collective-permute-start | bytes 393224 | tf_op jit(solution)/shard_map/ppermute | solution.py:34
  40.9 1.7 %collective-permute-start.10 = (f16[32,2048]{1,0:T(8,128)(2,1)S(1)}, f16[32,2048]{1,0:T(8,128)(2,1)S(1)}, u32[]{:S(2)}, u32[]{:S(2)}) collective-permute-start(f16[32,2048]{1,0:T(8,128)(2,1)S(1)} %get-tuple-element.25), channel_id=1, source_target_pairs={{0,10},{2,8},{4,14},{6,12},{8,2},{10,0},{12,6},{14,4},{1,11},{3,9}... | collective-permute-start | bytes 393224 | tf_op jit(solution)/shard_map/ppermute | solution.py:34
  42.7 0.0 collective-permute-done.7
  42.7 0.3 collective-permute-start.9
  42.9 2.5 %collective-permute-start.8 = (f16[32,2048]{1,0:T(8,128)(2,1)S(1)}, f16[32,2048]{1,0:T(8,128)(2,1)S(1)}, u32[]{:S(2)}, u32[]{:S(2)}) collective-permute-start(f16[32,2048]{1,0:T(8,128)(2,1)S(1)} %get-tuple-element.27), channel_id=1, source_target_pairs={{0,12},{2,14},{4,0},{6,2},{8,4},{10,6},{12,8},{14,10},{1,13},{3,15... | collective-permute-start | bytes 393224 | tf_op jit(solution)/shard_map/ppermute | solution.py:34
  45.4 0.1 pad_add_fusion.place
  45.5 0.5 collective-permute-done.12
  46.0 4.7 %collective-permute-done.11 = f16[32,2048]{1,0:T(8,128)(2,1)S(1)} collective-permute-done((f16[32,2048]{1,0:T(8,128)(2,1)S(1)}, f16[32,2048]{1,0:T(8,128)(2,1)S(1)}, u32[]{:S(2)}, u32[]{:S(2)}) %collective-permute-start.11) | collective-permute-done | bytes 131104 | tf_op jit(solution)/shard_map/ppermute | solution.py:34
  50.7 0.0 collective-permute-done.10
  50.7 0.2 collective-permute-done.8
  50.9 0.1 convert_add_fusion.logits_ref
  51.1 0.8 shard_map.61.refs_0_
  51.9 4.4 %collective-permute-start.20 = (bf16[32,2176]{1,0:T(8,128)(2,1)S(1)}, bf16[32,2176]{1,0:T(8,128)(2,1)S(1)}, u32[]{:S(2)}, u32[]{:S(2)}) collective-permute-start(bf16[32,2176]{1,0:T(8,128)(2,1)S(1)} %shard_map.61.refs_0_), channel_id=1, source_target_pairs={{0,14},{2,12},{4,2},{6,0},{8,6},{10,4},{12,10},{14,8},{1,15},{3,13... | collective-permute-start | bytes 417800 | tf_op jit(solution)/shard_map/ppermute | solution.py:34
  56.2 1.3 %collective-permute-start.18 = (bf16[32,2176]{1,0:T(8,128)(2,1)S(1)}, bf16[32,2176]{1,0:T(8,128)(2,1)S(1)}, u32[]{:S(2)}, u32[]{:S(2)}) collective-permute-start(bf16[32,2176]{1,0:T(8,128)(2,1)S(1)} %shard_map.61.refs_0_), channel_id=1, source_target_pairs={{0,8},{2,10},{4,12},{6,14},{8,0},{10,2},{12,4},{14,6},{1,9},{3,11}... | collective-permute-start | bytes 417800 | tf_op jit(solution)/shard_map/ppermute | solution.py:34
  57.5 1.4 %collective-permute-start.17 = (bf16[32,2176]{1,0:T(8,128)(2,1)S(1)}, bf16[32,2176]{1,0:T(8,128)(2,1)S(1)}, u32[]{:S(2)}, u32[]{:S(2)}) collective-permute-start(bf16[32,2176]{1,0:T(8,128)(2,1)S(1)} %shard_map.61.refs_0_), channel_id=1, source_target_pairs={{0,10},{2,8},{4,14},{6,12},{8,2},{10,0},{12,6},{14,4},{1,11},{3,9}... | collective-permute-start | bytes 417800 | tf_op jit(solution)/shard_map/ppermute | solution.py:34
  58.8 1.5 %collective-permute-start.16 = (bf16[32,2176]{1,0:T(8,128)(2,1)S(1)}, bf16[32,2176]{1,0:T(8,128)(2,1)S(1)}, u32[]{:S(2)}, u32[]{:S(2)}) collective-permute-start(bf16[32,2176]{1,0:T(8,128)(2,1)S(1)} %shard_map.61.refs_0_), channel_id=1, source_target_pairs={{0,2},{2,0},{4,6},{6,4},{8,10},{10,8},{12,14},{14,12},{1,3},{3,1},... | collective-permute-start | bytes 417800 | tf_op jit(solution)/shard_map/ppermute | solution.py:34
  60.4 2.4 %collective-permute-start.15 = (bf16[32,2176]{1,0:T(8,128)(2,1)S(1)}, bf16[32,2176]{1,0:T(8,128)(2,1)S(1)}, u32[]{:S(2)}, u32[]{:S(2)}) collective-permute-start(bf16[32,2176]{1,0:T(8,128)(2,1)S(1)} %shard_map.61.refs_0_), channel_id=1, source_target_pairs={{0,12},{2,14},{4,0},{6,2},{8,4},{10,6},{12,8},{14,10},{1,13},{3,15... | collective-permute-start | bytes 417800 | tf_op jit(solution)/shard_map/ppermute | solution.py:34
  62.8 0.4 collective-permute-start.14
  63.2 0.1 stack.94.place
  63.3 5.8 %collective-permute-done.18.refs_5_ = bf16[32,2176]{1,0:T(8,128)(2,1)S(1)} collective-permute-done((bf16[32,2176]{1,0:T(8,128)(2,1)S(1)}, bf16[32,2176]{1,0:T(8,128)(2,1)S(1)}, u32[]{:S(2)}, u32[]{:S(2)}) %collective-permute-start.18) | collective-permute-done | bytes 139296 | tf_op jit(solution)/shard_map/ppermute | solution.py:34
  69.1 2.8 %collective-permute-done.14.refs_1_ = bf16[32,2176]{1,0:T(8,128)(2,1)S(1)} collective-permute-done((bf16[32,2176]{1,0:T(8,128)(2,1)S(1)}, bf16[32,2176]{1,0:T(8,128)(2,1)S(1)}, u32[]{:S(2)}, u32[]{:S(2)}) %collective-permute-start.14) | collective-permute-done | bytes 139296 | tf_op jit(solution)/shard_map/ppermute | solution.py:34
  71.9 0.7 shard_map.62
  72.6 1.2 %collective-permute-start.21 = (f32[8,256]{1,0:T(8,128)S(1)}, f32[8,256]{1,0:T(8,128)S(1)}, u32[]{:S(2)}, u32[]{:S(2)}) collective-permute-start(f32[8,256]{1,0:T(8,128)S(1)} %get-tuple-element.11.own_ref), channel_id=1, source_target_pairs={{0,1},{1,0},{2,3},{3,2},{4,5},{5,4},{6,7},{7,6},{8,9},{9,8},{10,11... | collective-permute-start | bytes 24584 | tf_op jit(solution)/shard_map/ppermute | solution.py:371
  73.8 0.8 collective-permute-done.21.oth_ref
  74.6 0.3 collective-permute-start.22
  75.0 0.1 pad_add_fusion.3.place
  75.1 0.7 shard_map.63
  75.7 5.4 %all-to-all-start = ((f32[16,8,256]{2,1,0:T(8,128)}), f32[16,8,256]{2,1,0:T(8,128)S(1)}, u32[]{:S(2)}, u32[]{:S(2)}) async-start(f32[16,8,256]{2,1,0:T(8,128)} %shard_map.63), calls=%async_computation | async-start | bytes 262144 | tf_op jit(solution)/shard_map/all_to_all | solution.py:374
  81.1 7.1 %shard_map.64 = (f32[2,256,768]{2,1,0:T(8,128)S(1)}, bf16[256,768]{1,0:T(8,128)(2,1)S(1)}) custom-call(s32[3]{0:T(128)S(1)} %pad_add_fusion.3.place, bf16[256,2176]{1,0:T(8,128)(2,1)S(1)} %get-tuple-element.14.own_ref, bf16[256,128]{1,0:T(8,128)(2,1)S(1)} %slice.25.ids_ref, bf16[256,2176]{1,0:T(8,128)(2,1)} %collective-permute-done.22.oth_ref, ...), custom_call_target="tpu_custom_call" | custom-call | flops 3221225472 | bytes 6291456 | tf_op jit(solution)/shard_map/pallas_call | solution.py:251
  88.3 3.2 %all-to-all-done.every_ref = f32[16,8,256]{2,1,0:T(8,128)S(1)} async-done(((f32[16,8,256]{2,1,0:T(8,128)}), f32[16,8,256]{2,1,0:T(8,128)S(1)}, u32[]{:S(2)}, u32[]{:S(2)}) %all-to-all-start) | async-done | bytes 131104 | tf_op jit(solution)/shard_map/all_to_all | solution.py:374
  91.5 0.2 shard_map.65
  91.7 0.2 slice_reduce_fusion.1
  91.9 1.1 fusion.10
  93.0 5.8 %all-to-all-start.1 = ((f16[16,16,768]{2,1,0:T(8,128)(2,1)}), f16[16,16,768]{2,1,0:T(8,128)(2,1)S(1)}, u32[]{:S(2)}, u32[]{:S(2)}) async-start(f16[16,16,768]{2,1,0:T(8,128)(2,1)} %bitcast.39), calls=%async_computation.1 | async-start | bytes 786432 | tf_op jit(solution)/shard_map/all_to_all | solution.py:382
  98.8 0.1 pad_add_fusion.4.place
  98.9 0.6 fusion.15
  99.5 9.1 %shard_map.66 = bf16[4096,768]{1,0:T(8,128)(2,1)} custom-call(s32[3]{0:T(128)S(1)} %pad_add_fusion.4.place, bf16[256,2176]{1,0:T(8,128)(2,1)S(1)} %get-tuple-element.14.own_ref, bf16[256,2176]{1,0:T(8,128)(2,1)} %collective-permute-done.22.oth_ref, bf16[256,896]{1,0:T(8,128)(2,1)} %copy-done, bf16[256,128]{1,0:T(8,128)(2,1)S(1)} %slice.25.ids_ref, ...), custom_call_target="tpu_custom_call" | custom-call | flops 1610612736 | bytes 8388608 | tf_op jit(solution)/shard_map/pallas_call | solution.py:309
  108.6 4.9 %all-to-all-done.1 = f16[16,16,768]{2,1,0:T(8,128)(2,1)S(1)} async-done(((f16[16,16,768]{2,1,0:T(8,128)(2,1)}), f16[16,16,768]{2,1,0:T(8,128)(2,1)S(1)}, u32[]{:S(2)}, u32[]{:S(2)}) %all-to-all-start.1) | async-done | bytes 393248 | tf_op jit(solution)/shard_map/all_to_all | solution.py:382
  113.5 0.7 multiply_reduce_fusion
  (12 shorter events, 0.0 us)
Async XLA Ops:
  2.1 10.3 %collective-permute-start.2 = (bf16[16,896]{1,0:T(8,128)(2,1)S(1)}, bf16[16,896]{1,0:T(8,128)(2,1)S(1)}, u32[]{:S(2)}, u32[]{:S(2)}) collective-permute-start(bf16[16,896]{1,0:T(8,128)(2,1)S(1)} %shard_map.58.refs_0_), channel_id=1, source_target_pairs={{0,32},{16,48},{32,0},{48,16},{1,33},{17,49},{33,1},{49,17},{2,34}... | collective-permute-start | bytes 86024 | tf_op jit(solution)/shard_map/ppermute | solution.py:86
  9.9 3.6 %collective-permute-start.1 = (bf16[16,896]{1,0:T(8,128)(2,1)S(1)}, bf16[16,896]{1,0:T(8,128)(2,1)S(1)}, u32[]{:S(2)}, u32[]{:S(2)}) collective-permute-start(bf16[16,896]{1,0:T(8,128)(2,1)S(1)} %shard_map.58.refs_0_), channel_id=1, source_target_pairs={{0,48},{16,0},{32,16},{48,32},{1,49},{17,1},{33,17},{49,33},{2,50}... | collective-permute-start | bytes 86024 | tf_op jit(solution)/shard_map/ppermute | solution.py:86
  9.9 4.9 %collective-permute-start = (bf16[16,896]{1,0:T(8,128)(2,1)S(1)}, bf16[16,896]{1,0:T(8,128)(2,1)S(1)}, u32[]{:S(2)}, u32[]{:S(2)}) collective-permute-start(bf16[16,896]{1,0:T(8,128)(2,1)S(1)} %shard_map.58.refs_0_), channel_id=1, source_target_pairs={{0,16},{16,32},{32,48},{48,0},{1,17},{17,33},{33,49},{49,1},{2,18}... | collective-permute-start | bytes 86024 | tf_op jit(solution)/shard_map/ppermute | solution.py:86
  15.4 5.2 %collective-permute-start.5 = (bf16[64,896]{1,0:T(8,128)(2,1)S(1)}, bf16[64,896]{1,0:T(8,128)(2,1)S(1)}, u32[]{:S(2)}, u32[]{:S(2)}) collective-permute-start(bf16[64,896]{1,0:T(8,128)(2,1)S(1)} %shard_map.59.refs_0_), channel_id=1, source_target_pairs={{0,128},{64,192},{128,0},{192,64},{1,129},{65,193},{129,1},{193,65... | collective-permute-start | bytes 344072 | tf_op jit(solution)/shard_map/ppermute | solution.py:86
  18.4 4.1 %collective-permute-start.4 = (bf16[64,896]{1,0:T(8,128)(2,1)S(1)}, bf16[64,896]{1,0:T(8,128)(2,1)S(1)}, u32[]{:S(2)}, u32[]{:S(2)}) collective-permute-start(bf16[64,896]{1,0:T(8,128)(2,1)S(1)} %shard_map.59.refs_0_), channel_id=1, source_target_pairs={{0,192},{64,0},{128,64},{192,128},{1,193},{65,1},{129,65},{193,129... | collective-permute-start | bytes 344072 | tf_op jit(solution)/shard_map/ppermute | solution.py:86
  19.2 5.6 %collective-permute-start.3 = (bf16[64,896]{1,0:T(8,128)(2,1)S(1)}, bf16[64,896]{1,0:T(8,128)(2,1)S(1)}, u32[]{:S(2)}, u32[]{:S(2)}) collective-permute-start(bf16[64,896]{1,0:T(8,128)(2,1)S(1)} %shard_map.59.refs_0_), channel_id=1, source_target_pairs={{0,64},{64,128},{128,192},{192,0},{1,65},{65,129},{129,193},{193,1... | collective-permute-start | bytes 344072 | tf_op jit(solution)/shard_map/ppermute | solution.py:86
  25.4 20.1 %copy-start = (bf16[256,896]{1,0:T(8,128)(2,1)}, bf16[256,896]{1,0:T(8,128)(2,1)S(1)}, u32[]{:S(2)}) copy-start(bf16[256,896]{1,0:T(8,128)(2,1)S(1)} %shard_map.60.hidden_ref) | copy-start | bytes 1376260
  28.5 5.9 %collective-permute-start.6 = (f16[256,2048]{1,0:T(8,128)(2,1)S(1)}, f16[256,2048]{1,0:T(8,128)(2,1)S(1)}, u32[]{:S(2)}, u32[]{:S(2)}) collective-permute-start(f16[256,2048]{1,0:T(8,128)(2,1)S(1)} %fusion.4), channel_id=1, source_target_pairs={{0,1},{1,0},{2,3},{3,2},{4,5},{5,4},{6,7},{7,6},{8,9},{9,8},{10,11... | collective-permute-start | bytes 3145736 | tf_op jit(solution)/shard_map/ppermute | solution.py:352
  34.8 7.9 %collective-permute-start.7 = (f16[32,2048]{1,0:T(8,128)(2,1)S(1)}, f16[32,2048]{1,0:T(8,128)(2,1)S(1)}, u32[]{:S(2)}, u32[]{:S(2)}) collective-permute-start(f16[32,2048]{1,0:T(8,128)(2,1)S(1)} %get-tuple-element.21), channel_id=1, source_target_pairs={{0,4},{2,6},{4,8},{6,10},{8,12},{10,14},{12,0},{14,2},{1,5},{3,7},... | collective-permute-start | bytes 393224 | tf_op jit(solution)/shard_map/ppermute | solution.py:34
  36.1 6.8 %collective-permute-start.13 = (f16[32,2048]{1,0:T(8,128)(2,1)S(1)}, f16[32,2048]{1,0:T(8,128)(2,1)S(1)}, u32[]{:S(2)}, u32[]{:S(2)}) collective-permute-start(f16[32,2048]{1,0:T(8,128)(2,1)S(1)} %get-tuple-element.22), channel_id=1, source_target_pairs={{0,14},{2,12},{4,2},{6,0},{8,6},{10,4},{12,10},{14,8},{1,15},{3,13... | collective-permute-start | bytes 393224 | tf_op jit(solution)/shard_map/ppermute | solution.py:34
  38.8 7.2 %collective-permute-start.12 = (f16[32,2048]{1,0:T(8,128)(2,1)S(1)}, f16[32,2048]{1,0:T(8,128)(2,1)S(1)}, u32[]{:S(2)}, u32[]{:S(2)}) collective-permute-start(f16[32,2048]{1,0:T(8,128)(2,1)S(1)} %get-tuple-element.23), channel_id=1, source_target_pairs={{0,6},{2,4},{4,10},{6,8},{8,14},{10,12},{12,2},{14,0},{1,7},{3,5},... | collective-permute-start | bytes 393224 | tf_op jit(solution)/shard_map/ppermute | solution.py:34
  38.8 11.9 %collective-permute-start.11 = (f16[32,2048]{1,0:T(8,128)(2,1)S(1)}, f16[32,2048]{1,0:T(8,128)(2,1)S(1)}, u32[]{:S(2)}, u32[]{:S(2)}) collective-permute-start(f16[32,2048]{1,0:T(8,128)(2,1)S(1)} %get-tuple-element.24), channel_id=1, source_target_pairs={{0,8},{2,10},{4,12},{6,14},{8,0},{10,2},{12,4},{14,6},{1,9},{3,11}... | collective-permute-start | bytes 393224 | tf_op jit(solution)/shard_map/ppermute | solution.py:34
  40.9 9.8 %collective-permute-start.10 = (f16[32,2048]{1,0:T(8,128)(2,1)S(1)}, f16[32,2048]{1,0:T(8,128)(2,1)S(1)}, u32[]{:S(2)}, u32[]{:S(2)}) collective-permute-start(f16[32,2048]{1,0:T(8,128)(2,1)S(1)} %get-tuple-element.25), channel_id=1, source_target_pairs={{0,10},{2,8},{4,14},{6,12},{8,2},{10,0},{12,6},{14,4},{1,11},{3,9}... | collective-permute-start | bytes 393224 | tf_op jit(solution)/shard_map/ppermute | solution.py:34
  42.7 8.1 %collective-permute-start.9 = (f16[32,2048]{1,0:T(8,128)(2,1)S(1)}, f16[32,2048]{1,0:T(8,128)(2,1)S(1)}, u32[]{:S(2)}, u32[]{:S(2)}) collective-permute-start(f16[32,2048]{1,0:T(8,128)(2,1)S(1)} %get-tuple-element.26), channel_id=1, source_target_pairs={{0,2},{2,0},{4,6},{6,4},{8,10},{10,8},{12,14},{14,12},{1,3},{3,1},... | collective-permute-start | bytes 393224 | tf_op jit(solution)/shard_map/ppermute | solution.py:34
  42.9 8.0 %collective-permute-start.8 = (f16[32,2048]{1,0:T(8,128)(2,1)S(1)}, f16[32,2048]{1,0:T(8,128)(2,1)S(1)}, u32[]{:S(2)}, u32[]{:S(2)}) collective-permute-start(f16[32,2048]{1,0:T(8,128)(2,1)S(1)} %get-tuple-element.27), channel_id=1, source_target_pairs={{0,12},{2,14},{4,0},{6,2},{8,4},{10,6},{12,8},{14,10},{1,13},{3,15... | collective-permute-start | bytes 393224 | tf_op jit(solution)/shard_map/ppermute | solution.py:34
  51.9 8.5 %collective-permute-start.20 = (bf16[32,2176]{1,0:T(8,128)(2,1)S(1)}, bf16[32,2176]{1,0:T(8,128)(2,1)S(1)}, u32[]{:S(2)}, u32[]{:S(2)}) collective-permute-start(bf16[32,2176]{1,0:T(8,128)(2,1)S(1)} %shard_map.61.refs_0_), channel_id=1, source_target_pairs={{0,14},{2,12},{4,2},{6,0},{8,6},{10,4},{12,10},{14,8},{1,15},{3,13... | collective-permute-start | bytes 417800 | tf_op jit(solution)/shard_map/ppermute | solution.py:34
  56.2 6.6 %collective-permute-start.19 = (bf16[32,2176]{1,0:T(8,128)(2,1)S(1)}, bf16[32,2176]{1,0:T(8,128)(2,1)S(1)}, u32[]{:S(2)}, u32[]{:S(2)}) collective-permute-start(bf16[32,2176]{1,0:T(8,128)(2,1)S(1)} %shard_map.61.refs_0_), channel_id=1, source_target_pairs={{0,6},{2,4},{4,10},{6,8},{8,14},{10,12},{12,2},{14,0},{1,7},{3,5},... | collective-permute-start | bytes 417800 | tf_op jit(solution)/shard_map/ppermute | solution.py:34
  56.2 12.9 %collective-permute-start.18 = (bf16[32,2176]{1,0:T(8,128)(2,1)S(1)}, bf16[32,2176]{1,0:T(8,128)(2,1)S(1)}, u32[]{:S(2)}, u32[]{:S(2)}) collective-permute-start(bf16[32,2176]{1,0:T(8,128)(2,1)S(1)} %shard_map.61.refs_0_), channel_id=1, source_target_pairs={{0,8},{2,10},{4,12},{6,14},{8,0},{10,2},{12,4},{14,6},{1,9},{3,11}... | collective-permute-start | bytes 417800 | tf_op jit(solution)/shard_map/ppermute | solution.py:34
  57.5 11.6 %collective-permute-start.17 = (bf16[32,2176]{1,0:T(8,128)(2,1)S(1)}, bf16[32,2176]{1,0:T(8,128)(2,1)S(1)}, u32[]{:S(2)}, u32[]{:S(2)}) collective-permute-start(bf16[32,2176]{1,0:T(8,128)(2,1)S(1)} %shard_map.61.refs_0_), channel_id=1, source_target_pairs={{0,10},{2,8},{4,14},{6,12},{8,2},{10,0},{12,6},{14,4},{1,11},{3,9}... | collective-permute-start | bytes 417800 | tf_op jit(solution)/shard_map/ppermute | solution.py:34
  58.8 10.3 %collective-permute-start.16 = (bf16[32,2176]{1,0:T(8,128)(2,1)S(1)}, bf16[32,2176]{1,0:T(8,128)(2,1)S(1)}, u32[]{:S(2)}, u32[]{:S(2)}) collective-permute-start(bf16[32,2176]{1,0:T(8,128)(2,1)S(1)} %shard_map.61.refs_0_), channel_id=1, source_target_pairs={{0,2},{2,0},{4,6},{6,4},{8,10},{10,8},{12,14},{14,12},{1,3},{3,1},... | collective-permute-start | bytes 417800 | tf_op jit(solution)/shard_map/ppermute | solution.py:34
  60.4 8.8 %collective-permute-start.15 = (bf16[32,2176]{1,0:T(8,128)(2,1)S(1)}, bf16[32,2176]{1,0:T(8,128)(2,1)S(1)}, u32[]{:S(2)}, u32[]{:S(2)}) collective-permute-start(bf16[32,2176]{1,0:T(8,128)(2,1)S(1)} %shard_map.61.refs_0_), channel_id=1, source_target_pairs={{0,12},{2,14},{4,0},{6,2},{8,4},{10,6},{12,8},{14,10},{1,13},{3,15... | collective-permute-start | bytes 417800 | tf_op jit(solution)/shard_map/ppermute | solution.py:34
  62.8 9.1 %collective-permute-start.14 = (bf16[32,2176]{1,0:T(8,128)(2,1)S(1)}, bf16[32,2176]{1,0:T(8,128)(2,1)S(1)}, u32[]{:S(2)}, u32[]{:S(2)}) collective-permute-start(bf16[32,2176]{1,0:T(8,128)(2,1)S(1)} %shard_map.61.refs_0_), channel_id=1, source_target_pairs={{0,4},{2,6},{4,8},{6,10},{8,12},{10,14},{12,0},{14,2},{1,5},{3,7},... | collective-permute-start | bytes 417800 | tf_op jit(solution)/shard_map/ppermute | solution.py:34
  72.6 2.0 %collective-permute-start.21 = (f32[8,256]{1,0:T(8,128)S(1)}, f32[8,256]{1,0:T(8,128)S(1)}, u32[]{:S(2)}, u32[]{:S(2)}) collective-permute-start(f32[8,256]{1,0:T(8,128)S(1)} %get-tuple-element.11.own_ref), channel_id=1, source_target_pairs={{0,1},{1,0},{2,3},{3,2},{4,5},{5,4},{6,7},{7,6},{8,9},{9,8},{10,11... | collective-permute-start | bytes 24584 | tf_op jit(solution)/shard_map/ppermute | solution.py:371
  74.6 6.5 %collective-permute-start.22 = (bf16[256,2176]{1,0:T(8,128)(2,1)S(1)}, bf16[256,2176]{1,0:T(8,128)(2,1)}, u32[]{:S(2)}, u32[]{:S(2)}) collective-permute-start(bf16[256,2176]{1,0:T(8,128)(2,1)S(1)} %get-tuple-element.14.own_ref), channel_id=1, source_target_pairs={{0,1},{1,0},{2,3},{3,2},{4,5},{5,4},{6,7},{7,6},{8,9},{9,8},{10,11... | collective-permute-start | bytes 3342344 | tf_op jit(solution)/shard_map/ppermute | solution.py:373
  75.7 15.7 %all-to-all-start = ((f32[16,8,256]{2,1,0:T(8,128)}), f32[16,8,256]{2,1,0:T(8,128)S(1)}, u32[]{:S(2)}, u32[]{:S(2)}) async-start(f32[16,8,256]{2,1,0:T(8,128)} %shard_map.63), calls=%async_computation | async-start | bytes 262144 | tf_op jit(solution)/shard_map/all_to_all | solution.py:374
  93.0 20.5 %all-to-all-start.1 = ((f16[16,16,768]{2,1,0:T(8,128)(2,1)}), f16[16,16,768]{2,1,0:T(8,128)(2,1)S(1)}, u32[]{:S(2)}, u32[]{:S(2)}) async-start(f16[16,16,768]{2,1,0:T(8,128)(2,1)} %bitcast.39), calls=%async_computation.1 | async-start | bytes 786432 | tf_op jit(solution)/shard_map/all_to_all | solution.py:382

commit v5 on v4

--- a/solution.py
+++ b/solution.py
@@ -234,13 +234,23 @@
         if which == 1:
             fetch.wait()
         both[:tokens] = p_ref[:, :half]
-        for copy in copies[which * per_half : (which + 1) * per_half]:
-            copy.wait()
         if which == 0:
-            fetch.start()
+            d = None
+            for k in range(per_half):
+                copies[k].wait()
+                if k == 0:
+                    fetch.start()
+                copies[per_half + k].start()
+                part = jnp.dot(
+                    both[:, k * step : (k + 1) * step],
+                    held[k * step : (k + 1) * step],
+                    preferred_element_type=jnp.float32,
+                )
+                d = part if d is None else d + part
+        else:
             for copy in copies[per_half:]:
-                copy.start()
-        d = jnp.dot(both[...], held[which * half : (which + 1) * half], preferred_element_type=jnp.float32)
+                copy.wait()
+            d = jnp.dot(both[...], held[half:], preferred_element_type=jnp.float32)
         u_ref[which] = d[:tokens]
         t = d[tokens:] if t is None else t + d[tokens:]
     t_ref[...] = t.astype(jnp.bfloat16)

time: 115 us -> 115 us (level)
  no operation moved by 1% of the time
where the time goes in v5:
time: 115 us; the launch traced here: 114 us
  starting transfers between devices  52.5 us (46%)
  waiting for transfers between devices  30.3 us (26%)
  Pallas kernels  21.2 us (18%)
  matrix products  5.97 us (5%)
  other arithmetic  2.64 us (2%)
    ppermute x14, starting transfers between devices, to_chip(): return lax.ppermute(v, CHIPS, pairs)  21.9 us
    ppermute x6, starting transfers between devices, around(): lax.ppermute(v, axis, [(i, (i + k) % 4) for i in range(4)])  14.7 us
    ppermute x14, waiting for transfers between devices, to_chip(): return lax.ppermute(v, CHIPS, pairs)  14 us
    pallas_call x1, Pallas kernels, weight_gradient(): pl.pallas_call(functools.partial(weight_grad_kernel, steps), grid_spec=pl...  9.12 us
    ppermute x6, waiting for transfers between devices, around(): lax.ppermute(v, axis, [(i, (i + k) % 4) for i in range(4)])  7.34 us
    pallas_call x1, Pallas kernels, products(): pl.pallas_call(product_kernel, grid_spec=pltpu.PrefetchScalarGridSpec(num...  7.13 us
    all_to_all x1, starting transfers between devices, shards(): parts = lax.all_to_all(sent, PIPE, 0, 0)  5.87 us
    all_to_all x1, starting transfers between devices, shards(): everyone = lax.all_to_all(join_stats(st_own, st_oth, 16), PIPE, 0, 0)  5.39 us
  transfers between devices with their start and end apart: 25, of which 13 were waited for; matrix products, arithmetic and copies ran while one was open for 3% of the time, Pallas kernels for 15%

profile of v5, /device:TPU:1, one launch (start us, length us, event | category | flops | bytes accessed | tf_op | source)
XLA Modules:
  0.0 114.2 jit_solution(11145176374303940777)
XLA Ops:
  0.6 1.4 %shard_map.58.refs_0_ = bf16[16,896]{1,0:T(8,128)(2,1)S(1)} custom-call(s32[16]{0:T(128)} %targets_ref.1, bf16[16,768]{1,0:T(8,128)(2,1)} %hidden_ref.1), custom_call_target="tpu_custom_call" | custom-call | tf_op jit(solution)/shard_map/pallas_call | solution.py:66
  2.1 7.8 %collective-permute-start.2 = (bf16[16,896]{1,0:T(8,128)(2,1)S(1)}, bf16[16,896]{1,0:T(8,128)(2,1)S(1)}, u32[]{:S(2)}, u32[]{:S(2)}) collective-permute-start(bf16[16,896]{1,0:T(8,128)(2,1)S(1)} %shard_map.58.refs_0_), channel_id=1, source_target_pairs={{0,32},{16,48},{32,0},{48,16},{1,33},{17,49},{33,1},{49,17},{2,34}... | collective-permute-start | bytes 86024 | tf_op jit(solution)/shard_map/ppermute | solution.py:86
  9.9 0.0 collective-permute-start.1
  9.9 2.4 %collective-permute-start = (bf16[16,896]{1,0:T(8,128)(2,1)S(1)}, bf16[16,896]{1,0:T(8,128)(2,1)S(1)}, u32[]{:S(2)}, u32[]{:S(2)}) collective-permute-start(bf16[16,896]{1,0:T(8,128)(2,1)S(1)} %shard_map.58.refs_0_), channel_id=1, source_target_pairs={{0,16},{16,32},{32,48},{48,0},{1,17},{17,33},{33,49},{49,1},{2,18}... | collective-permute-start | bytes 86024 | tf_op jit(solution)/shard_map/ppermute | solution.py:86
  12.3 0.1 pad_add_fusion.2.place
  12.3 1.2 %collective-permute-done.1.refs_2_ = bf16[16,896]{1,0:T(8,128)(2,1)S(1)} collective-permute-done((bf16[16,896]{1,0:T(8,128)(2,1)S(1)}, bf16[16,896]{1,0:T(8,128)(2,1)S(1)}, u32[]{:S(2)}, u32[]{:S(2)}) %collective-permute-start.1) | collective-permute-done | bytes 28704 | tf_op jit(solution)/shard_map/ppermute | solution.py:86
  13.5 1.3 %collective-permute-done.refs_1_ = bf16[16,896]{1,0:T(8,128)(2,1)S(1)} collective-permute-done((bf16[16,896]{1,0:T(8,128)(2,1)S(1)}, bf16[16,896]{1,0:T(8,128)(2,1)S(1)}, u32[]{:S(2)}, u32[]{:S(2)}) %collective-permute-start) | collective-permute-done | bytes 28704 | tf_op jit(solution)/shard_map/ppermute | solution.py:86
  14.8 0.6 shard_map.59.refs_0_
  15.4 3.0 %collective-permute-start.5 = (bf16[64,896]{1,0:T(8,128)(2,1)S(1)}, bf16[64,896]{1,0:T(8,128)(2,1)S(1)}, u32[]{:S(2)}, u32[]{:S(2)}) collective-permute-start(bf16[64,896]{1,0:T(8,128)(2,1)S(1)} %shard_map.59.refs_0_), channel_id=1, source_target_pairs={{0,128},{64,192},{128,0},{192,64},{1,129},{65,193},{129,1},{193,65... | collective-permute-start | bytes 344072 | tf_op jit(solution)/shard_map/ppermute | solution.py:86
  18.4 0.8 collective-permute-start.4
  19.2 0.7 collective-permute-start.3
  19.9 0.1 pad_add_fusion.1.place
  19.9 0.7 collective-permute-done.5.refs_3_
  20.6 1.9 %collective-permute-done.4.refs_2_ = bf16[64,896]{1,0:T(8,128)(2,1)S(1)} collective-permute-done((bf16[64,896]{1,0:T(8,128)(2,1)S(1)}, bf16[64,896]{1,0:T(8,128)(2,1)S(1)}, u32[]{:S(2)}, u32[]{:S(2)}) %collective-permute-start.4) | collective-permute-done | bytes 114720 | tf_op jit(solution)/shard_map/ppermute | solution.py:86
  22.5 2.3 %collective-permute-done.3.refs_1_ = bf16[64,896]{1,0:T(8,128)(2,1)S(1)} collective-permute-done((bf16[64,896]{1,0:T(8,128)(2,1)S(1)}, bf16[64,896]{1,0:T(8,128)(2,1)S(1)}, u32[]{:S(2)}, u32[]{:S(2)}) %collective-permute-start.3) | collective-permute-done | bytes 114720 | tf_op jit(solution)/shard_map/ppermute | solution.py:86
  24.8 0.6 shard_map.60.hidden_ref
  25.4 3.1 %fusion.4 = f16[256,2048]{1,0:T(8,128)(2,1)S(1)} fusion(bf16[4096,768]{1,0:T(8,128)(2,1)} %w_ref.1, s32[]{:T(128)S(6)} %select_n.80, bf16[256,896]{1,0:T(8,128)(2,1)S(1)} %shard_map.60.hidden_ref), kind=kOutput, calls=%fused_computation.4 | convolution fusion | flops 805830656 | bytes 4587524 | tf_op jit(solution)/shard_map/dot_general | solution.py:361
  28.5 3.0 %collective-permute-start.6 = (f16[256,2048]{1,0:T(8,128)(2,1)S(1)}, f16[256,2048]{1,0:T(8,128)(2,1)S(1)}, u32[]{:S(2)}, u32[]{:S(2)}) collective-permute-start(f16[256,2048]{1,0:T(8,128)(2,1)S(1)} %fusion.4), channel_id=1, source_target_pairs={{0,1},{1,0},{2,3},{3,2},{4,5},{5,4},{6,7},{7,6},{8,9},{9,8},{10,11... | collective-permute-start | bytes 3145736 | tf_op jit(solution)/shard_map/ppermute | solution.py:362
  31.5 2.9 %fusion.2 = f32[256,2048]{1,0:T(8,128)S(1)} fusion(bf16[4096,768]{1,0:T(8,128)(2,1)} %w_ref.1, s32[]{:T(128)S(6)} %select_n.78, bf16[256,896]{1,0:T(8,128)(2,1)S(1)} %shard_map.60.hidden_ref), kind=kOutput, calls=%fused_computation.2 | convolution fusion | flops 805306368 | bytes 5636100 | tf_op jit(solution)/shard_map/dot_general | solution.py:363
  34.4 0.4 add_convert_fusion.6
  34.8 1.3 %collective-permute-start.7 = (f16[32,2048]{1,0:T(8,128)(2,1)S(1)}, f16[32,2048]{1,0:T(8,128)(2,1)S(1)}, u32[]{:S(2)}, u32[]{:S(2)}) collective-permute-start(f16[32,2048]{1,0:T(8,128)(2,1)S(1)} %get-tuple-element.21), channel_id=1, source_target_pairs={{0,4},{2,6},{4,8},{6,10},{8,12},{10,14},{12,0},{14,2},{1,5},{3,7},... | collective-permute-start | bytes 393224 | tf_op jit(solution)/shard_map/ppermute | solution.py:34
  36.1 2.7 %collective-permute-start.13 = (f16[32,2048]{1,0:T(8,128)(2,1)S(1)}, f16[32,2048]{1,0:T(8,128)(2,1)S(1)}, u32[]{:S(2)}, u32[]{:S(2)}) collective-permute-start(f16[32,2048]{1,0:T(8,128)(2,1)S(1)} %get-tuple-element.22), channel_id=1, source_target_pairs={{0,14},{2,12},{4,2},{6,0},{8,6},{10,4},{12,10},{14,8},{1,15},{3,13... | collective-permute-start | bytes 393224 | tf_op jit(solution)/shard_map/ppermute | solution.py:34
  38.8 0.0 collective-permute-start.12
  38.8 2.1 %collective-permute-start.11 = (f16[32,2048]{1,0:T(8,128)(2,1)S(1)}, f16[32,2048]{1,0:T(8,128)(2,1)S(1)}, u32[]{:S(2)}, u32[]{:S(2)}) collective-permute-start(f16[32,2048]{1,0:T(8,128)(2,1)S(1)} %get-tuple-element.24), channel_id=1, source_target_pairs={{0,8},{2,10},{4,12},{6,14},{8,0},{10,2},{12,4},{14,6},{1,9},{3,11}... | collective-permute-start | bytes 393224 | tf_op jit(solution)/shard_map/ppermute | solution.py:34
  40.9 1.7 %collective-permute-start.10 = (f16[32,2048]{1,0:T(8,128)(2,1)S(1)}, f16[32,2048]{1,0:T(8,128)(2,1)S(1)}, u32[]{:S(2)}, u32[]{:S(2)}) collective-permute-start(f16[32,2048]{1,0:T(8,128)(2,1)S(1)} %get-tuple-element.25), channel_id=1, source_target_pairs={{0,10},{2,8},{4,14},{6,12},{8,2},{10,0},{12,6},{14,4},{1,11},{3,9}... | collective-permute-start | bytes 393224 | tf_op jit(solution)/shard_map/ppermute | solution.py:34
  42.7 0.3 collective-permute-start.9
  42.9 0.0 collective-permute-done.13
  42.9 2.5 %collective-permute-start.8 = (f16[32,2048]{1,0:T(8,128)(2,1)S(1)}, f16[32,2048]{1,0:T(8,128)(2,1)S(1)}, u32[]{:S(2)}, u32[]{:S(2)}) collective-permute-start(f16[32,2048]{1,0:T(8,128)(2,1)S(1)} %get-tuple-element.27), channel_id=1, source_target_pairs={{0,12},{2,14},{4,0},{6,2},{8,4},{10,6},{12,8},{14,10},{1,13},{3,15... | collective-permute-start | bytes 393224 | tf_op jit(solution)/shard_map/ppermute | solution.py:34
  45.4 0.1 pad_add_fusion.place
  45.5 0.5 collective-permute-done.12
  46.0 4.7 %collective-permute-done.11 = f16[32,2048]{1,0:T(8,128)(2,1)S(1)} collective-permute-done((f16[32,2048]{1,0:T(8,128)(2,1)S(1)}, f16[32,2048]{1,0:T(8,128)(2,1)S(1)}, u32[]{:S(2)}, u32[]{:S(2)}) %collective-permute-start.11) | collective-permute-done | bytes 131104 | tf_op jit(solution)/shard_map/ppermute | solution.py:34
  50.7 0.0 collective-permute-done.10
  50.7 0.2 collective-permute-done.8
  50.9 0.1 convert_add_fusion.logits_ref
  51.1 0.8 shard_map.61.refs_0_
  51.9 4.4 %collective-permute-start.20 = (bf16[32,2176]{1,0:T(8,128)(2,1)S(1)}, bf16[32,2176]{1,0:T(8,128)(2,1)S(1)}, u32[]{:S(2)}, u32[]{:S(2)}) collective-permute-start(bf16[32,2176]{1,0:T(8,128)(2,1)S(1)} %shard_map.61.refs_0_), channel_id=1, source_target_pairs={{0,14},{2,12},{4,2},{6,0},{8,6},{10,4},{12,10},{14,8},{1,15},{3,13... | collective-permute-start | bytes 417800 | tf_op jit(solution)/shard_map/ppermute | solution.py:34
  56.2 0.0 collective-permute-start.19
  56.2 1.3 %collective-permute-start.18 = (bf16[32,2176]{1,0:T(8,128)(2,1)S(1)}, bf16[32,2176]{1,0:T(8,128)(2,1)S(1)}, u32[]{:S(2)}, u32[]{:S(2)}) collective-permute-start(bf16[32,2176]{1,0:T(8,128)(2,1)S(1)} %shard_map.61.refs_0_), channel_id=1, source_target_pairs={{0,8},{2,10},{4,12},{6,14},{8,0},{10,2},{12,4},{14,6},{1,9},{3,11}... | collective-permute-start | bytes 417800 | tf_op jit(solution)/shard_map/ppermute | solution.py:34
  57.5 1.4 %collective-permute-start.17 = (bf16[32,2176]{1,0:T(8,128)(2,1)S(1)}, bf16[32,2176]{1,0:T(8,128)(2,1)S(1)}, u32[]{:S(2)}, u32[]{:S(2)}) collective-permute-start(bf16[32,2176]{1,0:T(8,128)(2,1)S(1)} %shard_map.61.refs_0_), channel_id=1, source_target_pairs={{0,10},{2,8},{4,14},{6,12},{8,2},{10,0},{12,6},{14,4},{1,11},{3,9}... | collective-permute-start | bytes 417800 | tf_op jit(solution)/shard_map/ppermute | solution.py:34
  58.8 1.5 %collective-permute-start.16 = (bf16[32,2176]{1,0:T(8,128)(2,1)S(1)}, bf16[32,2176]{1,0:T(8,128)(2,1)S(1)}, u32[]{:S(2)}, u32[]{:S(2)}) collective-permute-start(bf16[32,2176]{1,0:T(8,128)(2,1)S(1)} %shard_map.61.refs_0_), channel_id=1, source_target_pairs={{0,2},{2,0},{4,6},{6,4},{8,10},{10,8},{12,14},{14,12},{1,3},{3,1},... | collective-permute-start | bytes 417800 | tf_op jit(solution)/shard_map/ppermute | solution.py:34
  60.4 0.0 collective-permute-done.20.refs_7_
  60.4 2.4 %collective-permute-start.15 = (bf16[32,2176]{1,0:T(8,128)(2,1)S(1)}, bf16[32,2176]{1,0:T(8,128)(2,1)S(1)}, u32[]{:S(2)}, u32[]{:S(2)}) collective-permute-start(bf16[32,2176]{1,0:T(8,128)(2,1)S(1)} %shard_map.61.refs_0_), channel_id=1, source_target_pairs={{0,12},{2,14},{4,0},{6,2},{8,4},{10,6},{12,8},{14,10},{1,13},{3,15... | collective-permute-start | bytes 417800 | tf_op jit(solution)/shard_map/ppermute | solution.py:34
  62.8 0.4 collective-permute-start.14
  63.2 0.1 stack.94.place
  63.3 5.8 %collective-permute-done.18.refs_5_ = bf16[32,2176]{1,0:T(8,128)(2,1)S(1)} collective-permute-done((bf16[32,2176]{1,0:T(8,128)(2,1)S(1)}, bf16[32,2176]{1,0:T(8,128)(2,1)S(1)}, u32[]{:S(2)}, u32[]{:S(2)}) %collective-permute-start.18) | collective-permute-done | bytes 139296 | tf_op jit(solution)/shard_map/ppermute | solution.py:34
  69.1 2.8 %collective-permute-done.14.refs_1_ = bf16[32,2176]{1,0:T(8,128)(2,1)S(1)} collective-permute-done((bf16[32,2176]{1,0:T(8,128)(2,1)S(1)}, bf16[32,2176]{1,0:T(8,128)(2,1)S(1)}, u32[]{:S(2)}, u32[]{:S(2)}) %collective-permute-start.14) | collective-permute-done | bytes 139296 | tf_op jit(solution)/shard_map/ppermute | solution.py:34
  71.9 0.7 shard_map.62
  72.6 1.2 %collective-permute-start.21 = (f32[8,256]{1,0:T(8,128)S(1)}, f32[8,256]{1,0:T(8,128)S(1)}, u32[]{:S(2)}, u32[]{:S(2)}) collective-permute-start(f32[8,256]{1,0:T(8,128)S(1)} %get-tuple-element.11.own_ref), channel_id=1, source_target_pairs={{0,1},{1,0},{2,3},{3,2},{4,5},{5,4},{6,7},{7,6},{8,9},{9,8},{10,11... | collective-permute-start | bytes 24584 | tf_op jit(solution)/shard_map/ppermute | solution.py:381
  73.8 0.8 collective-permute-done.21.oth_ref
  74.6 0.3 collective-permute-start.22
  75.0 0.1 pad_add_fusion.3.place
  75.1 0.7 shard_map.63
  75.7 5.4 %all-to-all-start = ((f32[16,8,256]{2,1,0:T(8,128)}), f32[16,8,256]{2,1,0:T(8,128)S(1)}, u32[]{:S(2)}, u32[]{:S(2)}) async-start(f32[16,8,256]{2,1,0:T(8,128)} %shard_map.63), calls=%async_computation | async-start | bytes 262144 | tf_op jit(solution)/shard_map/all_to_all | solution.py:384
  81.1 7.1 %shard_map.64 = (f32[2,256,768]{2,1,0:T(8,128)S(1)}, bf16[256,768]{1,0:T(8,128)(2,1)S(1)}) custom-call(s32[3]{0:T(128)S(1)} %pad_add_fusion.3.place, bf16[256,2176]{1,0:T(8,128)(2,1)S(1)} %get-tuple-element.14.own_ref, bf16[256,128]{1,0:T(8,128)(2,1)S(1)} %slice.25.ids_ref, bf16[256,2176]{1,0:T(8,128)(2,1)} %collective-permute-done.22.oth_ref, ...), custom_call_target="tpu_custom_call" | custom-call | flops 3221225472 | bytes 6291456 | tf_op jit(solution)/shard_map/pallas_call | solution.py:261
  88.3 3.2 %all-to-all-done.every_ref = f32[16,8,256]{2,1,0:T(8,128)S(1)} async-done(((f32[16,8,256]{2,1,0:T(8,128)}), f32[16,8,256]{2,1,0:T(8,128)S(1)}, u32[]{:S(2)}, u32[]{:S(2)}) %all-to-all-start) | async-done | bytes 131104 | tf_op jit(solution)/shard_map/all_to_all | solution.py:384
  91.5 0.2 shard_map.65
  91.7 0.2 slice_reduce_fusion.1
  91.9 1.1 fusion.10
  93.0 5.9 %all-to-all-start.1 = ((f16[16,16,768]{2,1,0:T(8,128)(2,1)}), f16[16,16,768]{2,1,0:T(8,128)(2,1)S(1)}, u32[]{:S(2)}, u32[]{:S(2)}) async-start(f16[16,16,768]{2,1,0:T(8,128)(2,1)} %bitcast.39), calls=%async_computation.1 | async-start | bytes 786432 | tf_op jit(solution)/shard_map/all_to_all | solution.py:392
  98.8 0.1 pad_add_fusion.4.place
  98.9 0.6 fusion.15
  99.5 9.1 %shard_map.66 = bf16[4096,768]{1,0:T(8,128)(2,1)} custom-call(s32[3]{0:T(128)S(1)} %pad_add_fusion.4.place, bf16[256,2176]{1,0:T(8,128)(2,1)S(1)} %get-tuple-element.14.own_ref, bf16[256,2176]{1,0:T(8,128)(2,1)} %collective-permute-done.22.oth_ref, bf16[256,896]{1,0:T(8,128)(2,1)} %copy-done, bf16[256,128]{1,0:T(8,128)(2,1)S(1)} %slice.25.ids_ref, ...), custom_call_target="tpu_custom_call" | custom-call | flops 1610612736 | bytes 8388608 | tf_op jit(solution)/shard_map/pallas_call | solution.py:319
  108.6 4.9 %all-to-all-done.1 = f16[16,16,768]{2,1,0:T(8,128)(2,1)S(1)} async-done(((f16[16,16,768]{2,1,0:T(8,128)(2,1)}), f16[16,16,768]{2,1,0:T(8,128)(2,1)S(1)}, u32[]{:S(2)}, u32[]{:S(2)}) %all-to-all-start.1) | async-done | bytes 393248 | tf_op jit(solution)/shard_map/all_to_all | solution.py:392
  113.5 0.7 multiply_reduce_fusion
  (12 shorter events, 0.0 us)
Async XLA Ops:
  2.1 10.3 %collective-permute-start.2 = (bf16[16,896]{1,0:T(8,128)(2,1)S(1)}, bf16[16,896]{1,0:T(8,128)(2,1)S(1)}, u32[]{:S(2)}, u32[]{:S(2)}) collective-permute-start(bf16[16,896]{1,0:T(8,128)(2,1)S(1)} %shard_map.58.refs_0_), channel_id=1, source_target_pairs={{0,32},{16,48},{32,0},{48,16},{1,33},{17,49},{33,1},{49,17},{2,34}... | collective-permute-start | bytes 86024 | tf_op jit(solution)/shard_map/ppermute | solution.py:86
  9.9 3.6 %collective-permute-start.1 = (bf16[16,896]{1,0:T(8,128)(2,1)S(1)}, bf16[16,896]{1,0:T(8,128)(2,1)S(1)}, u32[]{:S(2)}, u32[]{:S(2)}) collective-permute-start(bf16[16,896]{1,0:T(8,128)(2,1)S(1)} %shard_map.58.refs_0_), channel_id=1, source_target_pairs={{0,48},{16,0},{32,16},{48,32},{1,49},{17,1},{33,17},{49,33},{2,50}... | collective-permute-start | bytes 86024 | tf_op jit(solution)/shard_map/ppermute | solution.py:86
  9.9 4.9 %collective-permute-start = (bf16[16,896]{1,0:T(8,128)(2,1)S(1)}, bf16[16,896]{1,0:T(8,128)(2,1)S(1)}, u32[]{:S(2)}, u32[]{:S(2)}) collective-permute-start(bf16[16,896]{1,0:T(8,128)(2,1)S(1)} %shard_map.58.refs_0_), channel_id=1, source_target_pairs={{0,16},{16,32},{32,48},{48,0},{1,17},{17,33},{33,49},{49,1},{2,18}... | collective-permute-start | bytes 86024 | tf_op jit(solution)/shard_map/ppermute | solution.py:86
  15.4 5.2 %collective-permute-start.5 = (bf16[64,896]{1,0:T(8,128)(2,1)S(1)}, bf16[64,896]{1,0:T(8,128)(2,1)S(1)}, u32[]{:S(2)}, u32[]{:S(2)}) collective-permute-start(bf16[64,896]{1,0:T(8,128)(2,1)S(1)} %shard_map.59.refs_0_), channel_id=1, source_target_pairs={{0,128},{64,192},{128,0},{192,64},{1,129},{65,193},{129,1},{193,65... | collective-permute-start | bytes 344072 | tf_op jit(solution)/shard_map/ppermute | solution.py:86
  18.4 4.1 %collective-permute-start.4 = (bf16[64,896]{1,0:T(8,128)(2,1)S(1)}, bf16[64,896]{1,0:T(8,128)(2,1)S(1)}, u32[]{:S(2)}, u32[]{:S(2)}) collective-permute-start(bf16[64,896]{1,0:T(8,128)(2,1)S(1)} %shard_map.59.refs_0_), channel_id=1, source_target_pairs={{0,192},{64,0},{128,64},{192,128},{1,193},{65,1},{129,65},{193,129... | collective-permute-start | bytes 344072 | tf_op jit(solution)/shard_map/ppermute | solution.py:86
  19.2 5.6 %collective-permute-start.3 = (bf16[64,896]{1,0:T(8,128)(2,1)S(1)}, bf16[64,896]{1,0:T(8,128)(2,1)S(1)}, u32[]{:S(2)}, u32[]{:S(2)}) collective-permute-start(bf16[64,896]{1,0:T(8,128)(2,1)S(1)} %shard_map.59.refs_0_), channel_id=1, source_target_pairs={{0,64},{64,128},{128,192},{192,0},{1,65},{65,129},{129,193},{193,1... | collective-permute-start | bytes 344072 | tf_op jit(solution)/shard_map/ppermute | solution.py:86
  25.4 20.1 %copy-start = (bf16[256,896]{1,0:T(8,128)(2,1)}, bf16[256,896]{1,0:T(8,128)(2,1)S(1)}, u32[]{:S(2)}) copy-start(bf16[256,896]{1,0:T(8,128)(2,1)S(1)} %shard_map.60.hidden_ref) | copy-start | bytes 1376260
  28.5 5.9 %collective-permute-start.6 = (f16[256,2048]{1,0:T(8,128)(2,1)S(1)}, f16[256,2048]{1,0:T(8,128)(2,1)S(1)}, u32[]{:S(2)}, u32[]{:S(2)}) collective-permute-start(f16[256,2048]{1,0:T(8,128)(2,1)S(1)} %fusion.4), channel_id=1, source_target_pairs={{0,1},{1,0},{2,3},{3,2},{4,5},{5,4},{6,7},{7,6},{8,9},{9,8},{10,11... | collective-permute-start | bytes 3145736 | tf_op jit(solution)/shard_map/ppermute | solution.py:362
  34.8 7.9 %collective-permute-start.7 = (f16[32,2048]{1,0:T(8,128)(2,1)S(1)}, f16[32,2048]{1,0:T(8,128)(2,1)S(1)}, u32[]{:S(2)}, u32[]{:S(2)}) collective-permute-start(f16[32,2048]{1,0:T(8,128)(2,1)S(1)} %get-tuple-element.21), channel_id=1, source_target_pairs={{0,4},{2,6},{4,8},{6,10},{8,12},{10,14},{12,0},{14,2},{1,5},{3,7},... | collective-permute-start | bytes 393224 | tf_op jit(solution)/shard_map/ppermute | solution.py:34
  36.1 6.8 %collective-permute-start.13 = (f16[32,2048]{1,0:T(8,128)(2,1)S(1)}, f16[32,2048]{1,0:T(8,128)(2,1)S(1)}, u32[]{:S(2)}, u32[]{:S(2)}) collective-permute-start(f16[32,2048]{1,0:T(8,128)(2,1)S(1)} %get-tuple-element.22), channel_id=1, source_target_pairs={{0,14},{2,12},{4,2},{6,0},{8,6},{10,4},{12,10},{14,8},{1,15},{3,13... | collective-permute-start | bytes 393224 | tf_op jit(solution)/shard_map/ppermute | solution.py:34
  38.8 7.2 %collective-permute-start.12 = (f16[32,2048]{1,0:T(8,128)(2,1)S(1)}, f16[32,2048]{1,0:T(8,128)(2,1)S(1)}, u32[]{:S(2)}, u32[]{:S(2)}) collective-permute-start(f16[32,2048]{1,0:T(8,128)(2,1)S(1)} %get-tuple-element.23), channel_id=1, source_target_pairs={{0,6},{2,4},{4,10},{6,8},{8,14},{10,12},{12,2},{14,0},{1,7},{3,5},... | collective-permute-start | bytes 393224 | tf_op jit(solution)/shard_map/ppermute | solution.py:34
  38.8 11.9 %collective-permute-start.11 = (f16[32,2048]{1,0:T(8,128)(2,1)S(1)}, f16[32,2048]{1,0:T(8,128)(2,1)S(1)}, u32[]{:S(2)}, u32[]{:S(2)}) collective-permute-start(f16[32,2048]{1,0:T(8,128)(2,1)S(1)} %get-tuple-element.24), channel_id=1, source_target_pairs={{0,8},{2,10},{4,12},{6,14},{8,0},{10,2},{12,4},{14,6},{1,9},{3,11}... | collective-permute-start | bytes 393224 | tf_op jit(solution)/shard_map/ppermute | solution.py:34
  40.9 9.8 %collective-permute-start.10 = (f16[32,2048]{1,0:T(8,128)(2,1)S(1)}, f16[32,2048]{1,0:T(8,128)(2,1)S(1)}, u32[]{:S(2)}, u32[]{:S(2)}) collective-permute-start(f16[32,2048]{1,0:T(8,128)(2,1)S(1)} %get-tuple-element.25), channel_id=1, source_target_pairs={{0,10},{2,8},{4,14},{6,12},{8,2},{10,0},{12,6},{14,4},{1,11},{3,9}... | collective-permute-start | bytes 393224 | tf_op jit(solution)/shard_map/ppermute | solution.py:34
  42.7 8.1 %collective-permute-start.9 = (f16[32,2048]{1,0:T(8,128)(2,1)S(1)}, f16[32,2048]{1,0:T(8,128)(2,1)S(1)}, u32[]{:S(2)}, u32[]{:S(2)}) collective-permute-start(f16[32,2048]{1,0:T(8,128)(2,1)S(1)} %get-tuple-element.26), channel_id=1, source_target_pairs={{0,2},{2,0},{4,6},{6,4},{8,10},{10,8},{12,14},{14,12},{1,3},{3,1},... | collective-permute-start | bytes 393224 | tf_op jit(solution)/shard_map/ppermute | solution.py:34
  42.9 8.0 %collective-permute-start.8 = (f16[32,2048]{1,0:T(8,128)(2,1)S(1)}, f16[32,2048]{1,0:T(8,128)(2,1)S(1)}, u32[]{:S(2)}, u32[]{:S(2)}) collective-permute-start(f16[32,2048]{1,0:T(8,128)(2,1)S(1)} %get-tuple-element.27), channel_id=1, source_target_pairs={{0,12},{2,14},{4,0},{6,2},{8,4},{10,6},{12,8},{14,10},{1,13},{3,15... | collective-permute-start | bytes 393224 | tf_op jit(solution)/shard_map/ppermute | solution.py:34
  51.9 8.5 %collective-permute-start.20 = (bf16[32,2176]{1,0:T(8,128)(2,1)S(1)}, bf16[32,2176]{1,0:T(8,128)(2,1)S(1)}, u32[]{:S(2)}, u32[]{:S(2)}) collective-permute-start(bf16[32,2176]{1,0:T(8,128)(2,1)S(1)} %shard_map.61.refs_0_), channel_id=1, source_target_pairs={{0,14},{2,12},{4,2},{6,0},{8,6},{10,4},{12,10},{14,8},{1,15},{3,13... | collective-permute-start | bytes 417800 | tf_op jit(solution)/shard_map/ppermute | solution.py:34
  56.2 6.6 %collective-permute-start.19 = (bf16[32,2176]{1,0:T(8,128)(2,1)S(1)}, bf16[32,2176]{1,0:T(8,128)(2,1)S(1)}, u32[]{:S(2)}, u32[]{:S(2)}) collective-permute-start(bf16[32,2176]{1,0:T(8,128)(2,1)S(1)} %shard_map.61.refs_0_), channel_id=1, source_target_pairs={{0,6},{2,4},{4,10},{6,8},{8,14},{10,12},{12,2},{14,0},{1,7},{3,5},... | collective-permute-start | bytes 417800 | tf_op jit(solution)/shard_map/ppermute | solution.py:34
  56.2 12.9 %collective-permute-start.18 = (bf16[32,2176]{1,0:T(8,128)(2,1)S(1)}, bf16[32,2176]{1,0:T(8,128)(2,1)S(1)}, u32[]{:S(2)}, u32[]{:S(2)}) collective-permute-start(bf16[32,2176]{1,0:T(8,128)(2,1)S(1)} %shard_map.61.refs_0_), channel_id=1, source_target_pairs={{0,8},{2,10},{4,12},{6,14},{8,0},{10,2},{12,4},{14,6},{1,9},{3,11}... | collective-permute-start | bytes 417800 | tf_op jit(solution)/shard_map/ppermute | solution.py:34
  57.5 11.6 %collective-permute-start.17 = (bf16[32,2176]{1,0:T(8,128)(2,1)S(1)}, bf16[32,2176]{1,0:T(8,128)(2,1)S(1)}, u32[]{:S(2)}, u32[]{:S(2)}) collective-permute-start(bf16[32,2176]{1,0:T(8,128)(2,1)S(1)} %shard_map.61.refs_0_), channel_id=1, source_target_pairs={{0,10},{2,8},{4,14},{6,12},{8,2},{10,0},{12,6},{14,4},{1,11},{3,9}... | collective-permute-start | bytes 417800 | tf_op jit(solution)/shard_map/ppermute | solution.py:34
  58.8 10.3 %collective-permute-start.16 = (bf16[32,2176]{1,0:T(8,128)(2,1)S(1)}, bf16[32,2176]{1,0:T(8,128)(2,1)S(1)}, u32[]{:S(2)}, u32[]{:S(2)}) collective-permute-start(bf16[32,2176]{1,0:T(8,128)(2,1)S(1)} %shard_map.61.refs_0_), channel_id=1, source_target_pairs={{0,2},{2,0},{4,6},{6,4},{8,10},{10,8},{12,14},{14,12},{1,3},{3,1},... | collective-permute-start | bytes 417800 | tf_op jit(solution)/shard_map/ppermute | solution.py:34
  60.4 8.8 %collective-permute-start.15 = (bf16[32,2176]{1,0:T(8,128)(2,1)S(1)}, bf16[32,2176]{1,0:T(8,128)(2,1)S(1)}, u32[]{:S(2)}, u32[]{:S(2)}) collective-permute-start(bf16[32,2176]{1,0:T(8,128)(2,1)S(1)} %shard_map.61.refs_0_), channel_id=1, source_target_pairs={{0,12},{2,14},{4,0},{6,2},{8,4},{10,6},{12,8},{14,10},{1,13},{3,15... | collective-permute-start | bytes 417800 | tf_op jit(solution)/shard_map/ppermute | solution.py:34
  62.8 9.1 %collective-permute-start.14 = (bf16[32,2176]{1,0:T(8,128)(2,1)S(1)}, bf16[32,2176]{1,0:T(8,128)(2,1)S(1)}, u32[]{:S(2)}, u32[]{:S(2)}) collective-permute-start(bf16[32,2176]{1,0:T(8,128)(2,1)S(1)} %shard_map.61.refs_0_), channel_id=1, source_target_pairs={{0,4},{2,6},{4,8},{6,10},{8,12},{10,14},{12,0},{14,2},{1,5},{3,7},... | collective-permute-start | bytes 417800 | tf_op jit(solution)/shard_map/ppermute | solution.py:34
  72.6 2.0 %collective-permute-start.21 = (f32[8,256]{1,0:T(8,128)S(1)}, f32[8,256]{1,0:T(8,128)S(1)}, u32[]{:S(2)}, u32[]{:S(2)}) collective-permute-start(f32[8,256]{1,0:T(8,128)S(1)} %get-tuple-element.11.own_ref), channel_id=1, source_target_pairs={{0,1},{1,0},{2,3},{3,2},{4,5},{5,4},{6,7},{7,6},{8,9},{9,8},{10,11... | collective-permute-start | bytes 24584 | tf_op jit(solution)/shard_map/ppermute | solution.py:381
  74.6 6.5 %collective-permute-start.22 = (bf16[256,2176]{1,0:T(8,128)(2,1)S(1)}, bf16[256,2176]{1,0:T(8,128)(2,1)}, u32[]{:S(2)}, u32[]{:S(2)}) collective-permute-start(bf16[256,2176]{1,0:T(8,128)(2,1)S(1)} %get-tuple-element.14.own_ref), channel_id=1, source_target_pairs={{0,1},{1,0},{2,3},{3,2},{4,5},{5,4},{6,7},{7,6},{8,9},{9,8},{10,11... | collective-permute-start | bytes 3342344 | tf_op jit(solution)/shard_map/ppermute | solution.py:383
  75.7 15.7 %all-to-all-start = ((f32[16,8,256]{2,1,0:T(8,128)}), f32[16,8,256]{2,1,0:T(8,128)S(1)}, u32[]{:S(2)}, u32[]{:S(2)}) async-start(f32[16,8,256]{2,1,0:T(8,128)} %shard_map.63), calls=%async_computation | async-start | bytes 262144 | tf_op jit(solution)/shard_map/all_to_all | solution.py:384
  93.0 20.6 %all-to-all-start.1 = ((f16[16,16,768]{2,1,0:T(8,128)(2,1)}), f16[16,16,768]{2,1,0:T(8,128)(2,1)S(1)}, u32[]{:S(2)}, u32[]{:S(2)}) async-start(f16[16,16,768]{2,1,0:T(8,128)(2,1)} %bitcast.39), calls=%async_computation.1 | async-start | bytes 786432 | tf_op jit(solution)/shard_map/all_to_all | solution.py:392
